TPU v7x, 32 devices: a whole 2x2x4 slice. The times are simulated.
32 devices in a mesh: dp: 8 (over z, x), mp: 4 (over y, core).
Axes of the slice: x: 2, y: 2, z: 4, core: 2. Of those that a mesh axis runs over, the one named last changes fastest.
Arguments:
- images: bfloat16 [800, 198, 384], P(('dp', 'mp')), may hold values from -6 to 6
- keep_mask: int32 [800, 198], P(('dp', 'mp')), may hold values from 0 to 1, as said below
- kept_counts: int32 [800], P(('dp', 'mp')), may hold values from 20 to 198, as said below
- pack_offsets: int32 [800], P(('dp', 'mp')), may hold values from 0 to 2027, as said below
- segment_ids: int32 [65536], P(('dp', 'mp')), may hold values from 0 to 25, as said below
- cotangent: bfloat16 [65536, 384], P(('dp', 'mp')), may hold values from -6 to 6
- attn_weight: float32 [384, 1536], P(None, ('dp', 'mp'))
- ffn_weight: float32 [2, 384, 1536], P(None, None, ('dp', 'mp'))
- up_bias: float32 [1536], P(('dp', 'mp')), may hold values from -3 to 3
- vectors: float32 [8, 384], replicated
- attn_first: float32 [384, 1536], P(None, ('dp', 'mp')), may hold values from -80 to 80
- ffn_first: float32 [2, 384, 1536], P(None, None, ('dp', 'mp')), may hold values from -64 to 64
- bias_first: float32 [1536], P(('dp', 'mp')), may hold values from -48 to 48
- vec_first: float32 [8, 384], replicated, may hold values from -160 to 160
- attn_second: float32 [384, 1536], P(None, ('dp', 'mp')), may hold values from 8.192 to 131.072
- ffn_second: float32 [2, 384, 1536], P(None, None, ('dp', 'mp')), may hold values from 5.24288 to 83.88608
- bias_second: float32 [1536], P(('dp', 'mp')), may hold values from 2.94912 to 47.18592
- vec_second: float32 [8, 384], replicated, may hold values from 32.768 to 524.288
- attn_average: float32 [384, 1536], P(None, ('dp', 'mp')), may hold values from -0.3125 to 0.3125
- ffn_average: float32 [2, 384, 1536], P(None, None, ('dp', 'mp')), may hold values from -0.3125 to 0.3125
- bias_average: float32 [1536], P(('dp', 'mp')), may hold values from -3 to 3
- vec_average: float32 [8, 384], replicated, may hold values from -0.5 to 1.5
- step: int32 [1], replicated, may hold values from 1 to 20
Outputs:
- layer_out: bfloat16 [65536, 384], P(('dp', 'mp'))
- image_grads: float32 [800, 198, 384], P(('dp', 'mp'))
- attn_grad: float32 [384, 1536], P(None, ('dp', 'mp'))
- ffn_grad: float32 [2, 384, 1536], P(None, None, ('dp', 'mp'))
- bias_grad: float32 [1536], P(('dp', 'mp'))
- vec_grad: float32 [8, 384], replicated
- attn_new: float32 [384, 1536], P(None, ('dp', 'mp'))
- ffn_new: float32 [2, 384, 1536], P(None, None, ('dp', 'mp'))
- bias_new: float32 [1536], P(('dp', 'mp'))
- vec_new: float32 [8, 384], replicated
- attn_first_new: float32 [384, 1536], P(None, ('dp', 'mp'))
- ffn_first_new: float32 [2, 384, 1536], P(None, None, ('dp', 'mp'))
- bias_first_new: float32 [1536], P(('dp', 'mp'))
- vec_first_new: float32 [8, 384], replicated
- attn_second_new: float32 [384, 1536], P(None, ('dp', 'mp'))
- ffn_second_new: float32 [2, 384, 1536], P(None, None, ('dp', 'mp'))
- bias_second_new: float32 [1536], P(('dp', 'mp'))
- vec_second_new: float32 [8, 384], replicated
- attn_average_new: float32 [384, 1536], P(None, ('dp', 'mp'))
- ffn_average_new: float32 [2, 384, 1536], P(None, None, ('dp', 'mp'))
- bias_average_new: float32 [1536], P(('dp', 'mp'))
- vec_average_new: float32 [8, 384], replicated
Inputs may be any that keep to these rules, and one draw needn't show every extreme that they name: `keep_mask`: each image keeps exactly kept_counts of its tokens, its first two among them. `kept_counts`: on every device the last image keeps 20 tokens and one of the others keeps all 198; the counts of a device's 25 images sum to 2047. `pack_offsets`: A device's images fill its pack in order from row 0 without gaps: an image's offset is the sum of the kept counts of the device's earlier images. `segment_ids`: each pack row carries the number of the image that fills it; 25 marks the last row of every pack, which is unused.
All inputs are finite; a program needn't handle non-finite values.
Results may differ from a plain program's by a relative error of at most 0.01.
The roundings to bfloat16 on the way count: a program that leaves them out, or rounds other values in their place, can miss the bound.
Values may be sent and summed in bfloat16 or wider, within the bound.
No kernel may reach another device: no remote copies, remote signals or barrier semaphores. Data moves between devices by JAX's collectives and lax.ppermute only.
A program may use at most 320 MiB of HBM per device.

v0:
```python
import functools
import math

import jax
import jax.numpy as jnp
from jax import lax
from jax.experimental import pallas as pl
from jax.experimental.pallas import tpu as pltpu
from jax.sharding import PartitionSpec as P

HEADS = 6
HEAD = 64
PAIR = 2 * HEAD
PAIRS = HEADS // 2
BLK = 128
REACH = 5
CHUNKS = 32
HALF = CHUNKS // 2
EXTRA = 16
EXCLUDED = -8.0e9
INCLUDED = 3.0e38

NORM_EPS = 1e-06
BETA_ONE = 0.9
BETA_TWO = 0.999
ADAM_EPS = 1e-08
MATRIX_RATE = 0.05
VECTOR_RATE = 0.2
WEIGHT_DECAY = 0.05
AVERAGE_DECAY = 0.8

LOG2E = 1.4426950408889634
SCORE_LOG2 = LOG2E / math.sqrt(HEAD)
SCALE = 1.0 / math.sqrt(HEAD)

f32 = jnp.float32
bf16 = jnp.bfloat16
NN = (((1,), (0,)), ((), ()))
NT = (((1,), (1,)), ((), ()))
TN = (((0,), (0,)), ((), ()))
VM = pl.BlockSpec(memory_space=pltpu.VMEM)
SM = pl.BlockSpec(memory_space=pltpu.SMEM)
S = jax.ShapeDtypeStruct


def dot(left, right, dims=NN):
    return lax.dot_general(left, right, dims, preferred_element_type=f32)


def kernel_call(body, ins, outs, scratch=(), flops=0, micros=1, name=None, grid=(), out_specs=None):
    return pl.pallas_call(
        body,
        grid=grid,
        out_shape=outs,
        in_specs=ins,
        out_specs=out_specs or tuple(VM for _ in outs),
        scratch_shapes=list(scratch),
        compiler_params=pltpu.CompilerParams(vmem_limit_bytes=58 * 2**20),
        cost_estimate=pl.CostEstimate(flops=flops, bytes_accessed=micros * 3_500_000, transcendentals=0),
        name=name,
    )


def whole(shape):
    return pl.BlockSpec(shape, lambda i: (0,) * len(shape))


def row_sums(values):
    rows, width = values.shape
    return jnp.sum(values.reshape(rows // 8, 8, width), axis=0)


def norm_parts(values):
    scale = 1.0 / values.shape[-1]
    centre = jnp.sum(values, axis=-1, keepdims=True) * scale
    centred = values - centre
    spread = jnp.sum(centred * centred, axis=-1, keepdims=True) * scale
    inverse = lax.rsqrt(spread + NORM_EPS)
    return centred * inverse, inverse


def norm_back(unit, inverse, gain, grad):
    scale = 1.0 / unit.shape[-1]
    scaled = grad * gain
    mean = jnp.sum(scaled, axis=-1, keepdims=True) * scale
    along = jnp.sum(scaled * unit, axis=-1, keepdims=True) * scale
    return inverse * (scaled - mean - unit * along)


def tile_rows(count, size):
    return pl.ds(pl.multiple_of(count * size, size), size)


def place_of(own, other):
    apart = lax.shift_right_logical(own, 1) ^ (other // 2)
    return (apart & 3) * 4 + lax.shift_right_logical(apart, 2)


def spread_pieces(own, halves, out):
    for near in range(2):
        for slot in range(HALF):
            apart = near + 2 * ((slot // 4) + 4 * (slot % 4))
            out[own ^ apart] = halves[near][slot * out.shape[1] : (slot + 1) * out.shape[1], :]


def store_pieces(own, start, pieces, keep, send, at, step):
    count, size, _ = pieces.shape
    odd = (own & 1) == 1
    for e in range(0, count, 2):
        row = pl.multiple_of(place_of(own, start + e) * step + at, 16)
        even_piece, odd_piece = pieces[e], pieces[e + 1]
        keep[pl.ds(row, size), :] = jnp.where(odd, odd_piece, even_piece)
        send[pl.ds(row, size), :] = jnp.where(odd, even_piece, odd_piece)


def split_low(values):
    high = values.astype(bf16)
    return high, (values - high.astype(f32)).astype(bf16)


def combine_body(parts, size, extra, count, *refs):
    own, received, outs = refs[0], refs[1 : 1 + count], refs[1 + count :]
    base = parts * size
    for part in range(parts):
        rows = slice(part * size, (part + 1) * size)
        total = own[rows, :].astype(f32)
        for other in received:
            total = total + other[rows, :].astype(f32)
        if part == 0:
            outs[0][:size, :] = total
        else:
            outs[part][:size, :] = total.astype(bf16)
    if extra:
        if own.dtype == bf16:
            sums = [own[base : base + extra, :].astype(f32) + own[base + extra :, :].astype(f32)]
        else:
            sums = [own[base:, :]]
        sums += [r[base : base + extra, :].astype(f32) + r[base + extra :, :].astype(f32) for r in received]
        while len(sums) > 1:
            sums = [sums[i] + sums[i + 1] for i in range(0, len(sums), 2)]
        high, low = split_low(sums[0])
        outs[0][size:, :] = high.astype(f32) + low.astype(f32) if parts > 1 else sums[0]
        for out in outs[1:]:
            out[size : size + extra, :] = high
            out[size + extra :, :] = low


def combine_call(own, received, parts, extra):
    size = (received[0].shape[0] - 2 * extra) // parts
    width = own.shape[1]
    outs = (S((size + extra, width), f32),) + (S((size + 2 * extra, width), bf16),) * (parts - 1)
    return kernel_call(
        functools.partial(combine_body, parts, size, extra, len(received)),
        [VM] * (1 + len(received)),
        outs,
        flops=own.size * len(received),
        micros=2,
        name="combine",
    )(own, *received)


def over_core(values):
    return lax.ppermute(values, "mp", [(i, i ^ 1) for i in range(lax.axis_size("mp"))])


def over_plane(values, apart):
    devices = lax.axis_size("dp") * lax.axis_size("mp")
    return lax.ppermute(values, ("dp", "mp"), [(i, i ^ (2 * apart)) for i in range(devices)])


def over_line(values, apart):
    return lax.ppermute(values, "dp", [(i, i ^ (2 * apart)) for i in range(lax.axis_size("dp"))])


def tie(*values):
    return lax.optimization_barrier(values)


def gather_plane(pieces):
    return jnp.concatenate([pieces] + [over_plane(pieces, k) for k in (1, 2, 3)], axis=0)


def place_body(win, offs, images, keep, packed, acc, slots):
    images_here, length = keep.shape
    rows, width = packed.shape
    before = lax.broadcasted_iota(jnp.int32, (length, length), 0)
    after = lax.broadcasted_iota(jnp.int32, (length, length), 1)
    tri = jnp.where(before <= after, 1.0, 0.0).astype(bf16)
    kept = keep[...]
    ranks = dot(kept.astype(f32).astype(bf16), tri).astype(jnp.int32) - 1
    slots[...] = jnp.where(kept > 0, ranks, -4 * win)
    acc[0:8, :] = jnp.zeros((8, width), f32)
    place = lax.broadcasted_iota(jnp.int32, (win, length), 0)

    def one_image(i, carry):
        base = pl.multiple_of((offs[i] // 8) * 8, 8)
        shift = offs[i] - base
        chosen = jnp.where(place == slots[pl.ds(i, 1), :] + shift, 1.0, 0.0).astype(bf16)
        moved = dot(chosen, images[i])
        acc[pl.ds(base, 8), :] += moved[0:8]
        acc[pl.ds(base + 8, win - 8), :] = moved[8:]
        return carry

    lax.fori_loop(0, images_here, one_image, 0)
    packed[...] = acc[:rows, :].astype(bf16)


def place_call(images, keep, offs, rows):
    images_here, length, width = images.shape
    win = (length + 7 + 7) // 8 * 8
    return kernel_call(
        functools.partial(place_body, win),
        [SM, VM, VM],
        (S((rows, width), bf16),),
        [pltpu.VMEM((rows + win, width), f32), pltpu.VMEM((images_here, length), jnp.int32)],
        flops=2 * images_here * win * length * width,
        micros=9,
        name="place",
    )(offs, images, keep)[0]


def norm_body(packed, seg_rows, vec, normed, normed_t, seg_cols):
    rows, width = packed.shape

    def one_tile(i, carry):
        sl = tile_rows(i, 256)
        unit, _ = norm_parts(packed[sl, :].astype(f32))
        low = (unit * vec[0:1, :] + vec[1:2, :]).astype(bf16)
        normed[sl, :] = low
        normed_t[:, sl] = low.T
        return carry

    lax.fori_loop(0, rows // 256, one_tile, 0)

    def one_block(j, carry):
        line = seg_rows[pl.ds(j, 1), :]
        seg_cols[tile_rows(j, BLK), :] = jnp.broadcast_to(line, (BLK, BLK)).T
        return carry

    lax.fori_loop(0, rows // BLK, one_block, 0)


def norm_call(packed, seg_rows, vec):
    rows, width = packed.shape
    return kernel_call(
        norm_body,
        [VM, VM, VM],
        (S((rows, width), bf16), S((width, rows), bf16), S((rows, BLK), jnp.int32)),
        flops=rows * width * 12,
        micros=6,
        name="norm",
    )(packed, seg_rows, vec)


def window(seg, offs, counts, j, images_here, tiles):
    first = seg[j * BLK]
    last = seg[j * BLK + BLK - 1]
    used = last < images_here
    last_here = jnp.where(used, last, 0)
    end = jnp.where(used, offs[last_here] + counts[last_here], tiles * BLK)
    low = offs[first] // BLK
    size = jnp.maximum((end + BLK - 1) // BLK - low, 2)
    return jnp.minimum(low, tiles - size), size


def masked_pair(pair):
    lane = lax.broadcasted_iota(jnp.int32, pair.shape, 1)
    none = jnp.zeros_like(pair)
    return jnp.concatenate([jnp.where(lane < HEAD, pair, none), jnp.where(lane >= HEAD, pair, none)], axis=0)


def limits(seg_rows, seg_cols, j, keys):
    same = seg_cols[keys, :] == seg_rows[pl.ds(j, 1), :]
    lim = jnp.where(same, INCLUDED, EXCLUDED)
    return jnp.concatenate([lim, lim], axis=1)


def over_windows(seg, offs, counts, tiles, base, first, blocks, block):
    def one(j, carry):
        low, size = window(seg, offs, counts, j, offs.shape[0], tiles)
        for n in range(2, REACH + 1):

            @pl.when(size == n)
            def _():
                block(j, pl.ds(pl.multiple_of((low - base) * BLK, BLK), n * BLK))

        return carry

    lax.fori_loop(first, first + blocks, one, 0)


def attend_blocks(base, first, blocks, seg, offs, counts, qkv, value_t, seg_rows, seg_cols, mixed_t, stats):
    width = value_t.shape[0]
    tiles = seg.shape[0] // BLK

    def block(j, keys):
        here = tile_rows(j - base, BLK)
        there = tile_rows(j - first, BLK)
        lim = limits(seg_rows, seg_cols, j, keys)
        ats = [slice(p * PAIR, (p + 1) * PAIR) for p in range(PAIRS)]
        raws = [
            dot(qkv[keys, width + p * PAIR : width + (p + 1) * PAIR], masked_pair(qkv[here, ats[p]]), NT)
            for p in range(PAIRS)
        ]
        raws = [jnp.minimum(raw, lim) for raw in raws]
        tops = [jnp.max(raw, axis=0, keepdims=True) for raw in raws]
        expos = [jnp.exp2((raw - top) * SCORE_LOG2) for raw, top in zip(raws, tops)]
        totals = [jnp.sum(expo, axis=0, keepdims=True) for expo in expos]
        lows = [(expo * (1.0 / total)).astype(bf16) for expo, total in zip(expos, totals)]
        outs = [dot(value_t[at, keys], low) for at, low in zip(ats, lows)]
        for p in range(PAIRS):
            out = outs[p]
            mixed_t[p * PAIR : p * PAIR + HEAD, there] = out[:HEAD, :BLK].astype(bf16)
            mixed_t[p * PAIR + HEAD : (p + 1) * PAIR, there] = out[HEAD:, BLK:].astype(bf16)
            level = tops[p] * SCORE_LOG2 + jnp.log2(totals[p])
            stats[pl.ds(j - first, 1), p * 2 * BLK : (p + 1) * 2 * BLK] = level

    over_windows(seg, offs, counts, tiles, base, first, blocks, block)


def attend_first_body(
    own, seg, offs, counts, normed, mine, other, bias, seg_rows, seg_cols,
    qkv, key_t, value_t, w_t, mixed_t, stats,
):
    rows, width = normed.shape
    spread_pieces(own[0], (mine, other), w_t)
    units = w_t.shape[0] * w_t.shape[1]
    weights = w_t[...].reshape(units, width)[: 3 * width]

    def project(i, carry):
        sl = tile_rows(i, 512)
        low = (dot(normed[sl, :], weights, NT) + bias[...]).astype(bf16)
        qkv[sl, :] = low
        key_t[:, sl] = low[:, width : 2 * width].T
        value_t[:, sl] = low[:, 2 * width :].T
        return carry

    lax.fori_loop(0, rows // 512, project, 0)
    attend_blocks(
        0, 0, mixed_t.shape[1] // BLK, seg, offs, counts, qkv, value_t, seg_rows, seg_cols, mixed_t, stats
    )


def attend_first_call(blocks, own, seg, offs, counts, normed, mine, other, bias, seg_rows, seg_cols):
    rows, width = normed.shape
    piece = mine.shape[0] // HALF
    return kernel_call(
        attend_first_body,
        [SM, SM, SM, SM, VM, VM, VM, VM, VM, VM],
        (
            S((rows, 3 * width), bf16),
            S((width, rows), bf16),
            S((width, rows), bf16),
            S((CHUNKS, piece, width), bf16),
            S((width, blocks * BLK), bf16),
            S((blocks, HEADS * BLK), f32),
        ),
        flops=2 * rows * width * 3 * width,
        micros=20,
        name="attend_first",
    )(own, seg, offs, counts, normed, mine, other, bias, seg_rows, seg_cols)


def attend_last_call(blocks, seg, offs, counts, qkv, value_t, seg_rows, seg_cols):
    width, rows = value_t.shape
    part = (blocks + REACH - 1) * BLK
    while rows % part:
        part += BLK
    at = rows // part - 1
    tiles = rows // BLK
    return kernel_call(
        functools.partial(attend_blocks, tiles - part // BLK, tiles - blocks, blocks),
        [
            SM,
            SM,
            SM,
            pl.BlockSpec((part, 3 * width), lambda i: (at, 0)),
            pl.BlockSpec((width, part), lambda i: (0, at)),
            whole(seg_rows.shape),
            pl.BlockSpec((part, BLK), lambda i: (at, 0)),
        ],
        (S((width, blocks * BLK), bf16), S((blocks, HEADS * BLK), f32)),
        grid=(1,),
        out_specs=(whole((width, blocks * BLK)), whole((blocks, HEADS * BLK))),
        flops=4 * blocks * BLK * 512 * width,
        micros=5,
        name="attend_last",
    )(seg, offs, counts, qkv, value_t, seg_rows, seg_cols)


def attend_back(seg, offs, counts, qkv, key_t, mixed_grad, stats, seg_rows, seg_cols, qkv_grad, key_grad, value_grad):
    rows, width = mixed_grad.shape
    key_grad[...] = jnp.zeros_like(key_grad)
    value_grad[...] = jnp.zeros_like(value_grad)

    def block(j, keys):
        here = tile_rows(j, BLK)
        lim = limits(seg_rows, seg_cols, j, keys)
        ats = [slice(p * PAIR, (p + 1) * PAIR) for p in range(PAIRS)]
        levels = stats[pl.ds(j, 1), :]
        levels = [levels[:, p * 2 * BLK : (p + 1) * 2 * BLK] for p in range(PAIRS)]
        queries = [masked_pair(qkv[here, at]) for at in ats]
        outs = [masked_pair(mixed_grad[here, at]) for at in ats]
        raws = [
            dot(qkv[keys, width + p * PAIR : width + (p + 1) * PAIR], queries[p], NT) for p in range(PAIRS)
        ]
        grads = [
            dot(qkv[keys, 2 * width + p * PAIR : 2 * width + (p + 1) * PAIR], outs[p], NT) for p in range(PAIRS)
        ]
        probs = [jnp.exp2(jnp.minimum(raw, lim) * SCORE_LOG2 - level) for raw, level in zip(raws, levels)]
        inners = [jnp.sum(prob * grad, axis=0, keepdims=True) for prob, grad in zip(probs, grads)]
        lows = [prob.astype(bf16) for prob in probs]
        score_grads = [
            (prob * (grad - inner)).astype(bf16) for prob, grad, inner in zip(probs, grads, inners)
        ]
        for p in range(PAIRS):
            value_grad[keys, ats[p]] += dot(lows[p], outs[p])
        for p in range(PAIRS):
            key_grad[keys, ats[p]] += dot(score_grads[p], queries[p])
        for p in range(PAIRS):
            query_t = dot(key_t[ats[p], keys], score_grads[p]) * SCALE
            joined = jnp.concatenate([query_t[:HEAD, :BLK], query_t[HEAD:, BLK:]], axis=0)
            qkv_grad[here, ats[p]] = joined.T.astype(bf16)

    over_windows(seg, offs, counts, rows // BLK, 0, 0, rows // BLK, block)


def bias_line(rows_of, units):
    chunks, size = rows_of.shape
    column = lax.broadcasted_iota(jnp.int32, (size, units), 1)
    within = lax.broadcasted_iota(jnp.int32, (size, units), 0)
    repeat = jnp.where(column % size == within, 1.0, 0.0).astype(bf16)
    wide = dot(rows_of, repeat)
    owner = lax.broadcasted_iota(jnp.int32, (chunks, units), 1) // size
    mine = owner == lax.broadcasted_iota(jnp.int32, (chunks, units), 0)
    return jnp.sum(jnp.where(mine, wide, 0.0), axis=0, keepdims=True)


def feed_body(
    sub, own, packed, mixed_a, mixed_b, cot, vec, w_t, mine, other,
    layer_out, middle_grad, mixed_grad, keep, send,
    all_s, up_s, down_s, hid_s, gi_s, n2t_s, glt_s, bias_s, sums, bias_sum, mixed,
):
    size, width = packed.shape
    step, steps = pl.program_id(0), pl.num_programs(0)
    me = own[0]
    units = up_s.shape[0]
    piece = units // CHUNKS

    @pl.when(step == 0)
    def _():
        spread_pieces(me, (mine, other), all_s)
        up_s[...] = all_s[:, :piece, :].reshape(units, width)
        down_s[...] = all_s[:, piece : 2 * piece, :].reshape(units, width)
        bias_s[...] = bias_line(all_s[:, 2 * piece, :piece], units)
        bias_sum[...] = jnp.zeros_like(bias_sum)
        sums[...] = jnp.zeros_like(sums)

    @pl.when(step < steps - 1)
    def _():
        mixed[...] = mixed_a[...]

    @pl.when(step == steps - 1)
    def _():
        mixed[...] = mixed_b[...]

    w_out_t = w_t[...].reshape(width, width)
    parts = [slice(k * sub, (k + 1) * sub) for k in range(size // sub)]
    rows = [pl.ds(pl.multiple_of(step * size + k * sub, sub), sub) for k in range(size // sub)]
    mids = [packed[at, :].astype(f32) + dot(mixed[:, at].T, w_out_t, NT) + vec[4:5, :] for at in parts]
    units_of = [norm_parts(middle) for middle in mids]
    lows = [(unit * vec[5:6, :] + vec[6:7, :]).astype(bf16) for unit, _ in units_of]
    valids = [
        lax.broadcasted_iota(jnp.int32, (sub, 1), 0) + step * size + k * sub < steps * size - 1
        for k in range(size // sub)
    ]
    outs = [jnp.where(valid, cot[at, :].astype(f32), 0.0) for valid, at in zip(valids, parts)]
    out_lows = [out.astype(bf16) for out in outs]
    us = [dot(low, up_s[...], NT) + bias_s[...] for low in lows]
    grads = [dot(out_low, down_s[...], NT) for out_low in out_lows]
    downs, backs = [], []
    for k in range(size // sub):
        n2t_s[:, rows[k]] = lows[k].T
        glt_s[:, rows[k]] = out_lows[k].T
        u = us[k]
        phi = 0.5 + 0.5 * lax.erf(u * (1.0 / math.sqrt(2.0)))
        hidden = (u * phi).astype(bf16)
        hid_s[rows[k], :] = hidden
        slope = phi + u * jnp.exp2(u * u * (-0.5 * LOG2E)) * (1.0 / math.sqrt(2.0 * math.pi))
        grad_in = grads[k] * slope
        bias_sum[...] += row_sums(grad_in)
        grad_in_low = grad_in.astype(bf16)
        gi_s[rows[k], :] = grad_in_low
        downs.append(dot(hidden, down_s[...]))
        backs.append(dot(grad_in_low, up_s[...]))
    totals = []
    for k, at in enumerate(parts):
        unit, inverse = units_of[k]
        layer_out[at, :] = jnp.where(valids[k], mids[k] + downs[k] + vec[7:8, :], 0.0).astype(bf16)
        n2_grad = backs[k]
        sums[8:16, :] += row_sums(n2_grad * unit)
        sums[16:24, :] += row_sums(n2_grad)
        total = outs[k] + norm_back(unit, inverse, vec[5:6, :], n2_grad)
        middle_grad[at, :] = total
        sums[0:8, :] += row_sums(total)
        sums[24:32, :] += row_sums(outs[k])
        totals.append(total.astype(bf16))
    for k, at in enumerate(parts):
        mixed_grad[at, :] = dot(totals[k], w_out_t).astype(bf16)

    @pl.when(step == steps - 1)
    def _():
        wide = 2 * width
        for lower in range(0, units, wide):
            hs = slice(lower, lower + wide)
            for index, (left, right) in enumerate(((n2t_s, gi_s), (glt_s, hid_s))):
                pieces = dot(left[...], right[:, hs]).T.astype(bf16).reshape(wide // piece, piece, width)
                store_pieces(me, lower // piece, pieces, keep, send, index * piece, 2 * piece)
        line = jnp.sum(bias_sum[...], axis=0, keepdims=True)
        lines = [jnp.sum(sums[8 * row : 8 * row + 8, :], axis=0, keepdims=True) for row in range(4)]
        lines += [line[:, row * width : (row + 1) * width] for row in range(units // width)]
        store_extra(lines, keep, send)


def store_extra(lines, keep, send):
    width = keep.shape[1]
    lines = jnp.concatenate(lines + [jnp.zeros((EXTRA - len(lines), width), f32)], axis=0)
    high, low = split_low(lines)
    base = keep.shape[0] - 2 * EXTRA
    for out in (keep, send):
        out[base : base + EXTRA, :] = high
        out[base + EXTRA :, :] = low


def feed_call(own, packed, mixed_a, mixed_b, cot, vec, w_t, mine, other):
    rows, width = packed.shape
    units = 4 * width
    size = mixed_b.shape[1]
    steps = rows // size
    row_block = pl.BlockSpec((size, width), lambda i: (i, 0))
    sent = (units + 2 * EXTRA, width)
    return kernel_call(
        functools.partial(feed_body, size),
        [
            SM,
            row_block,
            pl.BlockSpec((width, size), lambda i: (0, jnp.minimum(i, steps - 2))),
            whole(mixed_b.shape),
            row_block,
            whole((8, width)),
            pl.BlockSpec((CHUNKS // 4, units // CHUNKS, width), lambda i: (3, 0, 0)),
            whole(mine.shape),
            whole(other.shape),
        ],
        (S((rows, width), bf16), S((rows, width), f32), S((rows, width), bf16), S(sent, bf16), S(sent, bf16)),
        [
            pltpu.VMEM((CHUNKS, mine.shape[0] // HALF, width), bf16),
            pltpu.VMEM((units, width), bf16),
            pltpu.VMEM((units, width), bf16),
            pltpu.VMEM((rows, units), bf16),
            pltpu.VMEM((rows, units), bf16),
            pltpu.VMEM((width, rows), bf16),
            pltpu.VMEM((width, rows), bf16),
            pltpu.VMEM((1, units), f32),
            pltpu.VMEM((32, width), f32),
            pltpu.VMEM((8, units), f32),
            pltpu.VMEM((width, size), bf16),
        ],
        grid=(steps,),
        out_specs=(row_block, row_block, row_block, whole(sent), whole(sent)),
        flops=12 * rows * width * units + 6 * rows * width * width,
        micros=30,
        name="feed",
    )(own, packed, mixed_a, mixed_b, cot, vec, w_t, mine, other)


def side_body(mixed_a, mixed_b, middle_grad, out_grad):
    first = mixed_a.shape[1]
    total = dot(mixed_a[...], middle_grad[:first, :].astype(bf16))
    total += dot(mixed_b[...], middle_grad[first:, :].astype(bf16))
    out_grad[...] = total.T.astype(bf16)


def side_call(mixed_a, mixed_b, middle_grad):
    rows, width = middle_grad.shape
    return kernel_call(
        side_body,
        [VM] * 3,
        (S((width, width), bf16),),
        flops=2 * rows * width * width,
        micros=4,
        name="side",
    )(mixed_a, mixed_b, middle_grad)[0]


def back_body(
    own, seg, offs, counts, qkv, key_t, mixed_grad, stats, seg_rows, seg_cols,
    w_t, packed, normed_t, middle_grad, out_grad, vec,
    input_grad, keep, send, qkv_grad, key_grad, value_grad, sums,
):
    rows, width = packed.shape
    me = own[0]
    piece = w_t.shape[1]
    size = 512
    attend_back(seg, offs, counts, qkv, key_t, mixed_grad, stats, seg_rows, seg_cols, qkv_grad, key_grad, value_grad)
    weights = w_t[: 3 * HALF // 2].reshape(3 * width, width)
    sums[...] = jnp.zeros_like(sums)

    def one(i, carry):
        sl = tile_rows(i, size)
        qkv_grad[sl, width : 2 * width] = (key_grad[sl, :] * SCALE).astype(bf16)
        qkv_grad[sl, 2 * width :] = value_grad[sl, :].astype(bf16)
        grads = qkv_grad[sl, :]
        normed_grad = dot(grads, weights)
        unit, inverse = norm_parts(packed[sl, :].astype(f32))
        sums[0:8, :] += row_sums(normed_grad * unit)
        sums[8:16, :] += row_sums(normed_grad)
        sums[16:24, :] += row_sums(grads[:, :width].astype(f32))
        sums[24:32, :] += row_sums(grads[:, 2 * width :].astype(f32))
        input_grad[sl, :] = middle_grad[sl, :] + norm_back(unit, inverse, vec[0:1, :], normed_grad)
        return carry

    lax.fori_loop(0, rows // size, one, 0)
    for lower in range(0, 3 * width, width):
        pieces = dot(normed_t[...], qkv_grad[:, lower : lower + width]).T.astype(bf16)
        store_pieces(me, lower // piece, pieces.reshape(width // piece, piece, width), keep, send, 0, piece)
    store_pieces(me, 3 * width // piece, out_grad[...].reshape(width // piece, piece, width), keep, send, 0, piece)
    lines = [jnp.sum(sums[8 * row : 8 * row + 8, :], axis=0, keepdims=True) for row in range(4)]
    store_extra(lines, keep, send)


def back_call(
    own, seg, offs, counts, qkv, key_t, mixed_grad, stats, seg_rows, seg_cols,
    w_t, packed, normed_t, middle_grad, out_grad, vec,
):
    rows, width = packed.shape
    sent = S((HALF * w_t.shape[1] + 2 * EXTRA, width), bf16)
    return kernel_call(
        back_body,
        [SM] * 4 + [VM] * 12,
        (S((rows, width), f32), sent, sent),
        [
            pltpu.VMEM((rows, 3 * width), bf16),
            pltpu.VMEM((rows, width), f32),
            pltpu.VMEM((rows, width), f32),
            pltpu.VMEM((32, width), f32),
        ],
        flops=22 * rows * width * width,
        micros=34,
        name="back",
    )(
        own, seg, offs, counts, qkv, key_t, mixed_grad, stats, seg_rows, seg_cols,
        w_t, packed, normed_t, middle_grad, out_grad, vec,
    )


def unpack_body(win, first, count, offs, keep, input_grad, *refs):
    image_grads, slots = refs[-2], refs[-1]
    images_here, length = keep.shape
    rows, width = input_grad.shape
    before = lax.broadcasted_iota(jnp.int32, (length, length), 0)
    after = lax.broadcasted_iota(jnp.int32, (length, length), 1)
    tri = jnp.where(before <= after, 1.0, 0.0).astype(bf16)
    place = lax.broadcasted_iota(jnp.int32, (win, length), 0)

    @pl.when(pl.program_id(0) == 0)
    def _():
        kept = keep[...]
        ranks = dot(kept.astype(f32).astype(bf16), tri).astype(jnp.int32) - 1
        slots[...] = jnp.where(kept > 0, ranks, -4 * win)

    chosen, values = [], []
    for k in range(image_grads.shape[0]):
        i = first + pl.program_id(0) * image_grads.shape[0] + k
        base = pl.multiple_of(jnp.minimum((offs[i] // 8) * 8, rows - win), 8)
        shift = offs[i] - base
        chosen.append(jnp.where(place == slots[pl.ds(i, 1), :] + shift, 1.0, 0.0).astype(bf16))
        values.append(input_grad[pl.ds(base, win), :])
    highs = [value.astype(bf16) for value in values]
    rests = [(value - high.astype(f32)).astype(bf16) for value, high in zip(values, highs)]
    for k in range(image_grads.shape[0]):
        image_grads[k] = dot(chosen[k], highs[k], TN) + dot(chosen[k], rests[k], TN)


def unpack_call(first, count, offs, keep, input_grad, filled=None):
    images_here, length = keep.shape
    rows, width = input_grad.shape
    win = (length + 7 + 7) // 8 * 8
    size = 5
    out = pl.BlockSpec((size, length, width), lambda i: (first // size + i, 0, 0))
    extra_in = [] if filled is None else [pl.BlockSpec(memory_space=pl.ANY)]
    extra = [] if filled is None else [filled]
    return pl.pallas_call(
        functools.partial(unpack_body, win, first, count),
        grid=(count // size,),
        out_shape=S((images_here, length, width), f32),
        in_specs=[SM, whole(keep.shape), whole(input_grad.shape)] + extra_in,
        out_specs=out,
        scratch_shapes=[pltpu.VMEM((images_here, length), jnp.int32)],
        input_output_aliases={} if filled is None else {3: 0},
        compiler_params=pltpu.CompilerParams(vmem_limit_bytes=58 * 2**20),
        cost_estimate=pl.CostEstimate(flops=0, bytes_accessed=7 * 3_500_000, transcendentals=0),
        name="unpack",
    )(offs, keep, input_grad, *extra)


def to_halves(chunks):
    _, size, width = chunks.shape
    ordered = chunks.reshape(4, 4, 2, size, width).transpose(2, 1, 0, 3, 4).reshape(2, HALF * size, width)
    return ordered[0], ordered[1]


def from_halves(keep, send, parts, width):
    size = keep.shape[0] // HALF // parts
    both = jnp.stack([keep, send]).reshape(2, 4, 4, parts, size, width)
    return both.transpose(2, 1, 0, 3, 4, 5).reshape(CHUNKS, parts, size, width)


def adamw(weight, grad, first, second, average, count, rate, decay):
    first_new = BETA_ONE * first + (1.0 - BETA_ONE) * grad
    second_new = BETA_TWO * second + (1.0 - BETA_TWO) * grad * grad
    first_hat = first_new / (1.0 - jnp.power(BETA_ONE, count))
    second_hat = second_new / (1.0 - jnp.power(BETA_TWO, count))
    weight_new = weight - rate * (first_hat / (jnp.sqrt(second_hat) + ADAM_EPS) + decay * weight)
    average_new = AVERAGE_DECAY * average + (1.0 - AVERAGE_DECAY) * weight_new
    return (weight_new, first_new, second_new, average_new)


def adamw_with(weight, grad, first, second, average, one, two, rate, decay):
    first_new = BETA_ONE * first + (1.0 - BETA_ONE) * grad
    second_new = BETA_TWO * second + (1.0 - BETA_TWO) * grad * grad
    weight_new = weight - rate * ((first_new / one) / (jnp.sqrt(second_new / two) + ADAM_EPS) + decay * weight)
    average_new = AVERAGE_DECAY * average + (1.0 - AVERAGE_DECAY) * weight_new
    return (weight_new, first_new, second_new, average_new)


def finish_body(powers, own, in_a, in_b, in_c, known, *refs):
    states, outs = refs[:8], refs[8:]
    size = states[0].shape[0]
    received = (in_a, in_b, in_c)
    grad = own[:size, :]
    for other in received:
        grad = grad + other[:size, :].astype(f32)
    sums = [own[size:, :]]
    sums += [r[size : size + EXTRA, :].astype(f32) + r[size + EXTRA :, :].astype(f32) for r in received]
    sums = (sums[0] + sums[1]) + (sums[2] + sums[3])
    vec_grad = jnp.concatenate([sums[:4], known[:4, :]], axis=0)
    news = adamw_with(states[0][...], grad, *(r[...] for r in states[1:4]), powers[0], powers[1], MATRIX_RATE, WEIGHT_DECAY)
    vec_news = adamw_with(states[4][...], vec_grad, *(r[...] for r in states[5:8]), powers[0], powers[1], VECTOR_RATE, 0.0)
    for ref, value in zip(outs, (grad, *news, vec_grad, *vec_news)):
        ref[...] = value


def finish_call(powers, own, received, known, states):
    main, vec = S(states[0].shape, f32), S(states[4].shape, f32)
    return kernel_call(
        finish_body,
        [SM] + [VM] * 13,
        (main,) * 5 + (vec,) * 5,
        micros=2,
        name="finish",
    )(powers, own, *received, known, *states)


def body(
    images, keep_mask, kept_counts, pack_offsets, segment_ids, cotangent,
    attn_weight, ffn_weight, up_bias, vectors,
    attn_first, ffn_first, bias_first, vec_first,
    attn_second, ffn_second, bias_second, vec_second,
    attn_average, ffn_average, bias_average, vec_average, step,
):
    width = images.shape[2]
    rows = segment_ids.shape[0]
    both = ("dp", "mp")
    piece = attn_weight.shape[1]
    tree = lax.axis_size("dp") == 8 and lax.axis_size("mp") == 4
    bias_row = jnp.pad(up_bias.astype(bf16)[None, :], ((0, 15), (0, width - piece)))
    seg_rows = segment_ids.reshape(rows // BLK, BLK)
    placed = place_call(images, keep_mask, pack_offsets, rows)
    count = step[0].astype(f32)
    powers = jnp.stack([1.0 - jnp.power(BETA_ONE, count), 1.0 - jnp.power(BETA_TWO, count)])
    if tree:
        own = (lax.axis_index("dp") * 4 + lax.axis_index("mp")).astype(jnp.int32)[None]
        pieces = jnp.concatenate(
            [attn_weight.astype(bf16).T, ffn_weight[0].astype(bf16).T, ffn_weight[1].astype(bf16).T, bias_row], axis=0
        )
        lines = [pieces] + [over_line(pieces, k) for k in (1, 2, 3)]
        placed, *lines = tie(placed, *lines)
        attn_line = jnp.concatenate([line[:piece] for line in lines], axis=0)
        ffn_line = jnp.concatenate([line[piece:] for line in lines], axis=0)
        attn_mine = gather_plane(attn_line)
        normed, normed_t, seg_cols = norm_call(placed, seg_rows, vectors)
        attn_mine, normed, ffn_line = tie(attn_mine, normed, ffn_line)
        attn_other = over_core(attn_mine)
        attn_other, ffn_line = tie(attn_other, ffn_line)
        ffn_lines = [ffn_line] + [over_plane(ffn_line, k) for k in (1, 2, 3)]
    else:
        own = jnp.zeros((1,), jnp.int32)
        attn_all = lax.all_gather(attn_weight.astype(bf16).T, both, axis=0, tiled=True)
        ffn_all = lax.all_gather(jnp.swapaxes(ffn_weight.astype(bf16), 1, 2), both, axis=1, tiled=True)
        bias_all = lax.all_gather(up_bias.astype(bf16), both, axis=0, tiled=True)
        size = 4 * width // CHUNKS
        ffn_all = jnp.concatenate(
            [
                ffn_all[0].reshape(CHUNKS, size, width),
                ffn_all[1].reshape(CHUNKS, size, width),
                jnp.pad(bias_all.reshape(CHUNKS, 1, size), ((0, 0), (0, 15), (0, width - size))),
            ],
            axis=1,
        )
        attn_mine, attn_other = to_halves(attn_all.reshape(CHUNKS, size, width))
        ffn_mine, ffn_other = to_halves(ffn_all)
        normed, normed_t, seg_cols = norm_call(placed, seg_rows, vectors)
    qkv_bias = jnp.concatenate([vectors[2], jnp.zeros_like(vectors[2]), vectors[3]])[None, :]
    where = (segment_ids, pack_offsets, kept_counts)
    blocks = rows // BLK
    late = blocks // 4
    qkv, key_t, value_t, w_t, mixed_a, stats_a = attend_first_call(
        blocks - late, own, *where, normed, attn_mine, attn_other, qkv_bias, seg_rows, seg_cols
    )
    if tree:
        qkv, mixed_a, *ffn_lines = tie(qkv, mixed_a, *ffn_lines)
        ffn_mine = jnp.concatenate(ffn_lines, axis=0)
        ffn_other = over_core(ffn_mine)
    mixed_b, stats_b = attend_last_call(late, *where, qkv, value_t, seg_rows, seg_cols)
    if tree:
        mixed_b, ffn_mine, ffn_other = tie(mixed_b, ffn_mine, ffn_other)
    layer_out, middle_grad, mixed_grad, ffn_keep, ffn_send = feed_call(
        own, placed, mixed_a, mixed_b, cotangent, vectors, w_t, ffn_mine, ffn_other
    )
    stats = jnp.concatenate([stats_a, stats_b], axis=0)
    if tree:
        ffn_in = over_core(ffn_send)
    out_grad = side_call(mixed_a, mixed_b, middle_grad)
    if tree:
        out_grad, ffn_in = tie(out_grad, ffn_in)
        ffn_own, *ffn_out = combine_call(ffn_keep, [ffn_in], 4, EXTRA)
        out_grad, ffn_own, *ffn_out = tie(out_grad, ffn_own, *ffn_out)
        ffn_in = [over_plane(p, k + 1) for k, p in enumerate(ffn_out)]
    input_grad, attn_keep, attn_send = back_call(
        own, *where, qkv, key_t, mixed_grad, stats, seg_rows, seg_cols,
        w_t, placed, normed_t, middle_grad, out_grad, vectors,
    )
    attn_states = (attn_weight, attn_first, attn_second, attn_average)
    vec_states = (vectors, vec_first, vec_second, vec_average)
    early = images.shape[0] * 2 // 5
    if tree:
        input_grad, attn_send, *ffn_in = tie(input_grad, attn_send, *ffn_in)
        attn_in = over_core(attn_send)
        ffn_own, *ffn_out = combine_call(ffn_own, ffn_in, 4, EXTRA)
        ffn_own, attn_in, *ffn_out = tie(ffn_own, attn_in, *ffn_out)
        attn_own, *attn_out = combine_call(attn_keep, [attn_in], 4, EXTRA)
        attn_in = [over_plane(p, k + 1) for k, p in enumerate(attn_out)]
        ffn_in = [over_line(p, k + 1) for k, p in enumerate(ffn_out)]
        image_grads = unpack_call(0, early, pack_offsets, keep_mask, input_grad)
        image_grads, *attn_in = tie(image_grads, *attn_in)
        attn_own, *attn_out = combine_call(attn_own, attn_in, 4, EXTRA)
        attn_in = [over_line(p, k + 1) for k, p in enumerate(attn_out)]
        image_grads = unpack_call(early, images.shape[0] - early, pack_offsets, keep_mask, input_grad, image_grads)
        ffn_t = combine_call(ffn_own, ffn_in, 1, EXTRA)[0]
        image_grads, *attn_in = tie(image_grads, *attn_in)
        ffn_grad = jnp.swapaxes(ffn_t[: 2 * piece].reshape(2, piece, width), 1, 2)
        known = ffn_t[2 * piece :]
        finished = finish_call(powers, attn_own, attn_in, known, [v.T for v in attn_states] + list(vec_states))
        attn_grad, *attn_up = [v.T for v in finished[:5]]
        vec_grad, *vec_up = finished[5:]
        bias_sums = known[4:8]
    else:
        image_grads = unpack_call(0, images.shape[0], pack_offsets, keep_mask, input_grad)
        base = ffn_keep.shape[0] - 2 * EXTRA
        ffn_t = from_halves(ffn_keep[:base], ffn_send[:base], 2, width)
        ffn_t = jnp.swapaxes(ffn_t, 0, 1).reshape(2, 4 * width, width)
        ffn_t = lax.psum_scatter(ffn_t.astype(f32), both, scatter_dimension=1, tiled=True)
        ffn_grad = jnp.swapaxes(ffn_t, 1, 2)
        known = ffn_keep[base : base + EXTRA].astype(f32) + ffn_keep[base + EXTRA :].astype(f32)
        base = attn_keep.shape[0] - 2 * EXTRA
        attn_t = from_halves(attn_keep[:base], attn_send[:base], 1, width).reshape(4 * width, width)
        attn_grad = lax.psum_scatter(attn_t.astype(f32), both, scatter_dimension=0, tiled=True).T
        sums = attn_keep[base : base + EXTRA].astype(f32) + attn_keep[base + EXTRA :].astype(f32)
        sums = lax.psum(jnp.concatenate([sums[:4], known[:8]], axis=0), both)
        vec_grad, bias_sums = sums[:8], sums[8:]
        attn_up = adamw(attn_weight, attn_grad, *attn_states[1:], count, MATRIX_RATE, WEIGHT_DECAY)
        vec_up = adamw(vectors, vec_grad, *vec_states[1:], count, VECTOR_RATE, 0.0)
    index = lax.axis_index("dp") * lax.axis_size("mp") + lax.axis_index("mp")
    bias_grad = lax.dynamic_slice_in_dim(bias_sums.reshape(4 * width), index * piece, piece, 0)
    ffn_up = adamw(ffn_weight, ffn_grad, ffn_first, ffn_second, ffn_average, count, MATRIX_RATE, WEIGHT_DECAY)
    bias_up = adamw(up_bias, bias_grad, bias_first, bias_second, bias_average, count, VECTOR_RATE, 0.0)
    news = [part[k] for k in range(4) for part in (attn_up, ffn_up, bias_up, vec_up)]
    return (layer_out, image_grads, attn_grad, ffn_grad, bias_grad, vec_grad, *news)


def solution(mesh):
    both = ("dp", "mp")
    matrix, slab, line = P(None, both), P(None, None, both), P(both)
    states = (matrix, slab, line, P())
    return jax.shard_map(
        body,
        mesh=mesh,
        in_specs=(P(both, None, None), P(both, None), line, line, line, P(both, None), *states * 4, P()),
        out_specs=(P(both, None), P(both, None, None), *states, *states * 4),
        check_vma=False,
    )
```

profile of v0, /device:TPU:0, one launch (start us, length us, event | category | flops | bytes accessed | tf_op | source)
XLA Modules:
  0.0 186.6 jit_solution(4525159868111418292)
XLA Ops:
  3.2 5.1 %collective-permute-start.2 = (bf16[160,384]{1,0:T(8,128)(2,1)S(1)}, bf16[160,384]{1,0:T(8,128)(2,1)S(1)}, u32[]{:S(2)}, u32[]{:S(2)}) collective-permute-start(bf16[160,384]{1,0:T(8,128)(2,1)S(1)} %fusion.2), channel_id=1, source_target_pairs={{0,24},{4,28},{8,16},{12,20},{16,8},{20,12},{24,0},{28,4},{1,25},{... | collective-permute-start | bytes 368648 | tf_op jit(solution)/shard_map/ppermute | solution.py:172
  8.9 8.9 %place.1.packed = bf16[2048,384]{1,0:T(8,128)(2,1)} custom-call(s32[25]{0:T(128)} %offs.11, bf16[25,198,384]{2,1,0:T(8,128)(2,1)} %images.1, s32[25,198]{1,0:T(8,128)} %keep.5), custom_call_target="tpu_custom_call" | custom-call | flops 790732800 | bytes 31500000 | tf_op jit(solution)/shard_map/place/pallas_call | solution.py:211
  18.8 1.6 collective-permute-start.3
  22.5 7.4 %norm.1 = (bf16[2048,384]{1,0:T(8,128)(2,1)}, bf16[384,2048]{1,0:T(8,128)(2,1)}, s32[2048,128]{1,0:T(8,128)}) custom-call(bf16[2048,384]{1,0:T(8,128)(2,1)} %place.1.packed, s32[16,128]{1,0:T(8,128)} %bitcast.34, f32[8,384]{1,0:T(8,128)} %refs_4_.1), custom_call_target="tpu_custom_call" | custom-call | flops 9437184 | bytes 21000000 | tf_op jit(solution)/shard_map/norm/pallas_call | solution.py:245
  30.1 2.0 %collective-permute-done.6.other = bf16[768,384]{1,0:T(8,128)(2,1)S(1)} collective-permute-done((bf16[768,384]{1,0:T(8,128)(2,1)S(1)}, bf16[768,384]{1,0:T(8,128)(2,1)S(1)}, u32[]{:S(2)}, u32[]{:S(2)}) %collective-permute-start.6) | collective-permute-done | bytes 589856 | tf_op jit(solution)/shard_map/ppermute | solution.py:163
  32.1 2.4 %collective-permute-start.9 = (bf16[448,384]{1,0:T(8,128)(2,1)S(1)}, bf16[448,384]{1,0:T(8,128)(2,1)S(1)}, u32[]{:S(2)}, u32[]{:S(2)}) collective-permute-start(bf16[448,384]{1,0:T(8,128)(2,1)S(1)} %pad_maximum_fusion), channel_id=1, source_target_pairs={{0,6},{1,7},{2,4},{3,5},{4,2},{5,3},{6,0},{7,1},{8,14},{9,15},{10,... | collective-permute-start | bytes 1032200 | tf_op jit(solution)/shard_map/ppermute | solution.py:168
  37.0 19.9 %attend_first.1 = (bf16[2048,1152]{1,0:T(8,128)(2,1)}, bf16[384,2048]{1,0:T(8,128)(2,1)}, bf16[384,2048]{1,0:T(8,128)(2,1)}, bf16[32,48,384]{2,1,0:T(8,128)(2,1)...) custom-call(s32[1]{0:T(128)} %bitcast.own, s32[2048]{0:T(1024)} %seg.5, s32[25]{0:T(128)} %offs.11, s32[25]{0:T(128)} %counts.5, ...), custom_call_target="tpu_custom_call" | custom-call | flops 1811939328 | bytes 70000000 | tf_op jit(solution)/shard_map/attend_first/pallas_call | solution.py:347
  57.3 6.4 %attend_last.1 = (bf16[384,512]{1,0:T(8,128)(2,1)}, f32[4,768]{1,0:T(4,128)}) custom-call(s32[2048]{0:T(1024)} %seg.5, s32[25]{0:T(128)} %offs.11, s32[25]{0:T(128)} %counts.5, bf16[2048,1152]{1,0:T(8,128)(2,1)} %get-tuple-element.126.qkv, bf16[384,2048]{1,0:T(8,128)(2,1)} %get-tuple-element.127.value_t, s32[16,128]{1,0:T(8,128)} %bitcast.36, ...), custom_call_target="tpu_custom_call" | custom-call | flops 402653184 | bytes 17500000 | tf_op jit(solution)/shard_map/attend_last/pallas_call | solution.py:371
  64.8 31.5 %feed.1 = (bf16[2048,384]{1,0:T(8,128)(2,1)}, f32[2048,384]{1,0:T(8,128)}, bf16[2048,384]{1,0:T(8,128)(2,1)}, bf16[1568,384]{1,0:T(8,128)(2,1)}, bf16[1568,384]{1,0:T(8,128)(2,1)}) custom-call(s32[1]{0:T(128)} %bitcast.own, bf16[2048,384]{1,0:T(8,128)(2,1)} %place.1.packed, bf16[384,1536]{1,0:T(8,128)(2,1)} %get-tuple-element.125.mixed_a, ...), custom_call_target="tpu_custom_call" | custom-call | flops 16307453952 | bytes 105000000 | tf_op jit(solution)/shard_map/feed/pallas_call | solution.py:542
  97.1 4.2 %side.1.out_grad = bf16[384,384]{1,0:T(8,128)(2,1)} custom-call(bf16[384,1536]{1,0:T(8,128)(2,1)} %get-tuple-element.125.mixed_a, bf16[384,512]{1,0:T(8,128)(2,1)} %get-tuple-element.133.mixed_b, f32[2048,384]{1,0:T(8,128)} %get-tuple-element.143.middle_grad), custom_call_target="tpu_custom_call" | custom-call | flops 603979776 | bytes 14000000 | tf_op jit(solution)/shard_map/side/pallas_call | solution.py:586
  102.3 2.9 %combine.5 = (f32[400,384]{1,0:T(8,128)}, bf16[416,384]{1,0:T(8,128)(2,1)}, bf16[416,384]{1,0:T(8,128)(2,1)}, bf16[416,384]{1,0:T(8,128)(2,1)}) custom-call(bf16[1568,384]{1,0:T(8,128)(2,1)} %get-tuple-element.146.refs_0_, bf16[1568,384]{1,0:T(8,128)(2,1)} %copy-done), custom_call_target="tpu_custom_call" | custom-call | flops 602112 | bytes 7000000 | tf_op jit(solution)/shard_map/combine/pallas_call | solution.py:152
  106.4 1.5 collective-permute-start.13
  108.7 34.0 %back.1 = (f32[2048,384]{1,0:T(8,128)}, bf16[800,384]{1,0:T(8,128)(2,1)}, bf16[800,384]{1,0:T(8,128)(2,1)}) custom-call(s32[1]{0:T(128)} %bitcast.own, s32[2048]{0:T(1024)} %seg.5, s32[25]{0:T(128)} %offs.11, s32[25]{0:T(128)} %counts.5, bf16[2048,1152]{1,0:T(8,128)(2,1)} %get-tuple-element.126.qkv, bf16[384,2048]{1,0:T(8,128)(2,1)} %get-tuple-element.138.key_t, ...), custom_call_target="tpu_custom_call" | custom-call | flops 6643777536 | bytes 119000000 | tf_op jit(solution)/shard_map/back/pallas_call | solution.py:638
  143.6 2.2 %combine.6 = (f32[112,384]{1,0:T(8,128)}, bf16[128,384]{1,0:T(8,128)(2,1)}, bf16[128,384]{1,0:T(8,128)(2,1)}, bf16[128,384]{1,0:T(8,128)(2,1)}) custom-call(f32[400,384]{1,0:T(8,128)} %get-tuple-element.160.refs_0_, bf16[416,384]{1,0:T(8,128)(2,1)} %copy-done.4, bf16[416,384]{1,0:T(8,128)(2,1)} %copy-done.5, bf16[416,384]{1,0:T(8,128)(2,1)} %copy-done.6), custom_call_target="tpu_custom_call" | custom-call | flops 460800 | bytes 7000000 | tf_op jit(solution)/shard_map/combine/pallas_call | solution.py:152
  146.1 2.3 %collective-permute-start.23 = (bf16[128,384]{1,0:T(8,128)(2,1)}, bf16[128,384]{1,0:T(8,128)(2,1)S(1)}, u32[]{:S(2)}, u32[]{:S(2)}) collective-permute-start(bf16[128,384]{1,0:T(8,128)(2,1)} %get-tuple-element.188), channel_id=1, source_target_pairs={{0,16},{4,20},{8,24},{12,28},{16,0},{20,4},{24,8},{28,12},{1,17},{... | collective-permute-start | bytes 294920 | tf_op jit(solution)/shard_map/ppermute | solution.py:172
  148.4 1.9 collective-permute-start.24
  150.8 4.8 %unpack.2.refs_0_ = f32[25,198,384]{2,1,0:T(8,128)} custom-call(s32[25]{0:T(128)} %offs.11, s32[25,198]{1,0:T(8,128)} %keep.5, f32[2048,384]{1,0:T(8,128)} %get-tuple-element.158.input_grad), custom_call_target="tpu_custom_call" | custom-call | bytes 24500000 | tf_op jit(solution)/shard_map/unpack/pallas_call | solution.py:693
  155.6 2.3 %combine.7 = (f32[208,384]{1,0:T(8,128)}, bf16[224,384]{1,0:T(8,128)(2,1)}, bf16[224,384]{1,0:T(8,128)(2,1)}, bf16[224,384]{1,0:T(8,128)(2,1)}) custom-call(bf16[800,384]{1,0:T(8,128)(2,1)} %get-tuple-element.159.refs_0_, bf16[800,384]{1,0:T(8,128)(2,1)} %copy-done.1), custom_call_target="tpu_custom_call" | custom-call | flops 307200 | bytes 7000000 | tf_op jit(solution)/shard_map/combine/pallas_call | solution.py:152
  162.7 1.8 combine.9
  167.2 1.7 collective-permute-done.18.refs_3_
  169.6 1.9 %combine.8 = (f32[64,384]{1,0:T(8,128)}, bf16[80,384]{1,0:T(8,128)(2,1)}, bf16[80,384]{1,0:T(8,128)(2,1)}, bf16[80,384]{1,0:T(8,128)(2,1)}) custom-call(f32[208,384]{1,0:T(8,128)} %get-tuple-element.174.refs_0_, bf16[224,384]{1,0:T(8,128)(2,1)} %copy-done.7, bf16[224,384]{1,0:T(8,128)(2,1)} %copy-done.8, bf16[224,384]{1,0:T(8,128)(2,1)} %copy-done.9), custom_call_target="tpu_custom_call" | custom-call | flops 239616 | bytes 7000000 | tf_op jit(solution)/shard_map/combine/pallas_call | solution.py:152
  171.9 3.1 %collective-permute-start.20 = (bf16[80,384]{1,0:T(8,128)(2,1)}, bf16[80,384]{1,0:T(8,128)(2,1)S(1)}, u32[]{:S(2)}, u32[]{:S(2)}) collective-permute-start(bf16[80,384]{1,0:T(8,128)(2,1)} %get-tuple-element.179), channel_id=1, source_target_pairs={{0,16},{4,20},{8,24},{12,28},{16,0},{20,4},{24,8},{28,12},{1,17},{... | collective-permute-start | bytes 184328 | tf_op jit(solution)/shard_map/ppermute | solution.py:172
  177.9 5.9 %unpack.3 = f32[25,198,384]{2,1,0:T(8,128)} custom-call(s32[25]{0:T(128)} %offs.11, s32[25,198]{1,0:T(8,128)} %keep.5, f32[2048,384]{1,0:T(8,128)} %get-tuple-element.158.input_grad, f32[25,198,384]{2,1,0:T(8,128)} %unpack.2.refs_0_), custom_call_target="tpu_custom_call", output_to_operand_aliasing={{}: (3, {})} | custom-call | bytes 24500000 | tf_op jit(solution)/shard_map/unpack/pallas_call | solution.py:693
  184.5 2.0 %finish.1 = (f32[48,384]{1,0:T(8,128)}, f32[48,384]{1,0:T(8,128)}, f32[48,384]{1,0:T(8,128)}, f32[48,384]{1,0:T(8,128)}, f32[48,384]{1,0:T(8,128)}, /*index=5*/f...) custom-call(f32[2]{0:T(128)} %pad_maximum_fusion.4.powers, ...), custom_call_target="tpu_custom_call" | custom-call | bytes 7000000 | tf_op jit(solution)/shard_map/finish/pallas_call | solution.py:756
  (133 shorter events, 26.9 us)
Async XLA Ops:
  3.2 14.7 %collective-permute-start.2 = (bf16[160,384]{1,0:T(8,128)(2,1)S(1)}, bf16[160,384]{1,0:T(8,128)(2,1)S(1)}, u32[]{:S(2)}, u32[]{:S(2)}) collective-permute-start(bf16[160,384]{1,0:T(8,128)(2,1)S(1)} %fusion.2), channel_id=1, source_target_pairs={{0,24},{4,28},{8,16},{12,20},{16,8},{20,12},{24,0},{28,4},{1,25},{... | collective-permute-start | bytes 368648 | tf_op jit(solution)/shard_map/ppermute | solution.py:172
  8.3 10.4 %collective-permute-start.1 = (bf16[160,384]{1,0:T(8,128)(2,1)S(1)}, bf16[160,384]{1,0:T(8,128)(2,1)S(1)}, u32[]{:S(2)}, u32[]{:S(2)}) collective-permute-start(bf16[160,384]{1,0:T(8,128)(2,1)S(1)} %fusion.2), channel_id=1, source_target_pairs={{0,16},{4,20},{8,24},{12,28},{16,0},{20,4},{24,8},{28,12},{1,17},{... | collective-permute-start | bytes 368648 | tf_op jit(solution)/shard_map/ppermute | solution.py:172
  8.3 10.4 %collective-permute-start = (bf16[160,384]{1,0:T(8,128)(2,1)S(1)}, bf16[160,384]{1,0:T(8,128)(2,1)S(1)}, u32[]{:S(2)}, u32[]{:S(2)}) collective-permute-start(bf16[160,384]{1,0:T(8,128)(2,1)S(1)} %fusion.2), channel_id=1, source_target_pairs={{0,8},{4,12},{8,0},{12,4},{16,24},{20,28},{24,16},{28,20},{1,9},{5... | collective-permute-start | bytes 368648 | tf_op jit(solution)/shard_map/ppermute | solution.py:172
  18.8 11.2 %collective-permute-start.3 = (bf16[192,384]{1,0:T(8,128)(2,1)S(1)}, bf16[192,384]{1,0:T(8,128)(2,1)S(1)}, u32[]{:S(2)}, u32[]{:S(2)}) collective-permute-start(bf16[192,384]{1,0:T(8,128)(2,1)S(1)} %pad_maximum_fusion.1), channel_id=1, source_target_pairs={{0,2},{1,3},{2,0},{3,1},{4,6},{5,7},{6,4},{7,5},{8,10},{9,11},{10,... | collective-permute-start | bytes 442376 | tf_op jit(solution)/shard_map/ppermute | solution.py:168
  20.4 9.6 %collective-permute-start.5 = (bf16[192,384]{1,0:T(8,128)(2,1)S(1)}, bf16[192,384]{1,0:T(8,128)(2,1)S(1)}, u32[]{:S(2)}, u32[]{:S(2)}) collective-permute-start(bf16[192,384]{1,0:T(8,128)(2,1)S(1)} %pad_maximum_fusion.1), channel_id=1, source_target_pairs={{0,6},{1,7},{2,4},{3,5},{4,2},{5,3},{6,0},{7,1},{8,14},{9,15},{10,... | collective-permute-start | bytes 442376 | tf_op jit(solution)/shard_map/ppermute | solution.py:168
  21.9 8.0 %collective-permute-start.4 = (bf16[192,384]{1,0:T(8,128)(2,1)S(1)}, bf16[192,384]{1,0:T(8,128)(2,1)S(1)}, u32[]{:S(2)}, u32[]{:S(2)}) collective-permute-start(bf16[192,384]{1,0:T(8,128)(2,1)S(1)} %pad_maximum_fusion.1), channel_id=1, source_target_pairs={{0,4},{1,5},{2,6},{3,7},{4,0},{5,1},{6,2},{7,3},{8,12},{9,13},{10,... | collective-permute-start | bytes 442376 | tf_op jit(solution)/shard_map/ppermute | solution.py:168
  32.1 24.8 %collective-permute-start.9 = (bf16[448,384]{1,0:T(8,128)(2,1)S(1)}, bf16[448,384]{1,0:T(8,128)(2,1)S(1)}, u32[]{:S(2)}, u32[]{:S(2)}) collective-permute-start(bf16[448,384]{1,0:T(8,128)(2,1)S(1)} %pad_maximum_fusion), channel_id=1, source_target_pairs={{0,6},{1,7},{2,4},{3,5},{4,2},{5,3},{6,0},{7,1},{8,14},{9,15},{10,... | collective-permute-start | bytes 1032200 | tf_op jit(solution)/shard_map/ppermute | solution.py:168
  34.6 22.4 %collective-permute-start.8 = (bf16[448,384]{1,0:T(8,128)(2,1)S(1)}, bf16[448,384]{1,0:T(8,128)(2,1)S(1)}, u32[]{:S(2)}, u32[]{:S(2)}) collective-permute-start(bf16[448,384]{1,0:T(8,128)(2,1)S(1)} %pad_maximum_fusion), channel_id=1, source_target_pairs={{0,4},{1,5},{2,6},{3,7},{4,0},{5,1},{6,2},{7,3},{8,12},{9,13},{10,... | collective-permute-start | bytes 1032200 | tf_op jit(solution)/shard_map/ppermute | solution.py:168
  35.1 21.9 %collective-permute-start.7 = (bf16[448,384]{1,0:T(8,128)(2,1)S(1)}, bf16[448,384]{1,0:T(8,128)(2,1)S(1)}, u32[]{:S(2)}, u32[]{:S(2)}) collective-permute-start(bf16[448,384]{1,0:T(8,128)(2,1)S(1)} %pad_maximum_fusion), channel_id=1, source_target_pairs={{0,2},{1,3},{2,0},{3,1},{4,6},{5,7},{6,4},{7,5},{8,10},{9,11},{10,... | collective-permute-start | bytes 1032200 | tf_op jit(solution)/shard_map/ppermute | solution.py:168
  57.2 6.5 %collective-permute-start.10 = (bf16[1792,384]{1,0:T(8,128)(2,1)S(1)}, bf16[1792,384]{1,0:T(8,128)(2,1)S(1)}, u32[]{:S(2)}, u32[]{:S(2)}) collective-permute-start(bf16[1792,384]{1,0:T(8,128)(2,1)S(1)} %constant_dynamic-update-slice_fusion.7.mine), channel_id=1, source_target_pairs={{0,1},{1,0},{2,3},{3,2},{4,5},{5,4},{6,7},{7,6},{8,9},{9,8},{10,11... | collective-permute-start | bytes 4128776 | tf_op jit(solution)/shard_map/ppermute | solution.py:163
  96.3 4.9 %collective-permute-start.11 = (bf16[1568,384]{1,0:T(8,128)(2,1)}, bf16[1568,384]{1,0:T(8,128)(2,1)S(1)}, u32[]{:S(2)}, u32[]{:S(2)}) collective-permute-start(bf16[1568,384]{1,0:T(8,128)(2,1)} %get-tuple-element.144), channel_id=1, source_target_pairs={{0,1},{1,0},{2,3},{3,2},{4,5},{5,4},{6,7},{7,6},{8,9},{9,8},{10,11... | collective-permute-start | bytes 3612680 | tf_op jit(solution)/shard_map/ppermute | solution.py:163
  105.2 37.5 %collective-permute-start.12 = (bf16[416,384]{1,0:T(8,128)(2,1)}, bf16[416,384]{1,0:T(8,128)(2,1)S(1)}, u32[]{:S(2)}, u32[]{:S(2)}) collective-permute-start(bf16[416,384]{1,0:T(8,128)(2,1)} %get-tuple-element.155), channel_id=1, source_target_pairs={{0,2},{1,3},{2,0},{3,1},{4,6},{5,7},{6,4},{7,5},{8,10},{9,11},{10,... | collective-permute-start | bytes 958472 | tf_op jit(solution)/shard_map/ppermute | solution.py:168
  106.4 36.3 %collective-permute-start.13 = (bf16[416,384]{1,0:T(8,128)(2,1)}, bf16[416,384]{1,0:T(8,128)(2,1)S(1)}, u32[]{:S(2)}, u32[]{:S(2)}) collective-permute-start(bf16[416,384]{1,0:T(8,128)(2,1)} %get-tuple-element.156), channel_id=1, source_target_pairs={{0,4},{1,5},{2,6},{3,7},{4,0},{5,1},{6,2},{7,3},{8,12},{9,13},{10,... | collective-permute-start | bytes 958472 | tf_op jit(solution)/shard_map/ppermute | solution.py:168
  107.9 34.8 %collective-permute-start.14 = (bf16[416,384]{1,0:T(8,128)(2,1)}, bf16[416,384]{1,0:T(8,128)(2,1)S(1)}, u32[]{:S(2)}, u32[]{:S(2)}) collective-permute-start(bf16[416,384]{1,0:T(8,128)(2,1)} %get-tuple-element.157), channel_id=1, source_target_pairs={{0,6},{1,7},{2,4},{3,5},{4,2},{5,3},{6,0},{7,1},{8,14},{9,15},{10,... | collective-permute-start | bytes 958472 | tf_op jit(solution)/shard_map/ppermute | solution.py:168
  142.7 3.1 %collective-permute-start.15 = (bf16[800,384]{1,0:T(8,128)(2,1)}, bf16[800,384]{1,0:T(8,128)(2,1)S(1)}, u32[]{:S(2)}, u32[]{:S(2)}) collective-permute-start(bf16[800,384]{1,0:T(8,128)(2,1)} %get-tuple-element.165), channel_id=1, source_target_pairs={{0,1},{1,0},{2,3},{3,2},{4,5},{5,4},{6,7},{7,6},{8,9},{9,8},{10,11... | collective-permute-start | bytes 1843208 | tf_op jit(solution)/shard_map/ppermute | solution.py:163
  145.8 14.6 %collective-permute-start.22 = (bf16[128,384]{1,0:T(8,128)(2,1)}, bf16[128,384]{1,0:T(8,128)(2,1)S(1)}, u32[]{:S(2)}, u32[]{:S(2)}) collective-permute-start(bf16[128,384]{1,0:T(8,128)(2,1)} %get-tuple-element.187), channel_id=1, source_target_pairs={{0,8},{4,12},{8,0},{12,4},{16,24},{20,28},{24,16},{28,20},{1,9},{5... | collective-permute-start | bytes 294920 | tf_op jit(solution)/shard_map/ppermute | solution.py:172
  146.1 15.4 %collective-permute-start.23 = (bf16[128,384]{1,0:T(8,128)(2,1)}, bf16[128,384]{1,0:T(8,128)(2,1)S(1)}, u32[]{:S(2)}, u32[]{:S(2)}) collective-permute-start(bf16[128,384]{1,0:T(8,128)(2,1)} %get-tuple-element.188), channel_id=1, source_target_pairs={{0,16},{4,20},{8,24},{12,28},{16,0},{20,4},{24,8},{28,12},{1,17},{... | collective-permute-start | bytes 294920 | tf_op jit(solution)/shard_map/ppermute | solution.py:172
  148.4 13.1 %collective-permute-start.24 = (bf16[128,384]{1,0:T(8,128)(2,1)}, bf16[128,384]{1,0:T(8,128)(2,1)S(1)}, u32[]{:S(2)}, u32[]{:S(2)}) collective-permute-start(bf16[128,384]{1,0:T(8,128)(2,1)} %get-tuple-element.189), channel_id=1, source_target_pairs={{0,24},{4,28},{8,16},{12,20},{16,8},{20,12},{24,0},{28,4},{1,25},{... | collective-permute-start | bytes 294920 | tf_op jit(solution)/shard_map/ppermute | solution.py:172
  157.9 9.2 %collective-permute-start.16 = (bf16[224,384]{1,0:T(8,128)(2,1)}, bf16[224,384]{1,0:T(8,128)(2,1)S(1)}, u32[]{:S(2)}, u32[]{:S(2)}) collective-permute-start(bf16[224,384]{1,0:T(8,128)(2,1)} %get-tuple-element.170), channel_id=1, source_target_pairs={{0,2},{1,3},{2,0},{3,1},{4,6},{5,7},{6,4},{7,5},{8,10},{9,11},{10,... | collective-permute-start | bytes 516104 | tf_op jit(solution)/shard_map/ppermute | solution.py:168
  159.0 8.2 %collective-permute-start.17 = (bf16[224,384]{1,0:T(8,128)(2,1)}, bf16[224,384]{1,0:T(8,128)(2,1)S(1)}, u32[]{:S(2)}, u32[]{:S(2)}) collective-permute-start(bf16[224,384]{1,0:T(8,128)(2,1)} %get-tuple-element.171), channel_id=1, source_target_pairs={{0,4},{1,5},{2,6},{3,7},{4,0},{5,1},{6,2},{7,3},{8,12},{9,13},{10,... | collective-permute-start | bytes 516104 | tf_op jit(solution)/shard_map/ppermute | solution.py:168
  160.4 8.5 %collective-permute-start.18 = (bf16[224,384]{1,0:T(8,128)(2,1)}, bf16[224,384]{1,0:T(8,128)(2,1)S(1)}, u32[]{:S(2)}, u32[]{:S(2)}) collective-permute-start(bf16[224,384]{1,0:T(8,128)(2,1)} %get-tuple-element.172), channel_id=1, source_target_pairs={{0,6},{1,7},{2,4},{3,5},{4,2},{5,3},{6,0},{7,1},{8,14},{9,15},{10,... | collective-permute-start | bytes 516104 | tf_op jit(solution)/shard_map/ppermute | solution.py:168
  171.5 12.2 %collective-permute-start.19 = (bf16[80,384]{1,0:T(8,128)(2,1)}, bf16[80,384]{1,0:T(8,128)(2,1)S(1)}, u32[]{:S(2)}, u32[]{:S(2)}) collective-permute-start(bf16[80,384]{1,0:T(8,128)(2,1)} %get-tuple-element.178), channel_id=1, source_target_pairs={{0,8},{4,12},{8,0},{12,4},{16,24},{20,28},{24,16},{28,20},{1,9},{5... | collective-permute-start | bytes 184328 | tf_op jit(solution)/shard_map/ppermute | solution.py:172
  171.9 11.9 %collective-permute-start.20 = (bf16[80,384]{1,0:T(8,128)(2,1)}, bf16[80,384]{1,0:T(8,128)(2,1)S(1)}, u32[]{:S(2)}, u32[]{:S(2)}) collective-permute-start(bf16[80,384]{1,0:T(8,128)(2,1)} %get-tuple-element.179), channel_id=1, source_target_pairs={{0,16},{4,20},{8,24},{12,28},{16,0},{20,4},{24,8},{28,12},{1,17},{... | collective-permute-start | bytes 184328 | tf_op jit(solution)/shard_map/ppermute | solution.py:172
  175.0 8.8 %collective-permute-start.21 = (bf16[80,384]{1,0:T(8,128)(2,1)}, bf16[80,384]{1,0:T(8,128)(2,1)S(1)}, u32[]{:S(2)}, u32[]{:S(2)}) collective-permute-start(bf16[80,384]{1,0:T(8,128)(2,1)} %get-tuple-element.180), channel_id=1, source_target_pairs={{0,24},{4,28},{8,16},{12,20},{16,8},{20,12},{24,0},{28,4},{1,25},{... | collective-permute-start | bytes 184328 | tf_op jit(solution)/shard_map/ppermute | solution.py:172
  (30 other events, 212.6 us)
where the time goes:
time: 188 us; the launch traced here: 187 us
  Pallas kernels  136 us (72%)
  starting transfers between devices  29 us (15%)
  local copies, waits for them, and re-layouts  9.65 us (5%)
  other arithmetic  5.3 us (3%)
  waiting for transfers between devices  4.6 us (2%)
  between operations  2.08 us (1%)
    pallas_call x1, Pallas kernels, back_call(): kernel_call(back_body, [SM] * 4 + [VM] * 12, (S((rows, width), f32), sent...  34 us
    pallas_call x1, Pallas kernels, feed_call(): kernel_call(functools.partial(feed_body, size), [SM, row_block, pl.BlockS...  31.5 us
    pallas_call x1, Pallas kernels, attend_first_call(): kernel_call(attend_first_body, [SM, SM, SM, SM, VM, VM, VM, VM, VM, VM],...  19.9 us
    ppermute x9, starting transfers between devices, over_line(): lax.ppermute(values, 'dp', [(i, i ^ 2 * apart) for i in range(lax.axis_si...  14.6 us
    ppermute x12, starting transfers between devices, over_plane(): lax.ppermute(values, ('dp', 'mp'), [(i, i ^ 2 * apart) for i in range(dev...  14.1 us
    pallas_call x5, Pallas kernels, combine_call(): kernel_call(functools.partial(combine_body, parts, size, extra, len(recei...  11.1 us
    pallas_call x2, Pallas kernels, unpack_call(): pl.pallas_call(functools.partial(unpack_body, win, first, count), grid=(c...  10.6 us
    pallas_call x1, Pallas kernels, place_call(): kernel_call(functools.partial(place_body, win), [SM, VM, VM], (S((rows, w...  8.92 us
  transfers between devices with their start and end apart: 25, of which 3 were waited for; matrix products, arithmetic and copies ran while one was open for 4% of the time, Pallas kernels for 52%

commit v1 on v0

--- a/solution.py
+++ b/solution.py
@@ -40,6 +40,7 @@
 TN = (((0,), (0,)), ((), ()))
 VM = pl.BlockSpec(memory_space=pltpu.VMEM)
 SM = pl.BlockSpec(memory_space=pltpu.SMEM)
+HB = pl.BlockSpec(memory_space=pl.ANY)
 S = jax.ShapeDtypeStruct
 
 
@@ -91,9 +92,12 @@
     return pl.ds(pl.multiple_of(count * size, size), size)
 
 
-def place_of(own, other):
-    apart = lax.shift_right_logical(own, 1) ^ (other // 2)
+def plane_first(apart):
     return (apart & 3) * 4 + lax.shift_right_logical(apart, 2)
+
+
+def line_first(apart):
+    return apart
 
 
 def spread_pieces(own, halves, out):
@@ -103,11 +107,12 @@
             out[own ^ apart] = halves[near][slot * out.shape[1] : (slot + 1) * out.shape[1], :]
 
 
-def store_pieces(own, start, pieces, keep, send, at, step):
+def store_pieces(own, start, pieces, keep, send, at, step, order):
     count, size, _ = pieces.shape
     odd = (own & 1) == 1
     for e in range(0, count, 2):
-        row = pl.multiple_of(place_of(own, start + e) * step + at, 16)
+        apart = lax.shift_right_logical(own, 1) ^ ((start + e) // 2)
+        row = pl.multiple_of(order(apart) * step + at, 16)
         even_piece, odd_piece = pieces[e], pieces[e + 1]
         keep[pl.ds(row, size), :] = jnp.where(odd, odd_piece, even_piece)
         send[pl.ds(row, size), :] = jnp.where(odd, even_piece, odd_piece)
@@ -275,8 +280,10 @@
     return jnp.concatenate([lim, lim], axis=1)
 
 
-def over_windows(seg, offs, counts, tiles, base, first, blocks, block):
+def over_windows(seg, offs, counts, tiles, base, first, blocks, block, before=None):
     def one(j, carry):
+        if before is not None:
+            before(j)
         low, size = window(seg, offs, counts, j, offs.shape[0], tiles)
         for n in range(2, REACH + 1):
 
@@ -319,46 +326,62 @@
 
 
 def attend_first_body(
-    own, seg, offs, counts, normed, mine, other, bias, seg_rows, seg_cols,
-    qkv, key_t, value_t, w_t, mixed_t, stats,
+    own, seg, offs, counts, normed, mine, other, vec, seg_rows, seg_cols,
+    qkv_out, key_out, value_out, w_out, mixed_t, stats,
+    qkv, key_t, value_t, w_t, sems,
 ):
     rows, width = normed.shape
+    size = 512
     spread_pieces(own[0], (mine, other), w_t)
     units = w_t.shape[0] * w_t.shape[1]
     weights = w_t[...].reshape(units, width)[: 3 * width]
+    bias = jnp.concatenate([vec[2:3, :], jnp.zeros((1, width), f32), vec[3:4, :]], axis=1)
+    last = pltpu.make_async_copy(w_t, w_out, sems.at[3, 0])
+    last.start()
+
+    def copies(i):
+        sl = tile_rows(i, size)
+        return [
+            pltpu.make_async_copy(qkv.at[sl, :], qkv_out.at[sl, :], sems.at[0, i]),
+            pltpu.make_async_copy(key_t.at[:, sl], key_out.at[:, sl], sems.at[1, i]),
+            pltpu.make_async_copy(value_t.at[:, sl], value_out.at[:, sl], sems.at[2, i]),
+        ]
 
     def project(i, carry):
-        sl = tile_rows(i, 512)
-        low = (dot(normed[sl, :], weights, NT) + bias[...]).astype(bf16)
+        sl = tile_rows(i, size)
+        low = (dot(normed[sl, :], weights, NT) + bias).astype(bf16)
         qkv[sl, :] = low
         key_t[:, sl] = low[:, width : 2 * width].T
         value_t[:, sl] = low[:, 2 * width :].T
+        for copy in copies(i):
+            copy.start()
         return carry
 
-    lax.fori_loop(0, rows // 512, project, 0)
+    lax.fori_loop(0, rows // size, project, 0)
     attend_blocks(
         0, 0, mixed_t.shape[1] // BLK, seg, offs, counts, qkv, value_t, seg_rows, seg_cols, mixed_t, stats
     )
-
-
-def attend_first_call(blocks, own, seg, offs, counts, normed, mine, other, bias, seg_rows, seg_cols):
+    for i in range(rows // size):
+        for copy in copies(i):
+            copy.wait()
+    last.wait()
+
+
+def attend_first_call(blocks, own, seg, offs, counts, normed, mine, other, vec, seg_rows, seg_cols):
     rows, width = normed.shape
     piece = mine.shape[0] // HALF
+    kept = ((rows, 3 * width), (width, rows), (width, rows), (CHUNKS, piece, width))
     return kernel_call(
         attend_first_body,
         [SM, SM, SM, SM, VM, VM, VM, VM, VM, VM],
-        (
-            S((rows, 3 * width), bf16),
-            S((width, rows), bf16),
-            S((width, rows), bf16),
-            S((CHUNKS, piece, width), bf16),
-            S((width, blocks * BLK), bf16),
-            S((blocks, HEADS * BLK), f32),
-        ),
+        tuple(S(shape, bf16) for shape in kept)
+        + (S((width, blocks * BLK), bf16), S((blocks, HEADS * BLK), f32)),
+        [pltpu.VMEM(shape, bf16) for shape in kept] + [pltpu.SemaphoreType.DMA((4, rows // 512))],
         flops=2 * rows * width * 3 * width,
         micros=20,
         name="attend_first",
-    )(own, seg, offs, counts, normed, mine, other, bias, seg_rows, seg_cols)
+        out_specs=(HB, HB, HB, HB, VM, VM),
+    )(own, seg, offs, counts, normed, mine, other, vec, seg_rows, seg_cols)
 
 
 def attend_last_call(blocks, seg, offs, counts, qkv, value_t, seg_rows, seg_cols):
@@ -388,10 +411,14 @@
     )(seg, offs, counts, qkv, value_t, seg_rows, seg_cols)
 
 
-def attend_back(seg, offs, counts, qkv, key_t, mixed_grad, stats, seg_rows, seg_cols, qkv_grad, key_grad, value_grad):
+def attend_back(
+    seg, offs, counts, qkv, key_t, mixed_grad, stats_a, stats_b, seg_rows, seg_cols, qkv_grad, key_grad, value_grad, stats, before
+):
     rows, width = mixed_grad.shape
     key_grad[...] = jnp.zeros_like(key_grad)
     value_grad[...] = jnp.zeros_like(value_grad)
+    stats[: stats_a.shape[0], :] = stats_a[...]
+    stats[stats_a.shape[0] :, :] = stats_b[...]
 
     def block(j, keys):
         here = tile_rows(j, BLK)
@@ -422,7 +449,7 @@
             joined = jnp.concatenate([query_t[:HEAD, :BLK], query_t[HEAD:, BLK:]], axis=0)
             qkv_grad[here, ats[p]] = joined.T.astype(bf16)
 
-    over_windows(seg, offs, counts, rows // BLK, 0, 0, rows // BLK, block)
+    over_windows(seg, offs, counts, rows // BLK, 0, 0, rows // BLK, block, before)
 
 
 def bias_line(rows_of, units):
@@ -515,7 +542,7 @@
             hs = slice(lower, lower + wide)
             for index, (left, right) in enumerate(((n2t_s, gi_s), (glt_s, hid_s))):
                 pieces = dot(left[...], right[:, hs]).T.astype(bf16).reshape(wide // piece, piece, width)
-                store_pieces(me, lower // piece, pieces, keep, send, index * piece, 2 * piece)
+                store_pieces(me, lower // piece, pieces, keep, send, index * piece, 2 * piece, line_first)
         line = jnp.sum(bias_sum[...], axis=0, keepdims=True)
         lines = [jnp.sum(sums[8 * row : 8 * row + 8, :], axis=0, keepdims=True) for row in range(4)]
         lines += [line[:, row * width : (row + 1) * width] for row in range(units // width)]
@@ -594,17 +621,62 @@
 
 
 def back_body(
-    own, seg, offs, counts, qkv, key_t, mixed_grad, stats, seg_rows, seg_cols,
-    w_t, packed, normed_t, middle_grad, out_grad, vec,
-    input_grad, keep, send, qkv_grad, key_grad, value_grad, sums,
+    own, seg, offs, counts, qkv_in, key_in, mixed_in, stats_a, stats_b, seg_rows, seg_cols,
+    w_in, packed_in, normed_in, middle_in, out_grad, vec,
+    input_out, keep, send,
+    qkv, key_t, mixed_grad, w_t, packed, normed_t, middle_grad, input_grad,
+    qkv_grad, key_grad, value_grad, stats, sums, sems, late_sems, out_sems,
 ):
     rows, width = packed.shape
     me = own[0]
     piece = w_t.shape[1]
     size = 512
-    attend_back(seg, offs, counts, qkv, key_t, mixed_grad, stats, seg_rows, seg_cols, qkv_grad, key_grad, value_grad)
+
+    def early(i):
+        sl = tile_rows(i, size)
+        return [
+            pltpu.make_async_copy(qkv_in.at[sl, :], qkv.at[sl, :], sems.at[0, i]),
+            pltpu.make_async_copy(key_in.at[:, sl], key_t.at[:, sl], sems.at[1, i]),
+            pltpu.make_async_copy(mixed_in.at[sl, :], mixed_grad.at[sl, :], sems.at[2, i]),
+        ]
+
+    late = [
+        pltpu.make_async_copy(source, target, late_sems.at[k])
+        for k, (source, target) in enumerate(
+            ((w_in, w_t), (packed_in, packed), (middle_in, middle_grad), (normed_in, normed_t))
+        )
+    ]
+    for i in range(rows // size):
+        for copy in early(i):
+            copy.start()
+    for copy in late:
+        copy.start()
+
+    def before(j):
+        step = size // BLK
+
+        @pl.when(j == 0)
+        def _():
+            for copy in early(0):
+                copy.wait()
+
+        @pl.when(((j + 2) % step == 0) & ((j + 2) // step < rows // size))
+        def _():
+            for copy in early((j + 2) // step):
+                copy.wait()
+
+    attend_back(
+        seg, offs, counts, qkv, key_t, mixed_grad, stats_a, stats_b, seg_rows, seg_cols,
+        qkv_grad, key_grad, value_grad, stats, before,
+    )
+    for copy in late:
+        copy.wait()
     weights = w_t[: 3 * HALF // 2].reshape(3 * width, width)
     sums[...] = jnp.zeros_like(sums)
+
+    def result(i):
+        sl = tile_rows(i, size)
+        return pltpu.make_async_copy(input_grad.at[sl, :], input_out.at[sl, :], out_sems.at[i])
 
     def one(i, carry):
         sl = tile_rows(i, size)
@@ -618,38 +690,52 @@
         sums[16:24, :] += row_sums(grads[:, :width].astype(f32))
         sums[24:32, :] += row_sums(grads[:, 2 * width :].astype(f32))
         input_grad[sl, :] = middle_grad[sl, :] + norm_back(unit, inverse, vec[0:1, :], normed_grad)
+        result(i).start()
         return carry
 
     lax.fori_loop(0, rows // size, one, 0)
     for lower in range(0, 3 * width, width):
         pieces = dot(normed_t[...], qkv_grad[:, lower : lower + width]).T.astype(bf16)
-        store_pieces(me, lower // piece, pieces.reshape(width // piece, piece, width), keep, send, 0, piece)
-    store_pieces(me, 3 * width // piece, out_grad[...].reshape(width // piece, piece, width), keep, send, 0, piece)
+        pieces = pieces.reshape(width // piece, piece, width)
+        store_pieces(me, lower // piece, pieces, keep, send, 0, piece, plane_first)
+    pieces = out_grad[...].reshape(width // piece, piece, width)
+    store_pieces(me, 3 * width // piece, pieces, keep, send, 0, piece, plane_first)
     lines = [jnp.sum(sums[8 * row : 8 * row + 8, :], axis=0, keepdims=True) for row in range(4)]
     store_extra(lines, keep, send)
+    for i in range(rows // size):
+        result(i).wait()
 
 
 def back_call(
-    own, seg, offs, counts, qkv, key_t, mixed_grad, stats, seg_rows, seg_cols,
+    own, seg, offs, counts, qkv, key_t, mixed_grad, stats_a, stats_b, seg_rows, seg_cols,
     w_t, packed, normed_t, middle_grad, out_grad, vec,
 ):
     rows, width = packed.shape
     sent = S((HALF * w_t.shape[1] + 2 * EXTRA, width), bf16)
+    moved = (qkv, key_t, mixed_grad, w_t, packed, normed_t, middle_grad)
+    tiles = rows // 512
     return kernel_call(
         back_body,
-        [SM] * 4 + [VM] * 12,
+        [SM] * 4 + [HB] * 3 + [VM] * 4 + [HB] * 4 + [VM] * 2,
         (S((rows, width), f32), sent, sent),
-        [
+        [pltpu.VMEM(v.shape, v.dtype) for v in moved]
+        + [
+            pltpu.VMEM((rows, width), f32),
             pltpu.VMEM((rows, 3 * width), bf16),
             pltpu.VMEM((rows, width), f32),
             pltpu.VMEM((rows, width), f32),
+            pltpu.VMEM((rows // BLK, HEADS * BLK), f32),
             pltpu.VMEM((32, width), f32),
+            pltpu.SemaphoreType.DMA((3, tiles)),
+            pltpu.SemaphoreType.DMA((4,)),
+            pltpu.SemaphoreType.DMA((tiles,)),
         ],
         flops=22 * rows * width * width,
-        micros=34,
+        micros=30,
         name="back",
+        out_specs=(HB, VM, VM),
     )(
-        own, seg, offs, counts, qkv, key_t, mixed_grad, stats, seg_rows, seg_cols,
+        own, seg, offs, counts, qkv, key_t, mixed_grad, stats_a, stats_b, seg_rows, seg_cols,
         w_t, packed, normed_t, middle_grad, out_grad, vec,
     )
 
@@ -682,7 +768,8 @@
         image_grads[k] = dot(chosen[k], highs[k], TN) + dot(chosen[k], rests[k], TN)
 
 
-def unpack_call(first, count, offs, keep, input_grad, filled=None):
+def unpack_call(offs, keep, input_grad, first, last, filled=None):
+    count = last - first
     images_here, length = keep.shape
     rows, width = input_grad.shape
     win = (length + 7 + 7) // 8 * 8
@@ -710,10 +797,11 @@
     return ordered[0], ordered[1]
 
 
-def from_halves(keep, send, parts, width):
+def from_halves(keep, send, parts, width, line_first):
     size = keep.shape[0] // HALF // parts
     both = jnp.stack([keep, send]).reshape(2, 4, 4, parts, size, width)
-    return both.transpose(2, 1, 0, 3, 4, 5).reshape(CHUNKS, parts, size, width)
+    both = both.transpose((1, 2, 0, 3, 4, 5) if line_first else (2, 1, 0, 3, 4, 5))
+    return both.reshape(CHUNKS, parts, size, width)
 
 
 def adamw(weight, grad, first, second, average, count, rate, decay):
@@ -726,6 +814,80 @@
     return (weight_new, first_new, second_new, average_new)
 
 
+def wide_of(ref, rows):
+    return ref[rows, :].astype(f32)
+
+
+def whole_extra(ref):
+    return wide_of(ref, slice(-2 * EXTRA, -EXTRA)) + wide_of(ref, slice(-EXTRA, None))
+
+
+def paired(values):
+    while len(values) > 1:
+        values = [values[i] + values[i + 1] for i in range(0, len(values), 2)]
+    return values[0]
+
+
+def put_extra(values, out, pieces):
+    high, low = split_low(values)
+    out[-EXTRA:, :] = high.astype(f32) + low.astype(f32)
+    for piece in pieces:
+        piece[-2 * EXTRA : -EXTRA, :] = high
+        piece[-EXTRA:, :] = low
+
+
+def merge_first_body(ffn_own, ffn_a, ffn_b, ffn_c, attn_own, attn_in, own, *pieces):
+    ffn_size, attn_size = (ffn_own.shape[0] - EXTRA) // 4, (attn_own.shape[0] - 2 * EXTRA) // 4
+    for part in range(4):
+        rows = slice(part * ffn_size, (part + 1) * ffn_size)
+        ffn = ffn_own[rows, :] + wide_of(ffn_a, rows) + wide_of(ffn_b, rows) + wide_of(ffn_c, rows)
+        rows = slice(part * attn_size, (part + 1) * attn_size)
+        attn = wide_of(attn_own, rows) + wide_of(attn_in, rows)
+        out = own if part == 0 else pieces[part - 1]
+        out[:ffn_size, :] = ffn.astype(out.dtype)
+        out[ffn_size : ffn_size + attn_size, :] = attn.astype(out.dtype)
+    known = paired([ffn_own[-EXTRA:, :]] + [whole_extra(r) for r in (ffn_a, ffn_b, ffn_c)])
+    fresh = whole_extra(attn_own) + whole_extra(attn_in)
+    put_extra(jnp.concatenate([fresh[:4], known[:8], fresh[12:]], axis=0), own, pieces)
+
+
+def merge_first_call(ffn_own, ffn_in, attn_own, attn_in):
+    width = ffn_own.shape[1]
+    size = (ffn_own.shape[0] - EXTRA) // 4 + (attn_own.shape[0] - 2 * EXTRA) // 4
+    out = kernel_call(
+        merge_first_body,
+        [VM] * 6,
+        (S((size + EXTRA, width), f32),) + (S((size + 2 * EXTRA, width), bf16),) * 3,
+        micros=3,
+        name="merge_first",
+    )(ffn_own, *ffn_in, attn_own, attn_in)
+    return out[0], out[1:]
+
+
+def merge_second_body(skip, own, in_a, in_b, in_c, out, *pieces):
+    received = (in_a, in_b, in_c)
+    size = out.shape[0] - EXTRA
+    for part in range(4):
+        rows = slice(skip + part * size, skip + (part + 1) * size)
+        total = own[rows, :] + wide_of(in_a, rows) + wide_of(in_b, rows) + wide_of(in_c, rows)
+        to = out if part == 0 else pieces[part - 1]
+        to[:size, :] = total.astype(to.dtype)
+    put_extra(paired([own[-EXTRA:, :]] + [whole_extra(r) for r in received]), out, pieces)
+
+
+def merge_second_call(skip, own, received):
+    width = own.shape[1]
+    size = (own.shape[0] - EXTRA - skip) // 4
+    out = kernel_call(
+        functools.partial(merge_second_body, skip),
+        [VM] * 4,
+        (S((size + EXTRA, width), f32),) + (S((size + 2 * EXTRA, width), bf16),) * 3,
+        micros=2,
+        name="merge_second",
+    )(own, *received)
+    return out[0], out[1:]
+
+
 def adamw_with(weight, grad, first, second, average, one, two, rate, decay):
     first_new = BETA_ONE * first + (1.0 - BETA_ONE) * grad
     second_new = BETA_TWO * second + (1.0 - BETA_TWO) * grad * grad
@@ -734,32 +896,64 @@
     return (weight_new, first_new, second_new, average_new)
 
 
-def finish_body(powers, own, in_a, in_b, in_c, known, *refs):
+def update(powers, states, grad, rate, decay, grad_out, outs, at=slice(None)):
+    held = [ref[at] for ref in states]
+    grad_out[at] = grad
+    for ref, value in zip(outs, adamw_with(held[0], grad, *held[1:], powers[0], powers[1], rate, decay)):
+        ref[at] = value
+
+
+def finish_ffn_body(me, powers, own, in_a, in_b, in_c, *refs):
     states, outs = refs[:8], refs[8:]
-    size = states[0].shape[0]
+    _, piece, width = states[0].shape
     received = (in_a, in_b, in_c)
-    grad = own[:size, :]
-    for other in received:
-        grad = grad + other[:size, :].astype(f32)
-    sums = [own[size:, :]]
-    sums += [r[size : size + EXTRA, :].astype(f32) + r[size + EXTRA :, :].astype(f32) for r in received]
-    sums = (sums[0] + sums[1]) + (sums[2] + sums[3])
-    vec_grad = jnp.concatenate([sums[:4], known[:4, :]], axis=0)
-    news = adamw_with(states[0][...], grad, *(r[...] for r in states[1:4]), powers[0], powers[1], MATRIX_RATE, WEIGHT_DECAY)
-    vec_news = adamw_with(states[4][...], vec_grad, *(r[...] for r in states[5:8]), powers[0], powers[1], VECTOR_RATE, 0.0)
-    for ref, value in zip(outs, (grad, *news, vec_grad, *vec_news)):
-        ref[...] = value
-
-
-def finish_call(powers, own, received, known, states):
-    main, vec = S(states[0].shape, f32), S(states[4].shape, f32)
-    return kernel_call(
-        finish_body,
-        [SM] + [VM] * 13,
-        (main,) * 5 + (vec,) * 5,
+    for k in range(2):
+        rows = slice(k * piece, (k + 1) * piece)
+        grad = own[rows, :] + wide_of(in_a, rows) + wide_of(in_b, rows) + wide_of(in_c, rows)
+        update(powers, states[:4], grad, MATRIX_RATE, WEIGHT_DECAY, outs[0], outs[2:6], k)
+    sums = paired([own[-EXTRA:, :]] + [whole_extra(r) for r in received])
+    across = width // piece
+    row = lax.broadcasted_iota(jnp.int32, (EXTRA, width), 0)
+    line = jnp.sum(jnp.where(row == 8 + me[0] // across, sums, 0.0), axis=0, keepdims=True)
+    line = jnp.broadcast_to(line, (8, width))
+    shift = (me[0] % across) * piece
+    line = jnp.where(shift == 0, line, pltpu.roll(line, width - shift, 1))
+    update(powers, states[4:], line[:1, :piece], VECTOR_RATE, 0.0, outs[1], outs[6:])
+
+
+def finish_ffn_call(me, powers, own, received, states):
+    kinds = [S(states[k].shape, f32) for k in (0, 4)]
+    out = kernel_call(
+        finish_ffn_body,
+        [SM, SM] + [VM] * 12,
+        tuple(kinds) + tuple(kind for kind in kinds for _ in range(4)),
         micros=2,
-        name="finish",
-    )(powers, own, *received, known, *states)
+        name="finish_ffn",
+    )(me, powers, own, *received, *states)
+    return out[0], out[1], out[2:6], out[6:]
+
+
+def finish_attn_body(powers, own, in_a, in_b, in_c, *refs):
+    states, outs = refs[:8], refs[8:]
+    piece = states[0].shape[0]
+    rows = slice(0, piece)
+    grad = own[rows, :] + wide_of(in_a, rows) + wide_of(in_b, rows) + wide_of(in_c, rows)
+    update(powers, states[:4], grad, MATRIX_RATE, WEIGHT_DECAY, outs[0], outs[2:6])
+    sums = paired([own[-EXTRA:, :]] + [whole_extra(r) for r in (in_a, in_b, in_c)])
+    vec = jnp.concatenate([sums[:4], own[-EXTRA + 4 : -EXTRA + 8, :]], axis=0)
+    update(powers, states[4:], vec, VECTOR_RATE, 0.0, outs[1], outs[6:])
+
+
+def finish_attn_call(powers, own, received, states):
+    kinds = [S(states[k].shape, f32) for k in (0, 4)]
+    out = kernel_call(
+        finish_attn_body,
+        [SM] + [VM] * 12,
+        tuple(kinds) + tuple(kind for kind in kinds for _ in range(4)),
+        micros=2,
+        name="finish_attn",
+    )(powers, own, *received, *states)
+    return out[0], out[1], out[2:6], out[6:]
 
 
 def body(
@@ -811,12 +1005,11 @@
         attn_mine, attn_other = to_halves(attn_all.reshape(CHUNKS, size, width))
         ffn_mine, ffn_other = to_halves(ffn_all)
         normed, normed_t, seg_cols = norm_call(placed, seg_rows, vectors)
-    qkv_bias = jnp.concatenate([vectors[2], jnp.zeros_like(vectors[2]), vectors[3]])[None, :]
     where = (segment_ids, pack_offsets, kept_counts)
     blocks = rows // BLK
     late = blocks // 4
     qkv, key_t, value_t, w_t, mixed_a, stats_a = attend_first_call(
-        blocks - late, own, *where, normed, attn_mine, attn_other, qkv_bias, seg_rows, seg_cols
+        blocks - late, own, *where, normed, attn_mine, attn_other, vectors, seg_rows, seg_cols
     )
     if tree:
         qkv, mixed_a, *ffn_lines = tie(qkv, mixed_a, *ffn_lines)
@@ -828,7 +1021,6 @@
     layer_out, middle_grad, mixed_grad, ffn_keep, ffn_send = feed_call(
         own, placed, mixed_a, mixed_b, cotangent, vectors, w_t, ffn_mine, ffn_other
     )
-    stats = jnp.concatenate([stats_a, stats_b], axis=0)
     if tree:
         ffn_in = over_core(ffn_send)
     out_grad = side_call(mixed_a, mixed_b, middle_grad)
@@ -836,55 +1028,55 @@
         out_grad, ffn_in = tie(out_grad, ffn_in)
         ffn_own, *ffn_out = combine_call(ffn_keep, [ffn_in], 4, EXTRA)
         out_grad, ffn_own, *ffn_out = tie(out_grad, ffn_own, *ffn_out)
-        ffn_in = [over_plane(p, k + 1) for k, p in enumerate(ffn_out)]
+        ffn_in = [over_line(p, k + 1) for k, p in enumerate(ffn_out)]
     input_grad, attn_keep, attn_send = back_call(
-        own, *where, qkv, key_t, mixed_grad, stats, seg_rows, seg_cols,
+        own, *where, qkv, key_t, mixed_grad, stats_a, stats_b, seg_rows, seg_cols,
         w_t, placed, normed_t, middle_grad, out_grad, vectors,
     )
-    attn_states = (attn_weight, attn_first, attn_second, attn_average)
-    vec_states = (vectors, vec_first, vec_second, vec_average)
-    early = images.shape[0] * 2 // 5
+    index = lax.axis_index("dp") * lax.axis_size("mp") + lax.axis_index("mp")
     if tree:
         input_grad, attn_send, *ffn_in = tie(input_grad, attn_send, *ffn_in)
         attn_in = over_core(attn_send)
-        ffn_own, *ffn_out = combine_call(ffn_own, ffn_in, 4, EXTRA)
-        ffn_own, attn_in, *ffn_out = tie(ffn_own, attn_in, *ffn_out)
-        attn_own, *attn_out = combine_call(attn_keep, [attn_in], 4, EXTRA)
-        attn_in = [over_plane(p, k + 1) for k, p in enumerate(attn_out)]
-        ffn_in = [over_line(p, k + 1) for k, p in enumerate(ffn_out)]
-        image_grads = unpack_call(0, early, pack_offsets, keep_mask, input_grad)
-        image_grads, *attn_in = tie(image_grads, *attn_in)
-        attn_own, *attn_out = combine_call(attn_own, attn_in, 4, EXTRA)
-        attn_in = [over_line(p, k + 1) for k, p in enumerate(attn_out)]
-        image_grads = unpack_call(early, images.shape[0] - early, pack_offsets, keep_mask, input_grad, image_grads)
-        ffn_t = combine_call(ffn_own, ffn_in, 1, EXTRA)[0]
-        image_grads, *attn_in = tie(image_grads, *attn_in)
-        ffn_grad = jnp.swapaxes(ffn_t[: 2 * piece].reshape(2, piece, width), 1, 2)
-        known = ffn_t[2 * piece :]
-        finished = finish_call(powers, attn_own, attn_in, known, [v.T for v in attn_states] + list(vec_states))
-        attn_grad, *attn_up = [v.T for v in finished[:5]]
-        vec_grad, *vec_up = finished[5:]
-        bias_sums = known[4:8]
+        states = [v.T for v in (attn_weight, attn_first, attn_second, attn_average)]
+        states += [vectors, vec_first, vec_second, vec_average]
+        ffn_states = [jnp.swapaxes(v, 1, 2) for v in (ffn_weight, ffn_first, ffn_second, ffn_average)]
+        ffn_states += [v[None, :] for v in (up_bias, bias_first, bias_second, bias_average)]
+        cut = images.shape[0] * 3 // 5
+        unpack = functools.partial(unpack_call, pack_offsets, keep_mask)
+        merged, pieces = merge_first_call(ffn_own, ffn_in, attn_keep, attn_in)
+        input_grad, *pieces = tie(input_grad, *pieces)
+        received = [over_plane(p, k + 1) for k, p in enumerate(pieces)]
+        image_grads = unpack(input_grad, 0, cut)
+        image_grads, *received = tie(image_grads, *received)
+        attn_own, pieces = merge_second_call(2 * piece, merged, received)
+        image_grads, merged, *pieces = tie(image_grads, merged, *pieces)
+        last = [over_line(p, k + 1) for k, p in enumerate(pieces)]
+        image_grads = unpack(input_grad, cut, images.shape[0], image_grads)
+        ffn_grad, bias_grad, ffn_up, bias_up = finish_ffn_call(own, powers, merged, received, ffn_states)
+        image_grads, ffn_grad, *last = tie(image_grads, ffn_grad, *last)
+        attn_grad, vec_grad, attn_up, vec_up = finish_attn_call(powers, attn_own, last, states)
+        attn_grad, ffn_grad, bias_grad = attn_grad.T, jnp.swapaxes(ffn_grad, 1, 2), bias_grad[0]
+        attn_up, ffn_up = [v.T for v in attn_up], [jnp.swapaxes(v, 1, 2) for v in ffn_up]
+        bias_up = [v[0] for v in bias_up]
     else:
-        image_grads = unpack_call(0, images.shape[0], pack_offsets, keep_mask, input_grad)
+        image_grads = unpack_call(pack_offsets, keep_mask, input_grad, 0, images.shape[0])
         base = ffn_keep.shape[0] - 2 * EXTRA
-        ffn_t = from_halves(ffn_keep[:base], ffn_send[:base], 2, width)
+        ffn_t = from_halves(ffn_keep[:base], ffn_send[:base], 2, width, True)
         ffn_t = jnp.swapaxes(ffn_t, 0, 1).reshape(2, 4 * width, width)
         ffn_t = lax.psum_scatter(ffn_t.astype(f32), both, scatter_dimension=1, tiled=True)
         ffn_grad = jnp.swapaxes(ffn_t, 1, 2)
         known = ffn_keep[base : base + EXTRA].astype(f32) + ffn_keep[base + EXTRA :].astype(f32)
         base = attn_keep.shape[0] - 2 * EXTRA
-        attn_t = from_halves(attn_keep[:base], attn_send[:base], 1, width).reshape(4 * width, width)
+        attn_t = from_halves(attn_keep[:base], attn_send[:base], 1, width, False).reshape(4 * width, width)
         attn_grad = lax.psum_scatter(attn_t.astype(f32), both, scatter_dimension=0, tiled=True).T
         sums = attn_keep[base : base + EXTRA].astype(f32) + attn_keep[base + EXTRA :].astype(f32)
         sums = lax.psum(jnp.concatenate([sums[:4], known[:8]], axis=0), both)
         vec_grad, bias_sums = sums[:8], sums[8:]
-        attn_up = adamw(attn_weight, attn_grad, *attn_states[1:], count, MATRIX_RATE, WEIGHT_DECAY)
-        vec_up = adamw(vectors, vec_grad, *vec_states[1:], count, VECTOR_RATE, 0.0)
-    index = lax.axis_index("dp") * lax.axis_size("mp") + lax.axis_index("mp")
-    bias_grad = lax.dynamic_slice_in_dim(bias_sums.reshape(4 * width), index * piece, piece, 0)
-    ffn_up = adamw(ffn_weight, ffn_grad, ffn_first, ffn_second, ffn_average, count, MATRIX_RATE, WEIGHT_DECAY)
-    bias_up = adamw(up_bias, bias_grad, bias_first, bias_second, bias_average, count, VECTOR_RATE, 0.0)
+        bias_grad = lax.dynamic_slice_in_dim(bias_sums.reshape(4 * width), index * piece, piece, 0)
+        attn_up = adamw(attn_weight, attn_grad, attn_first, attn_second, attn_average, count, MATRIX_RATE, WEIGHT_DECAY)
+        vec_up = adamw(vectors, vec_grad, vec_first, vec_second, vec_average, count, VECTOR_RATE, 0.0)
+        ffn_up = adamw(ffn_weight, ffn_grad, ffn_first, ffn_second, ffn_average, count, MATRIX_RATE, WEIGHT_DECAY)
+        bias_up = adamw(up_bias, bias_grad, bias_first, bias_second, bias_average, count, VECTOR_RATE, 0.0)
     news = [part[k] for k in range(4) for part in (attn_up, ffn_up, bias_up, vec_up)]
     return (layer_out, image_grads, attn_grad, ffn_grad, bias_grad, vec_grad, *news)
 

time: 188 us -> 174 us (0.926)
  Pallas kernels: 136 us -> 128 us
  waiting for transfers between devices: 4.6 us -> 9.61 us
  local copies, waits for them, and re-layouts: 9.65 us -> 4.74 us
  starting transfers between devices: 29 us -> 26.2 us
  other arithmetic: 5.3 us -> 3.14 us
    pallas_call x5 -> x1, Pallas kernels: 11.1 us -> 2.9 us  [combine_call(): kernel_call(functools.partial(combine_body, parts, size, extra, len(recei...]
    slice x4 -> x0, local copies, waits for them, and re-layouts: 3.82 us -> none  [the longest x1 1.34 us: body(): known = ffn_t[2 * piece:]]
    ppermute x12 -> x9, starting transfers between devices: 14.1 us -> 10.5 us  [over_plane(): lax.ppermute(values, ('dp', 'mp'), [(i, i ^ 2 * apart) for i in range(dev...]
    pallas_call x1, Pallas kernels: 19.9 us -> 16.9 us  [attend_first_call(): kernel_call(attend_first_body, [SM, SM, SM, SM, VM, VM, VM, VM, VM, VM],...]
    pallas_call x2 -> x5, Pallas kernels: 36 us -> 38.9 us  [the longest x1 29.5 us: back_call(): kernel_call(back_body, [SM] * 4 + [HB] * 3 + [VM] * 4 + [HB] * 4 + [VM] *...]
    ppermute x12 -> x9, waiting for transfers between devices: 1.78 us -> 4.52 us  [over_plane(): lax.ppermute(values, ('dp', 'mp'), [(i, i ^ 2 * apart) for i in range(dev...]
    ppermute x4, waiting for transfers between devices: 1.99 us -> 4.23 us  [over_core(): lax.ppermute(values, 'mp', [(i, i ^ 1) for i in range(lax.axis_size('mp'))])]
    unnamed x63 -> x35, local copies, waits for them, and re-layouts: 5.04 us -> 4.55 us
  transfers between devices with their start and end apart: 25 -> 22, of which waited for: 3 -> 4; matrix products, arithmetic and copies ran while one was open for 4% -> 0% of each run, Pallas kernels for 52% -> 50%
where the time goes in v1:
time: 174 us; the launch traced here: 173 us
  Pallas kernels  128 us (74%)
  starting transfers between devices  26.2 us (15%)
  waiting for transfers between devices  9.61 us (6%)
  local copies, waits for them, and re-layouts  4.74 us (3%)
  other arithmetic  3.14 us (2%)
  between operations  1.96 us (1%)
    pallas_call x1, Pallas kernels, feed_call(): kernel_call(functools.partial(feed_body, size), [SM, row_block, pl.BlockS...  31.3 us
    pallas_call x1, Pallas kernels, back_call(): kernel_call(back_body, [SM] * 4 + [HB] * 3 + [VM] * 4 + [HB] * 4 + [VM] *...  29.5 us
    pallas_call x1, Pallas kernels, attend_first_call(): kernel_call(attend_first_body, [SM, SM, SM, SM, VM, VM, VM, VM, VM, VM],...  16.9 us
    ppermute x9, starting transfers between devices, over_line(): lax.ppermute(values, 'dp', [(i, i ^ 2 * apart) for i in range(lax.axis_si...  15.4 us
    pallas_call x2, Pallas kernels, unpack_call(): pl.pallas_call(functools.partial(unpack_body, win, first, count), grid=(c...  10.7 us
    ppermute x9, starting transfers between devices, over_plane(): lax.ppermute(values, ('dp', 'mp'), [(i, i ^ 2 * apart) for i in range(dev...  10.5 us
    pallas_call x1, Pallas kernels, place_call(): kernel_call(functools.partial(place_body, win), [SM, VM, VM], (S((rows, w...  8.88 us
    pallas_call x1, Pallas kernels, norm_call(): kernel_call(norm_body, [VM, VM, VM], (S((rows, width), bf16), S((width, r...  7.42 us
  transfers between devices with their start and end apart: 22, of which 4 were waited for; matrix products, arithmetic and copies ran while one was open for 0% of the time, Pallas kernels for 50%

profile of v1, /device:TPU:0, one launch (start us, length us, event | category | flops | bytes accessed | tf_op | source)
XLA Modules:
  0.0 173.2 jit_solution(5841705512810168598)
XLA Ops:
  3.2 3.1 %collective-permute-start = (bf16[160,384]{1,0:T(8,128)(2,1)S(1)}, bf16[160,384]{1,0:T(8,128)(2,1)S(1)}, u32[]{:S(2)}, u32[]{:S(2)}) collective-permute-start(bf16[160,384]{1,0:T(8,128)(2,1)S(1)} %fusion.1), channel_id=1, source_target_pairs={{0,8},{4,12},{8,0},{12,4},{16,24},{20,28},{24,16},{28,20},{1,9},{5... | collective-permute-start | bytes 368648 | tf_op jit(solution)/shard_map/ppermute | solution.py:177
  6.3 2.6 %collective-permute-start.1 = (bf16[160,384]{1,0:T(8,128)(2,1)S(1)}, bf16[160,384]{1,0:T(8,128)(2,1)S(1)}, u32[]{:S(2)}, u32[]{:S(2)}) collective-permute-start(bf16[160,384]{1,0:T(8,128)(2,1)S(1)} %fusion.1), channel_id=1, source_target_pairs={{0,16},{4,20},{8,24},{12,28},{16,0},{20,4},{24,8},{28,12},{1,17},{... | collective-permute-start | bytes 368648 | tf_op jit(solution)/shard_map/ppermute | solution.py:177
  8.9 8.9 %place.1.packed.packed_in = bf16[2048,384]{1,0:T(8,128)(2,1)} custom-call(s32[25]{0:T(128)} %offs.11, bf16[25,198,384]{2,1,0:T(8,128)(2,1)} %images.1, s32[25,198]{1,0:T(8,128)} %keep.5), custom_call_target="tpu_custom_call" | custom-call | flops 790732800 | bytes 31500000 | tf_op jit(solution)/shard_map/place/pallas_call | solution.py:216
  18.7 1.6 collective-permute-start.3
  22.3 7.4 %norm.1 = (bf16[2048,384]{1,0:T(8,128)(2,1)}, bf16[384,2048]{1,0:T(8,128)(2,1)}, s32[2048,128]{1,0:T(8,128)}) custom-call(bf16[2048,384]{1,0:T(8,128)(2,1)} %place.1.packed.packed_in, s32[16,128]{1,0:T(8,128)} %bitcast.49, f32[8,384]{1,0:T(8,128)} %refs_4_.1), custom_call_target="tpu_custom_call" | custom-call | flops 9437184 | bytes 21000000 | tf_op jit(solution)/shard_map/norm/pallas_call | solution.py:250
  30.0 2.0 %collective-permute-done.6.other = bf16[768,384]{1,0:T(8,128)(2,1)S(1)} collective-permute-done((bf16[768,384]{1,0:T(8,128)(2,1)S(1)}, bf16[768,384]{1,0:T(8,128)(2,1)S(1)}, u32[]{:S(2)}, u32[]{:S(2)}) %collective-permute-start.6) | collective-permute-done | bytes 589856 | tf_op jit(solution)/shard_map/ppermute | solution.py:168
  32.0 1.5 collective-permute-start.7
  35.5 16.9 %attend_first.1 = (bf16[2048,1152]{1,0:T(8,128)(2,1)}, bf16[384,2048]{1,0:T(8,128)(2,1)}, bf16[384,2048]{1,0:T(8,128)(2,1)}, bf16[32,48,384]{2,1,0:T(8,128)(2,1)...) custom-call(s32[1]{0:T(128)} %bitcast.own.me, s32[2048]{0:T(1024)} %seg.5, s32[25]{0:T(128)} %offs.11, s32[25]{0:T(128)} %counts.5, ...), custom_call_target="tpu_custom_call" | custom-call | flops 1811939328 | bytes 70000000 | tf_op jit(solution)/shard_map/attend_first/pallas_call | solution.py:374
  52.7 6.4 %attend_last.1 = (bf16[384,512]{1,0:T(8,128)(2,1)}, f32[4,768]{1,0:T(4,128)}) custom-call(s32[2048]{0:T(1024)} %seg.5, s32[25]{0:T(128)} %offs.11, s32[25]{0:T(128)} %counts.5, bf16[2048,1152]{1,0:T(8,128)(2,1)} %get-tuple-element.137.qkv.qkv_in, bf16[384,2048]{1,0:T(8,128)(2,1)} %get-tuple-element.138.value_t, s32[16,128]{1,0:T(8,128)} %bitcast.51, ...), custom_call_target="tpu_custom_call" | custom-call | flops 402653184 | bytes 17500000 | tf_op jit(solution)/shard_map/attend_last/pallas_call | solution.py:394
  60.2 31.3 %feed.1 = (bf16[2048,384]{1,0:T(8,128)(2,1)}, f32[2048,384]{1,0:T(8,128)}, bf16[2048,384]{1,0:T(8,128)(2,1)}, bf16[1568,384]{1,0:T(8,128)(2,1)}, bf16[1568,384]{1,0:T(8,128)(2,1)}) custom-call(s32[1]{0:T(128)} %bitcast.own.me, bf16[2048,384]{1,0:T(8,128)(2,1)} %place.1.packed.packed_in, bf16[384,1536]{1,0:T(8,128)(2,1)} %get-tuple-element.136.mixed_a, ...), custom_call_target="tpu_custom_call" | custom-call | flops 16307453952 | bytes 105000000 | tf_op jit(solution)/shard_map/feed/pallas_call | solution.py:569
  91.6 4.2 %side.1.out_grad = bf16[384,384]{1,0:T(8,128)(2,1)} custom-call(bf16[384,1536]{1,0:T(8,128)(2,1)} %get-tuple-element.136.mixed_a, bf16[384,512]{1,0:T(8,128)(2,1)} %get-tuple-element.144.mixed_b, f32[2048,384]{1,0:T(8,128)} %get-tuple-element.154.middle_grad.middle_in), custom_call_target="tpu_custom_call" | custom-call | flops 603979776 | bytes 14000000 | tf_op jit(solution)/shard_map/side/pallas_call | solution.py:613
  96.9 2.9 %combine.1 = (f32[400,384]{1,0:T(8,128)}, bf16[416,384]{1,0:T(8,128)(2,1)}, bf16[416,384]{1,0:T(8,128)(2,1)}, bf16[416,384]{1,0:T(8,128)(2,1)}) custom-call(bf16[1568,384]{1,0:T(8,128)(2,1)} %get-tuple-element.157.refs_0_, bf16[1568,384]{1,0:T(8,128)(2,1)} %copy-done), custom_call_target="tpu_custom_call" | custom-call | flops 602112 | bytes 7000000 | tf_op jit(solution)/shard_map/combine/pallas_call | solution.py:157
  99.8 2.7 %collective-permute-start.12 = (bf16[416,384]{1,0:T(8,128)(2,1)}, bf16[416,384]{1,0:T(8,128)(2,1)S(1)}, u32[]{:S(2)}, u32[]{:S(2)}) collective-permute-start(bf16[416,384]{1,0:T(8,128)(2,1)} %get-tuple-element.166), channel_id=1, source_target_pairs={{0,8},{4,12},{8,0},{12,4},{16,24},{20,28},{24,16},{28,20},{1,9},{5... | collective-permute-start | bytes 958472 | tf_op jit(solution)/shard_map/ppermute | solution.py:177
  104.9 29.5 %back.1 = (f32[2048,384]{1,0:T(8,128)}, bf16[800,384]{1,0:T(8,128)(2,1)}, bf16[800,384]{1,0:T(8,128)(2,1)}) custom-call(s32[1]{0:T(128)} %bitcast.own.me, s32[2048]{0:T(1024)} %seg.5, s32[25]{0:T(128)} %offs.11, s32[25]{0:T(128)} %counts.5, bf16[2048,1152]{1,0:T(8,128)(2,1)} %get-tuple-element.137.qkv.qkv_in, bf16[384,2048]{1,0:T(8,128)(2,1)} %get-tuple-element.149.key_in, ...), custom_call_target="tpu_custom_call" | custom-call | flops 6643777536 | bytes 105000000 | tf_op jit(solution)/shard_map/back/pallas_call | solution.py:717
  134.5 2.2 %collective-permute-done.15.attn_in = bf16[800,384]{1,0:T(8,128)(2,1)S(1)} collective-permute-done((bf16[800,384]{1,0:T(8,128)(2,1)}, bf16[800,384]{1,0:T(8,128)(2,1)S(1)}, u32[]{:S(2)}, u32[]{:S(2)}) %collective-permute-start.15) | collective-permute-done | bytes 614432 | tf_op jit(solution)/shard_map/ppermute | solution.py:168
  137.6 2.9 %merge_first.1 = (f32[304,384]{1,0:T(8,128)}, bf16[320,384]{1,0:T(8,128)(2,1)}, bf16[320,384]{1,0:T(8,128)(2,1)}, bf16[320,384]{1,0:T(8,128)(2,1)}) custom-call(f32[400,384]{1,0:T(8,128)} %get-tuple-element.170.ffn_own, bf16[416,384]{1,0:T(8,128)(2,1)} %copy-done.5, bf16[416,384]{1,0:T(8,128)(2,1)} %copy-done.6, bf16[416,384]{1,0:T(8,128)(2,1)} %copy-done.7, ...), custom_call_target="tpu_custom_call" | custom-call | bytes 10500000 | tf_op jit(solution)/shard_map/merge_first/pallas_call | solution.py:857
  141.2 2.3 %collective-permute-start.17 = (bf16[320,384]{1,0:T(8,128)(2,1)}, bf16[320,384]{1,0:T(8,128)(2,1)S(1)}, u32[]{:S(2)}, u32[]{:S(2)}) collective-permute-start(bf16[320,384]{1,0:T(8,128)(2,1)} %get-tuple-element.181), channel_id=1, source_target_pairs={{0,4},{1,5},{2,6},{3,7},{4,0},{5,1},{6,2},{7,3},{8,12},{9,13},{10,... | collective-permute-start | bytes 737288 | tf_op jit(solution)/shard_map/ppermute | solution.py:173
  144.7 5.9 %unpack.2.refs_0_ = f32[25,198,384]{2,1,0:T(8,128)} custom-call(s32[25]{0:T(128)} %offs.11, s32[25,198]{1,0:T(8,128)} %keep.5, f32[2048,384]{1,0:T(8,128)} %get-tuple-element.179.input_grad), custom_call_target="tpu_custom_call" | custom-call | bytes 24500000 | tf_op jit(solution)/shard_map/unpack/pallas_call | solution.py:780
  150.7 4.5 %collective-permute-done.18.in_c = bf16[320,384]{1,0:T(8,128)(2,1)S(1)} collective-permute-done((bf16[320,384]{1,0:T(8,128)(2,1)}, bf16[320,384]{1,0:T(8,128)(2,1)S(1)}, u32[]{:S(2)}, u32[]{:S(2)}) %collective-permute-start.18) | collective-permute-done | bytes 245792 | tf_op jit(solution)/shard_map/ppermute | solution.py:173
  155.8 2.0 %merge_second.1 = (f32[64,384]{1,0:T(8,128)}, bf16[80,384]{1,0:T(8,128)(2,1)}, bf16[80,384]{1,0:T(8,128)(2,1)}, bf16[80,384]{1,0:T(8,128)(2,1)}) custom-call(f32[304,384]{1,0:T(8,128)} %get-tuple-element.192.own, bf16[320,384]{1,0:T(8,128)(2,1)} %copy-done.1, bf16[320,384]{1,0:T(8,128)(2,1)} %copy-done.2, bf16[320,384]{1,0:T(8,128)(2,1)} %copy-done.3), custom_call_target="tpu_custom_call" | custom-call | bytes 7000000 | tf_op jit(solution)/shard_map/merge_second/pallas_call | solution.py:881
  157.9 2.3 %collective-permute-start.19 = (bf16[80,384]{1,0:T(8,128)(2,1)}, bf16[80,384]{1,0:T(8,128)(2,1)S(1)}, u32[]{:S(2)}, u32[]{:S(2)}) collective-permute-start(bf16[80,384]{1,0:T(8,128)(2,1)} %get-tuple-element.194), channel_id=1, source_target_pairs={{0,8},{4,12},{8,0},{12,4},{16,24},{20,28},{24,16},{28,20},{1,9},{5... | collective-permute-start | bytes 184328 | tf_op jit(solution)/shard_map/ppermute | solution.py:177
  163.1 4.8 %unpack.3 = f32[25,198,384]{2,1,0:T(8,128)} custom-call(s32[25]{0:T(128)} %offs.11, s32[25,198]{1,0:T(8,128)} %keep.5, f32[2048,384]{1,0:T(8,128)} %get-tuple-element.179.input_grad, f32[25,198,384]{2,1,0:T(8,128)} %unpack.2.refs_0_), custom_call_target="tpu_custom_call", output_to_operand_aliasing={{}: (3, {})} | custom-call | bytes 24500000 | tf_op jit(solution)/shard_map/unpack/pallas_call | solution.py:780
  167.9 2.5 %finish_ffn.1 = (f32[2,48,384]{2,1,0:T(8,128)}, f32[1,48]{1,0:T(1,128)}, f32[2,48,384]{2,1,0:T(8,128)}, f32[2,48,384]{2,1,0:T(8,128)}, f32[2,48,384]{2,1,0:T(8,1...) custom-call(s32[1]{0:T(128)} %bitcast.own.me, ...), custom_call_target="tpu_custom_call" | custom-call | bytes 7000000 | tf_op jit(solution)/shard_map/finish_ffn/pallas_call | solution.py:926
  171.1 2.0 %finish_attn.1 = (f32[48,384]{1,0:T(8,128)}, f32[8,384]{1,0:T(8,128)}, f32[48,384]{1,0:T(8,128)}, f32[48,384]{1,0:T(8,128)}, f32[48,384]{1,0:T(8,128)}, /*index=...) custom-call(f32[2]{0:T(128)} %pad_maximum_fusion.2.powers, ...), custom_call_target="tpu_custom_call" | custom-call | bytes 7000000 | tf_op jit(solution)/shard_map/finish_attn/pallas_call | solution.py:949
  (87 shorter events, 19.0 us)
Async XLA Ops:
  3.2 14.6 %collective-permute-start = (bf16[160,384]{1,0:T(8,128)(2,1)S(1)}, bf16[160,384]{1,0:T(8,128)(2,1)S(1)}, u32[]{:S(2)}, u32[]{:S(2)}) collective-permute-start(bf16[160,384]{1,0:T(8,128)(2,1)S(1)} %fusion.1), channel_id=1, source_target_pairs={{0,8},{4,12},{8,0},{12,4},{16,24},{20,28},{24,16},{28,20},{1,9},{5... | collective-permute-start | bytes 368648 | tf_op jit(solution)/shard_map/ppermute | solution.py:177
  6.3 12.3 %collective-permute-start.1 = (bf16[160,384]{1,0:T(8,128)(2,1)S(1)}, bf16[160,384]{1,0:T(8,128)(2,1)S(1)}, u32[]{:S(2)}, u32[]{:S(2)}) collective-permute-start(bf16[160,384]{1,0:T(8,128)(2,1)S(1)} %fusion.1), channel_id=1, source_target_pairs={{0,16},{4,20},{8,24},{12,28},{16,0},{20,4},{24,8},{28,12},{1,17},{... | collective-permute-start | bytes 368648 | tf_op jit(solution)/shard_map/ppermute | solution.py:177
  8.8 9.7 %collective-permute-start.2 = (bf16[160,384]{1,0:T(8,128)(2,1)S(1)}, bf16[160,384]{1,0:T(8,128)(2,1)S(1)}, u32[]{:S(2)}, u32[]{:S(2)}) collective-permute-start(bf16[160,384]{1,0:T(8,128)(2,1)S(1)} %fusion.1), channel_id=1, source_target_pairs={{0,24},{4,28},{8,16},{12,20},{16,8},{20,12},{24,0},{28,4},{1,25},{... | collective-permute-start | bytes 368648 | tf_op jit(solution)/shard_map/ppermute | solution.py:177
  18.7 11.1 %collective-permute-start.3 = (bf16[192,384]{1,0:T(8,128)(2,1)S(1)}, bf16[192,384]{1,0:T(8,128)(2,1)S(1)}, u32[]{:S(2)}, u32[]{:S(2)}) collective-permute-start(bf16[192,384]{1,0:T(8,128)(2,1)S(1)} %pad_maximum_fusion.1), channel_id=1, source_target_pairs={{0,2},{1,3},{2,0},{3,1},{4,6},{5,7},{6,4},{7,5},{8,10},{9,11},{10,... | collective-permute-start | bytes 442376 | tf_op jit(solution)/shard_map/ppermute | solution.py:173
  20.3 9.5 %collective-permute-start.4 = (bf16[192,384]{1,0:T(8,128)(2,1)S(1)}, bf16[192,384]{1,0:T(8,128)(2,1)S(1)}, u32[]{:S(2)}, u32[]{:S(2)}) collective-permute-start(bf16[192,384]{1,0:T(8,128)(2,1)S(1)} %pad_maximum_fusion.1), channel_id=1, source_target_pairs={{0,4},{1,5},{2,6},{3,7},{4,0},{5,1},{6,2},{7,3},{8,12},{9,13},{10,... | collective-permute-start | bytes 442376 | tf_op jit(solution)/shard_map/ppermute | solution.py:173
  21.7 8.1 %collective-permute-start.5 = (bf16[192,384]{1,0:T(8,128)(2,1)S(1)}, bf16[192,384]{1,0:T(8,128)(2,1)S(1)}, u32[]{:S(2)}, u32[]{:S(2)}) collective-permute-start(bf16[192,384]{1,0:T(8,128)(2,1)S(1)} %pad_maximum_fusion.1), channel_id=1, source_target_pairs={{0,6},{1,7},{2,4},{3,5},{4,2},{5,3},{6,0},{7,1},{8,14},{9,15},{10,... | collective-permute-start | bytes 442376 | tf_op jit(solution)/shard_map/ppermute | solution.py:173
  29.9 5.6 %copy-start.12 = (bf16[768,384]{1,0:T(8,128)(2,1)}, bf16[768,384]{1,0:T(8,128)(2,1)S(1)}, u32[]{:S(2)}) copy-start(bf16[768,384]{1,0:T(8,128)(2,1)S(1)} %constant_dynamic-update-slice_fusion.mine) | copy-start | bytes 1769476
  29.9 2.1 %collective-permute-start.6 = (bf16[768,384]{1,0:T(8,128)(2,1)S(1)}, bf16[768,384]{1,0:T(8,128)(2,1)S(1)}, u32[]{:S(2)}, u32[]{:S(2)}) collective-permute-start(bf16[768,384]{1,0:T(8,128)(2,1)S(1)} %constant_dynamic-update-slice_fusion.mine), channel_id=1, source_target_pairs={{0,1},{1,0},{2,3},{3,2},{4,5},{5,4},{6,7},{7,6},{8,9},{9,8},{10,11... | collective-permute-start | bytes 1769480 | tf_op jit(solution)/shard_map/ppermute | solution.py:168
  32.0 20.4 %collective-permute-start.7 = (bf16[448,384]{1,0:T(8,128)(2,1)S(1)}, bf16[448,384]{1,0:T(8,128)(2,1)S(1)}, u32[]{:S(2)}, u32[]{:S(2)}) collective-permute-start(bf16[448,384]{1,0:T(8,128)(2,1)S(1)} %pad_maximum_fusion), channel_id=1, source_target_pairs={{0,2},{1,3},{2,0},{3,1},{4,6},{5,7},{6,4},{7,5},{8,10},{9,11},{10,... | collective-permute-start | bytes 1032200 | tf_op jit(solution)/shard_map/ppermute | solution.py:173
  33.5 18.9 %collective-permute-start.8 = (bf16[448,384]{1,0:T(8,128)(2,1)S(1)}, bf16[448,384]{1,0:T(8,128)(2,1)S(1)}, u32[]{:S(2)}, u32[]{:S(2)}) collective-permute-start(bf16[448,384]{1,0:T(8,128)(2,1)S(1)} %pad_maximum_fusion), channel_id=1, source_target_pairs={{0,4},{1,5},{2,6},{3,7},{4,0},{5,1},{6,2},{7,3},{8,12},{9,13},{10,... | collective-permute-start | bytes 1032200 | tf_op jit(solution)/shard_map/ppermute | solution.py:173
  35.0 17.4 %collective-permute-start.9 = (bf16[448,384]{1,0:T(8,128)(2,1)S(1)}, bf16[448,384]{1,0:T(8,128)(2,1)S(1)}, u32[]{:S(2)}, u32[]{:S(2)}) collective-permute-start(bf16[448,384]{1,0:T(8,128)(2,1)S(1)} %pad_maximum_fusion), channel_id=1, source_target_pairs={{0,6},{1,7},{2,4},{3,5},{4,2},{5,3},{6,0},{7,1},{8,14},{9,15},{10,... | collective-permute-start | bytes 1032200 | tf_op jit(solution)/shard_map/ppermute | solution.py:173
  52.6 6.4 %copy-start.8 = (bf16[1792,384]{1,0:T(8,128)(2,1)}, bf16[1792,384]{1,0:T(8,128)(2,1)S(1)}, u32[]{:S(2)}) copy-start(bf16[1792,384]{1,0:T(8,128)(2,1)S(1)} %constant_dynamic-update-slice_fusion.7.mine) | copy-start | bytes 4128772
  52.6 6.4 %collective-permute-start.10 = (bf16[1792,384]{1,0:T(8,128)(2,1)S(1)}, bf16[1792,384]{1,0:T(8,128)(2,1)S(1)}, u32[]{:S(2)}, u32[]{:S(2)}) collective-permute-start(bf16[1792,384]{1,0:T(8,128)(2,1)S(1)} %constant_dynamic-update-slice_fusion.7.mine), channel_id=1, source_target_pairs={{0,1},{1,0},{2,3},{3,2},{4,5},{5,4},{6,7},{7,6},{8,9},{9,8},{10,11... | collective-permute-start | bytes 4128776 | tf_op jit(solution)/shard_map/ppermute | solution.py:168
  91.6 4.2 %collective-permute-start.11 = (bf16[1568,384]{1,0:T(8,128)(2,1)}, bf16[1568,384]{1,0:T(8,128)(2,1)S(1)}, u32[]{:S(2)}, u32[]{:S(2)}) collective-permute-start(bf16[1568,384]{1,0:T(8,128)(2,1)} %get-tuple-element.155), channel_id=1, source_target_pairs={{0,1},{1,0},{2,3},{3,2},{4,5},{5,4},{6,7},{7,6},{8,9},{9,8},{10,11... | collective-permute-start | bytes 3612680 | tf_op jit(solution)/shard_map/ppermute | solution.py:168
  99.8 34.6 %collective-permute-start.12 = (bf16[416,384]{1,0:T(8,128)(2,1)}, bf16[416,384]{1,0:T(8,128)(2,1)S(1)}, u32[]{:S(2)}, u32[]{:S(2)}) collective-permute-start(bf16[416,384]{1,0:T(8,128)(2,1)} %get-tuple-element.166), channel_id=1, source_target_pairs={{0,8},{4,12},{8,0},{12,4},{16,24},{20,28},{24,16},{28,20},{1,9},{5... | collective-permute-start | bytes 958472 | tf_op jit(solution)/shard_map/ppermute | solution.py:177
  102.5 31.9 %collective-permute-start.13 = (bf16[416,384]{1,0:T(8,128)(2,1)}, bf16[416,384]{1,0:T(8,128)(2,1)S(1)}, u32[]{:S(2)}, u32[]{:S(2)}) collective-permute-start(bf16[416,384]{1,0:T(8,128)(2,1)} %get-tuple-element.167), channel_id=1, source_target_pairs={{0,16},{4,20},{8,24},{12,28},{16,0},{20,4},{24,8},{28,12},{1,17},{... | collective-permute-start | bytes 958472 | tf_op jit(solution)/shard_map/ppermute | solution.py:177
  103.7 30.7 %collective-permute-start.14 = (bf16[416,384]{1,0:T(8,128)(2,1)}, bf16[416,384]{1,0:T(8,128)(2,1)S(1)}, u32[]{:S(2)}, u32[]{:S(2)}) collective-permute-start(bf16[416,384]{1,0:T(8,128)(2,1)} %get-tuple-element.168), channel_id=1, source_target_pairs={{0,24},{4,28},{8,16},{12,20},{16,8},{20,12},{24,0},{28,4},{1,25},{... | collective-permute-start | bytes 958472 | tf_op jit(solution)/shard_map/ppermute | solution.py:177
  134.5 2.3 %collective-permute-start.15 = (bf16[800,384]{1,0:T(8,128)(2,1)}, bf16[800,384]{1,0:T(8,128)(2,1)S(1)}, u32[]{:S(2)}, u32[]{:S(2)}) collective-permute-start(bf16[800,384]{1,0:T(8,128)(2,1)} %get-tuple-element.175), channel_id=1, source_target_pairs={{0,1},{1,0},{2,3},{3,2},{4,5},{5,4},{6,7},{7,6},{8,9},{9,8},{10,11... | collective-permute-start | bytes 1843208 | tf_op jit(solution)/shard_map/ppermute | solution.py:168
  140.5 10.1 %collective-permute-start.16 = (bf16[320,384]{1,0:T(8,128)(2,1)}, bf16[320,384]{1,0:T(8,128)(2,1)S(1)}, u32[]{:S(2)}, u32[]{:S(2)}) collective-permute-start(bf16[320,384]{1,0:T(8,128)(2,1)} %get-tuple-element.180), channel_id=1, source_target_pairs={{0,2},{1,3},{2,0},{3,1},{4,6},{5,7},{6,4},{7,5},{8,10},{9,11},{10,... | collective-permute-start | bytes 737288 | tf_op jit(solution)/shard_map/ppermute | solution.py:173
  141.2 9.5 %collective-permute-start.17 = (bf16[320,384]{1,0:T(8,128)(2,1)}, bf16[320,384]{1,0:T(8,128)(2,1)S(1)}, u32[]{:S(2)}, u32[]{:S(2)}) collective-permute-start(bf16[320,384]{1,0:T(8,128)(2,1)} %get-tuple-element.181), channel_id=1, source_target_pairs={{0,4},{1,5},{2,6},{3,7},{4,0},{5,1},{6,2},{7,3},{8,12},{9,13},{10,... | collective-permute-start | bytes 737288 | tf_op jit(solution)/shard_map/ppermute | solution.py:173
  143.4 11.7 %collective-permute-start.18 = (bf16[320,384]{1,0:T(8,128)(2,1)}, bf16[320,384]{1,0:T(8,128)(2,1)S(1)}, u32[]{:S(2)}, u32[]{:S(2)}) collective-permute-start(bf16[320,384]{1,0:T(8,128)(2,1)} %get-tuple-element.182), channel_id=1, source_target_pairs={{0,6},{1,7},{2,4},{3,5},{4,2},{5,3},{6,0},{7,1},{8,14},{9,15},{10,... | collective-permute-start | bytes 737288 | tf_op jit(solution)/shard_map/ppermute | solution.py:173
  157.9 12.5 %collective-permute-start.19 = (bf16[80,384]{1,0:T(8,128)(2,1)}, bf16[80,384]{1,0:T(8,128)(2,1)S(1)}, u32[]{:S(2)}, u32[]{:S(2)}) collective-permute-start(bf16[80,384]{1,0:T(8,128)(2,1)} %get-tuple-element.194), channel_id=1, source_target_pairs={{0,8},{4,12},{8,0},{12,4},{16,24},{20,28},{24,16},{28,20},{1,9},{5... | collective-permute-start | bytes 184328 | tf_op jit(solution)/shard_map/ppermute | solution.py:177
  160.1 10.3 %collective-permute-start.20 = (bf16[80,384]{1,0:T(8,128)(2,1)}, bf16[80,384]{1,0:T(8,128)(2,1)S(1)}, u32[]{:S(2)}, u32[]{:S(2)}) collective-permute-start(bf16[80,384]{1,0:T(8,128)(2,1)} %get-tuple-element.195), channel_id=1, source_target_pairs={{0,16},{4,20},{8,24},{12,28},{16,0},{20,4},{24,8},{28,12},{1,17},{... | collective-permute-start | bytes 184328 | tf_op jit(solution)/shard_map/ppermute | solution.py:177
  161.6 8.8 %collective-permute-start.21 = (bf16[80,384]{1,0:T(8,128)(2,1)}, bf16[80,384]{1,0:T(8,128)(2,1)S(1)}, u32[]{:S(2)}, u32[]{:S(2)}) collective-permute-start(bf16[80,384]{1,0:T(8,128)(2,1)} %get-tuple-element.196), channel_id=1, source_target_pairs={{0,24},{4,28},{8,16},{12,20},{16,8},{20,12},{24,0},{28,4},{1,25},{... | collective-permute-start | bytes 184328 | tf_op jit(solution)/shard_map/ppermute | solution.py:177
  (13 other events, 25.2 us)

commit v2 on v1

--- a/solution.py
+++ b/solution.py
@@ -48,7 +48,7 @@
     return lax.dot_general(left, right, dims, preferred_element_type=f32)
 
 
-def kernel_call(body, ins, outs, scratch=(), flops=0, micros=1, name=None, grid=(), out_specs=None):
+def kernel_call(body, ins, outs, scratch=(), flops=0, micros=1, name=None, grid=(), out_specs=None, mib=16):
     return pl.pallas_call(
         body,
         grid=grid,
@@ -56,7 +56,7 @@
         in_specs=ins,
         out_specs=out_specs or tuple(VM for _ in outs),
         scratch_shapes=list(scratch),
-        compiler_params=pltpu.CompilerParams(vmem_limit_bytes=58 * 2**20),
+        compiler_params=pltpu.CompilerParams(vmem_limit_bytes=mib * 2**20),
         cost_estimate=pl.CostEstimate(flops=flops, bytes_accessed=micros * 3_500_000, transcendentals=0),
         name=name,
     )
@@ -188,72 +188,85 @@
 def place_body(win, offs, images, keep, packed, acc, slots):
     images_here, length = keep.shape
     rows, width = packed.shape
-    before = lax.broadcasted_iota(jnp.int32, (length, length), 0)
-    after = lax.broadcasted_iota(jnp.int32, (length, length), 1)
-    tri = jnp.where(before <= after, 1.0, 0.0).astype(bf16)
-    kept = keep[...]
-    ranks = dot(kept.astype(f32).astype(bf16), tri).astype(jnp.int32) - 1
-    slots[...] = jnp.where(kept > 0, ranks, -4 * win)
-    acc[0:8, :] = jnp.zeros((8, width), f32)
+    size = images.shape[0]
+    step = pl.program_id(0)
+
+    @pl.when(step == 0)
+    def _():
+        before = lax.broadcasted_iota(jnp.int32, (length, length), 0)
+        after = lax.broadcasted_iota(jnp.int32, (length, length), 1)
+        tri = jnp.where(before <= after, 1.0, 0.0).astype(bf16)
+        kept = keep[...]
+        ranks = dot(kept.astype(f32).astype(bf16), tri).astype(jnp.int32) - 1
+        slots[...] = jnp.where(kept > 0, ranks, -4 * win)
+        acc[0:8, :] = jnp.zeros((8, width), f32)
+
     place = lax.broadcasted_iota(jnp.int32, (win, length), 0)
-
-    def one_image(i, carry):
-        base = pl.multiple_of((offs[i] // 8) * 8, 8)
-        shift = offs[i] - base
-        chosen = jnp.where(place == slots[pl.ds(i, 1), :] + shift, 1.0, 0.0).astype(bf16)
-        moved = dot(chosen, images[i])
-        acc[pl.ds(base, 8), :] += moved[0:8]
-        acc[pl.ds(base + 8, win - 8), :] = moved[8:]
-        return carry
-
-    lax.fori_loop(0, images_here, one_image, 0)
-    packed[...] = acc[:rows, :].astype(bf16)
+    starts = [offs[step * size + k] for k in range(size)]
+    bases = [pl.multiple_of((start // 8) * 8, 8) for start in starts]
+    lines = [slots[pl.ds(step * size + k, 1), :] + (starts[k] - bases[k]) for k in range(size)]
+    chosen = [jnp.where(place == line, 1.0, 0.0).astype(bf16) for line in lines]
+    moved = [dot(chosen[k], images[k]) for k in range(size)]
+    for base, part in zip(bases, moved):
+        acc[pl.ds(base, 8), :] += part[0:8]
+        acc[pl.ds(base + 8, win - 8), :] = part[8:]
+
+    @pl.when(step == pl.num_programs(0) - 1)
+    def _():
+        packed[...] = acc[:rows, :].astype(bf16)
 
 
 def place_call(images, keep, offs, rows):
     images_here, length, width = images.shape
     win = (length + 7 + 7) // 8 * 8
+    size = 5
     return kernel_call(
         functools.partial(place_body, win),
-        [SM, VM, VM],
+        [SM, pl.BlockSpec((size, length, width), lambda i: (i, 0, 0)), whole(keep.shape)],
         (S((rows, width), bf16),),
         [pltpu.VMEM((rows + win, width), f32), pltpu.VMEM((images_here, length), jnp.int32)],
         flops=2 * images_here * win * length * width,
-        micros=9,
+        micros=6,
         name="place",
+        mib=60,
+        grid=(images_here // size,),
+        out_specs=(whole((rows, width)),),
     )(offs, images, keep)[0]
 
 
 def norm_body(packed, seg_rows, vec, normed, normed_t, seg_cols):
     rows, width = packed.shape
-
-    def one_tile(i, carry):
-        sl = tile_rows(i, 256)
-        unit, _ = norm_parts(packed[sl, :].astype(f32))
-        low = (unit * vec[0:1, :] + vec[1:2, :]).astype(bf16)
-        normed[sl, :] = low
-        normed_t[:, sl] = low.T
-        return carry
-
-    lax.fori_loop(0, rows // 256, one_tile, 0)
-
-    def one_block(j, carry):
-        line = seg_rows[pl.ds(j, 1), :]
-        seg_cols[tile_rows(j, BLK), :] = jnp.broadcast_to(line, (BLK, BLK)).T
-        return carry
-
-    lax.fori_loop(0, rows // BLK, one_block, 0)
+    step = pl.program_id(0)
+    sub = 128
+    parts = [slice(k * sub, (k + 1) * sub) for k in range(rows // sub)]
+    units = [norm_parts(packed[at, :].astype(f32))[0] for at in parts]
+    lows = [(unit * vec[0:1, :] + vec[1:2, :]).astype(bf16) for unit in units]
+    for at, low in zip(parts, lows):
+        normed[at, :] = low
+    for at, low in zip(parts, lows):
+        normed_t[:, at] = low.T
+    for k in range(rows // BLK):
+        line = seg_rows[pl.ds(step * (rows // BLK) + k, 1), :]
+        seg_cols[k * BLK : (k + 1) * BLK, :] = jnp.broadcast_to(line, (BLK, BLK)).T
 
 
 def norm_call(packed, seg_rows, vec):
     rows, width = packed.shape
+    size = 512
     return kernel_call(
         norm_body,
-        [VM, VM, VM],
+        [pl.BlockSpec((size, width), lambda i: (i, 0)), whole(seg_rows.shape), whole(vec.shape)],
         (S((rows, width), bf16), S((width, rows), bf16), S((rows, BLK), jnp.int32)),
         flops=rows * width * 12,
-        micros=6,
+        micros=5,
         name="norm",
+        mib=60,
+        grid=(rows // size,),
+        out_specs=(
+            pl.BlockSpec((size, width), lambda i: (i, 0)),
+            pl.BlockSpec((width, size), lambda i: (0, i)),
+            pl.BlockSpec((size, BLK), lambda i: (i, 0)),
+        ),
     )(packed, seg_rows, vec)
 
 
@@ -380,6 +393,7 @@
         flops=2 * rows * width * 3 * width,
         micros=20,
         name="attend_first",
+        mib=60,
         out_specs=(HB, HB, HB, HB, VM, VM),
     )(own, seg, offs, counts, normed, mine, other, vec, seg_rows, seg_cols)
 
@@ -408,6 +422,7 @@
         flops=4 * blocks * BLK * 512 * width,
         micros=5,
         name="attend_last",
+        mib=60,
     )(seg, offs, counts, qkv, value_t, seg_rows, seg_cols)
 
 
@@ -495,16 +510,16 @@
     parts = [slice(k * sub, (k + 1) * sub) for k in range(size // sub)]
     rows = [pl.ds(pl.multiple_of(step * size + k * sub, sub), sub) for k in range(size // sub)]
     mids = [packed[at, :].astype(f32) + dot(mixed[:, at].T, w_out_t, NT) + vec[4:5, :] for at in parts]
-    units_of = [norm_parts(middle) for middle in mids]
-    lows = [(unit * vec[5:6, :] + vec[6:7, :]).astype(bf16) for unit, _ in units_of]
     valids = [
         lax.broadcasted_iota(jnp.int32, (sub, 1), 0) + step * size + k * sub < steps * size - 1
         for k in range(size // sub)
     ]
     outs = [jnp.where(valid, cot[at, :].astype(f32), 0.0) for valid, at in zip(valids, parts)]
     out_lows = [out.astype(bf16) for out in outs]
+    grads = [dot(out_low, down_s[...], NT) for out_low in out_lows]
+    units_of = [norm_parts(middle) for middle in mids]
+    lows = [(unit * vec[5:6, :] + vec[6:7, :]).astype(bf16) for unit, _ in units_of]
     us = [dot(low, up_s[...], NT) + bias_s[...] for low in lows]
-    grads = [dot(out_low, down_s[...], NT) for out_low in out_lows]
     downs, backs = [], []
     for k in range(size // sub):
         n2t_s[:, rows[k]] = lows[k].T
@@ -598,6 +613,7 @@
         flops=12 * rows * width * units + 6 * rows * width * width,
         micros=30,
         name="feed",
+        mib=60,
     )(own, packed, mixed_a, mixed_b, cot, vec, w_t, mine, other)
 
 
@@ -617,6 +633,7 @@
         flops=2 * rows * width * width,
         micros=4,
         name="side",
+        mib=20,
     )(mixed_a, mixed_b, middle_grad)[0]
 
 
@@ -733,6 +750,7 @@
         flops=22 * rows * width * width,
         micros=30,
         name="back",
+        mib=60,
         out_specs=(HB, VM, VM),
     )(
         own, seg, offs, counts, qkv, key_t, mixed_grad, stats_a, stats_b, seg_rows, seg_cols,
@@ -740,8 +758,7 @@
     )
 
 
-def unpack_body(win, first, count, offs, keep, input_grad, *refs):
-    image_grads, slots = refs[-2], refs[-1]
+def unpack_body(win, offs, keep, input_grad, image_grads, slots):
     images_here, length = keep.shape
     rows, width = input_grad.shape
     before = lax.broadcasted_iota(jnp.int32, (length, length), 0)
@@ -757,7 +774,7 @@
 
     chosen, values = [], []
     for k in range(image_grads.shape[0]):
-        i = first + pl.program_id(0) * image_grads.shape[0] + k
+        i = pl.program_id(0) * image_grads.shape[0] + k
         base = pl.multiple_of(jnp.minimum((offs[i] // 8) * 8, rows - win), 8)
         shift = offs[i] - base
         chosen.append(jnp.where(place == slots[pl.ds(i, 1), :] + shift, 1.0, 0.0).astype(bf16))
@@ -768,27 +785,23 @@
         image_grads[k] = dot(chosen[k], highs[k], TN) + dot(chosen[k], rests[k], TN)
 
 
-def unpack_call(offs, keep, input_grad, first, last, filled=None):
-    count = last - first
+def unpack_call(offs, keep, input_grad):
     images_here, length = keep.shape
     rows, width = input_grad.shape
     win = (length + 7 + 7) // 8 * 8
     size = 5
-    out = pl.BlockSpec((size, length, width), lambda i: (first // size + i, 0, 0))
-    extra_in = [] if filled is None else [pl.BlockSpec(memory_space=pl.ANY)]
-    extra = [] if filled is None else [filled]
-    return pl.pallas_call(
-        functools.partial(unpack_body, win, first, count),
-        grid=(count // size,),
-        out_shape=S((images_here, length, width), f32),
-        in_specs=[SM, whole(keep.shape), whole(input_grad.shape)] + extra_in,
-        out_specs=out,
-        scratch_shapes=[pltpu.VMEM((images_here, length), jnp.int32)],
-        input_output_aliases={} if filled is None else {3: 0},
-        compiler_params=pltpu.CompilerParams(vmem_limit_bytes=58 * 2**20),
-        cost_estimate=pl.CostEstimate(flops=0, bytes_accessed=7 * 3_500_000, transcendentals=0),
+    return kernel_call(
+        functools.partial(unpack_body, win),
+        [SM, whole(keep.shape), whole(input_grad.shape)],
+        (S((images_here, length, width), f32),),
+        [pltpu.VMEM((images_here, length), jnp.int32)],
+        flops=4 * images_here * win * length * width,
+        micros=9,
         name="unpack",
-    )(offs, keep, input_grad, *extra)
+        mib=60,
+        grid=(images_here // size,),
+        out_specs=(pl.BlockSpec((size, length, width), lambda i: (i, 0, 0)),),
+    )(offs, keep, input_grad)[0]
 
 
 def to_halves(chunks):
@@ -986,7 +999,6 @@
         normed, normed_t, seg_cols = norm_call(placed, seg_rows, vectors)
         attn_mine, normed, ffn_line = tie(attn_mine, normed, ffn_line)
         attn_other = over_core(attn_mine)
-        attn_other, ffn_line = tie(attn_other, ffn_line)
         ffn_lines = [ffn_line] + [over_plane(ffn_line, k) for k in (1, 2, 3)]
     else:
         own = jnp.zeros((1,), jnp.int32)
@@ -1041,17 +1053,14 @@
         states += [vectors, vec_first, vec_second, vec_average]
         ffn_states = [jnp.swapaxes(v, 1, 2) for v in (ffn_weight, ffn_first, ffn_second, ffn_average)]
         ffn_states += [v[None, :] for v in (up_bias, bias_first, bias_second, bias_average)]
-        cut = images.shape[0] * 3 // 5
-        unpack = functools.partial(unpack_call, pack_offsets, keep_mask)
         merged, pieces = merge_first_call(ffn_own, ffn_in, attn_keep, attn_in)
         input_grad, *pieces = tie(input_grad, *pieces)
         received = [over_plane(p, k + 1) for k, p in enumerate(pieces)]
-        image_grads = unpack(input_grad, 0, cut)
+        image_grads = unpack_call(pack_offsets, keep_mask, input_grad)
         image_grads, *received = tie(image_grads, *received)
         attn_own, pieces = merge_second_call(2 * piece, merged, received)
         image_grads, merged, *pieces = tie(image_grads, merged, *pieces)
         last = [over_line(p, k + 1) for k, p in enumerate(pieces)]
-        image_grads = unpack(input_grad, cut, images.shape[0], image_grads)
         ffn_grad, bias_grad, ffn_up, bias_up = finish_ffn_call(own, powers, merged, received, ffn_states)
         image_grads, ffn_grad, *last = tie(image_grads, ffn_grad, *last)
         attn_grad, vec_grad, attn_up, vec_up = finish_attn_call(powers, attn_own, last, states)
@@ -1059,7 +1068,7 @@
         attn_up, ffn_up = [v.T for v in attn_up], [jnp.swapaxes(v, 1, 2) for v in ffn_up]
         bias_up = [v[0] for v in bias_up]
     else:
-        image_grads = unpack_call(pack_offsets, keep_mask, input_grad, 0, images.shape[0])
+        image_grads = unpack_call(pack_offsets, keep_mask, input_grad)
         base = ffn_keep.shape[0] - 2 * EXTRA
         ffn_t = from_halves(ffn_keep[:base], ffn_send[:base], 2, width, True)
         ffn_t = jnp.swapaxes(ffn_t, 0, 1).reshape(2, 4 * width, width)

time: 174 us -> 155 us (0.89)
  Pallas kernels: 128 us -> 107 us
    pallas_call x4 -> x3, Pallas kernels: 27 us -> 19.2 us  [the longest x1 8.04 us: unpack_call(): kernel_call(functools.partial(unpack_body, win), [SM, whole(keep.shape),...]
    ppermute x9, waiting for transfers between devices: 0.86 us -> 5.87 us  [over_line(): lax.ppermute(values, 'dp', [(i, i ^ 2 * apart) for i in range(lax.axis_si...]
    pallas_call x1, Pallas kernels: 4.17 us -> 1.05 us  [side_call(): kernel_call(side_body, [VM] * 3, (S((width, width), bf16),), flops=2 * ro...]
    pallas_call x1, Pallas kernels: 2.9 us -> 0.3 us  [combine_call(): kernel_call(functools.partial(combine_body, parts, size, extra, len(recei...]
    pallas_call x1, Pallas kernels: 2.9 us -> 0.32 us  [merge_first_call(): kernel_call(merge_first_body, [VM] * 6, (S((size + EXTRA, width), f32),)...]
    ppermute x4, waiting for transfers between devices: 4.23 us -> 1.92 us  [over_core(): lax.ppermute(values, 'mp', [(i, i ^ 1) for i in range(lax.axis_size('mp'))])]
    pallas_call x1, Pallas kernels: 2.03 us -> 0.1 us  [merge_second_call(): kernel_call(functools.partial(merge_second_body, skip), [VM] * 4, (S((siz...]
    unnamed x35 -> x57, local copies, waits for them, and re-layouts: 4.55 us -> 5.45 us
  transfers between devices with their start and end apart: 22 -> 22, of which waited for: 4 -> 6; matrix products, arithmetic and copies ran while one was open for 0% -> 0% of each run, Pallas kernels for 50% -> 49%
where the time goes in v2:
time: 155 us
  Pallas kernels  107 us (69%)
  starting transfers between devices  26.6 us (17%)
  waiting for transfers between devices  10.6 us (7%)
  local copies, waits for them, and re-layouts  5.63 us (4%)
  other arithmetic  2.62 us (2%)
  between operations  2 us (1%)
    pallas_call x1, Pallas kernels, back_call(): kernel_call(back_body, [SM] * 4 + [HB] * 3 + [VM] * 4 + [HB] * 4 + [VM] *...  30 us
    pallas_call x1, Pallas kernels, feed_call(): kernel_call(functools.partial(feed_body, size), [SM, row_block, pl.BlockS...  29.7 us
    pallas_call x1, Pallas kernels, attend_first_call(): kernel_call(attend_first_body, [SM, SM, SM, SM, VM, VM, VM, VM, VM, VM],...  17 us
    ppermute x9, starting transfers between devices, over_line(): lax.ppermute(values, 'dp', [(i, i ^ 2 * apart) for i in range(lax.axis_si...  15.1 us
    ppermute x9, starting transfers between devices, over_plane(): lax.ppermute(values, ('dp', 'mp'), [(i, i ^ 2 * apart) for i in range(dev...  10.7 us
    pallas_call x1, Pallas kernels, unpack_call(): kernel_call(functools.partial(unpack_body, win), [SM, whole(keep.shape),...  8.04 us
    pallas_call x1, Pallas kernels, attend_last_call(): kernel_call(functools.partial(attend_blocks, tiles - part // BLK, tiles -...  6.51 us
    pallas_call x1, Pallas kernels, place_call(): kernel_call(functools.partial(place_body, win), [SM, pl.BlockSpec((size,...  6.31 us
  transfers between devices with their start and end apart: 22, of which 6 were waited for; matrix products, arithmetic and copies ran while one was open for 0% of the time, Pallas kernels for 49%

profile of v2, /device:TPU:0, one launch (start us, length us, event | category | flops | bytes accessed | tf_op | source)
XLA Modules:
  0.0 154.6 jit_solution(7673619421642515513)
XLA Ops:
  3.2 3.1 %collective-permute-start = (bf16[160,384]{1,0:T(8,128)(2,1)S(1)}, bf16[160,384]{1,0:T(8,128)(2,1)S(1)}, u32[]{:S(2)}, u32[]{:S(2)}) collective-permute-start(bf16[160,384]{1,0:T(8,128)(2,1)S(1)} %fusion.1), channel_id=1, source_target_pairs={{0,8},{4,12},{8,0},{12,4},{16,24},{20,28},{24,16},{28,20},{1,9},{5... | collective-permute-start | bytes 368648 | tf_op jit(solution)/shard_map/ppermute | solution.py:177
  6.3 2.6 %collective-permute-start.1 = (bf16[160,384]{1,0:T(8,128)(2,1)S(1)}, bf16[160,384]{1,0:T(8,128)(2,1)S(1)}, u32[]{:S(2)}, u32[]{:S(2)}) collective-permute-start(bf16[160,384]{1,0:T(8,128)(2,1)S(1)} %fusion.1), channel_id=1, source_target_pairs={{0,16},{4,20},{8,24},{12,28},{16,0},{20,4},{24,8},{28,12},{1,17},{... | collective-permute-start | bytes 368648 | tf_op jit(solution)/shard_map/ppermute | solution.py:177
  8.9 6.3 %place.1.packed.packed_in = bf16[2048,384]{1,0:T(8,128)(2,1)} custom-call(s32[25]{0:T(128)} %offs.9, bf16[25,198,384]{2,1,0:T(8,128)(2,1)} %images.1, s32[25,198]{1,0:T(8,128)} %keep.3), custom_call_target="tpu_custom_call" | custom-call | flops 790732800 | bytes 21000000 | tf_op jit(solution)/shard_map/place/pallas_call | solution.py:223
  15.2 3.4 %collective-permute-done.1 = bf16[160,384]{1,0:T(8,128)(2,1)S(1)} collective-permute-done((bf16[160,384]{1,0:T(8,128)(2,1)S(1)}, bf16[160,384]{1,0:T(8,128)(2,1)S(1)}, u32[]{:S(2)}, u32[]{:S(2)}) %collective-permute-start.1) | collective-permute-done | bytes 122912 | tf_op jit(solution)/shard_map/ppermute | solution.py:177
  18.7 1.6 %collective-permute-start.3 = (bf16[192,384]{1,0:T(8,128)(2,1)S(1)}, bf16[192,384]{1,0:T(8,128)(2,1)S(1)}, u32[]{:S(2)}, u32[]{:S(2)}) collective-permute-start(bf16[192,384]{1,0:T(8,128)(2,1)S(1)} %pad_maximum_fusion.1), channel_id=1, source_target_pairs={{0,2},{1,3},{2,0},{3,1},{4,6},{5,7},{6,4},{7,5},{8,10},{9,11},{10,... | collective-permute-start | bytes 442376 | tf_op jit(solution)/shard_map/ppermute | solution.py:173
  20.3 1.5 collective-permute-start.4
  22.3 4.9 %norm.1 = (bf16[2048,384]{1,0:T(8,128)(2,1)}, bf16[384,2048]{1,0:T(8,128)(2,1)}, s32[2048,128]{1,0:T(8,128)}) custom-call(bf16[2048,384]{1,0:T(8,128)(2,1)} %place.1.packed.packed_in, s32[16,128]{1,0:T(8,128)} %bitcast.53, f32[8,384]{1,0:T(8,128)} %refs_4_.1), custom_call_target="tpu_custom_call" | custom-call | flops 9437184 | bytes 17500000 | tf_op jit(solution)/shard_map/norm/pallas_call | solution.py:256
  29.0 1.5 collective-permute-start.8
  32.3 17.0 %attend_first.1 = (bf16[2048,1152]{1,0:T(8,128)(2,1)}, bf16[384,2048]{1,0:T(8,128)(2,1)}, bf16[384,2048]{1,0:T(8,128)(2,1)}, bf16[32,48,384]{2,1,0:T(8,128)(2,1)...) custom-call(s32[1]{0:T(128)} %bitcast.own.me, s32[2048]{0:T(1024)} %seg.5, s32[25]{0:T(128)} %offs.9, s32[25]{0:T(128)} %counts.5, ...), custom_call_target="tpu_custom_call" | custom-call | flops 1811939328 | bytes 70000000 | tf_op jit(solution)/shard_map/attend_first/pallas_call | solution.py:387
  49.7 6.5 %attend_last.1 = (bf16[384,512]{1,0:T(8,128)(2,1)}, f32[4,768]{1,0:T(4,128)}) custom-call(s32[2048]{0:T(1024)} %seg.5, s32[25]{0:T(128)} %offs.9, s32[25]{0:T(128)} %counts.5, bf16[2048,1152]{1,0:T(8,128)(2,1)} %get-tuple-element.133.qkv.qkv_in, bf16[384,2048]{1,0:T(8,128)(2,1)} %get-tuple-element.134.value_t, s32[16,128]{1,0:T(8,128)} %bitcast.55, ...), custom_call_target="tpu_custom_call" | custom-call | flops 402653184 | bytes 17500000 | tf_op jit(solution)/shard_map/attend_last/pallas_call | solution.py:408
  57.4 29.7 %feed.1 = (bf16[2048,384]{1,0:T(8,128)(2,1)}, f32[2048,384]{1,0:T(8,128)}, bf16[2048,384]{1,0:T(8,128)(2,1)}, bf16[1568,384]{1,0:T(8,128)(2,1)}, bf16[1568,384]{1,0:T(8,128)(2,1)}) custom-call(s32[1]{0:T(128)} %bitcast.own.me, bf16[2048,384]{1,0:T(8,128)(2,1)} %place.1.packed.packed_in, bf16[384,1536]{1,0:T(8,128)(2,1)} %get-tuple-element.132.mixed_a, ...), custom_call_target="tpu_custom_call" | custom-call | flops 16307453952 | bytes 105000000 | tf_op jit(solution)/shard_map/feed/pallas_call | solution.py:584
  87.4 1.9 %copy-done = f32[2048,384]{1,0:T(8,128)S(1)} copy-done((f32[2048,384]{1,0:T(8,128)S(1)}, f32[2048,384]{1,0:T(8,128)}, u32[]{:S(2)}) %copy-start) | copy-done | bytes 3145752
  90.9 1.8 %collective-permute-start.12 = (bf16[416,384]{1,0:T(8,128)(2,1)S(1)}, bf16[416,384]{1,0:T(8,128)(2,1)S(1)}, u32[]{:S(2)}, u32[]{:S(2)}) collective-permute-start(bf16[416,384]{1,0:T(8,128)(2,1)S(1)} %get-tuple-element.162), channel_id=1, source_target_pairs={{0,8},{4,12},{8,0},{12,4},{16,24},{20,28},{24,16},{28,20},{1,9},{5... | collective-permute-start | bytes 958472 | tf_op jit(solution)/shard_map/ppermute | solution.py:177
  92.7 1.8 %collective-permute-start.13 = (bf16[416,384]{1,0:T(8,128)(2,1)S(1)}, bf16[416,384]{1,0:T(8,128)(2,1)S(1)}, u32[]{:S(2)}, u32[]{:S(2)}) collective-permute-start(bf16[416,384]{1,0:T(8,128)(2,1)S(1)} %get-tuple-element.163), channel_id=1, source_target_pairs={{0,16},{4,20},{8,24},{12,28},{16,0},{20,4},{24,8},{28,12},{1,17},{... | collective-permute-start | bytes 958472 | tf_op jit(solution)/shard_map/ppermute | solution.py:177
  95.8 30.0 %back.1 = (f32[2048,384]{1,0:T(8,128)}, bf16[800,384]{1,0:T(8,128)(2,1)}, bf16[800,384]{1,0:T(8,128)(2,1)}) custom-call(s32[1]{0:T(128)} %bitcast.own.me, s32[2048]{0:T(1024)} %seg.5, s32[25]{0:T(128)} %offs.9, s32[25]{0:T(128)} %counts.5, bf16[2048,1152]{1,0:T(8,128)(2,1)} %get-tuple-element.133.qkv.qkv_in, bf16[384,2048]{1,0:T(8,128)(2,1)} %get-tuple-element.145.key_in, ...), custom_call_target="tpu_custom_call" | custom-call | flops 6643777536 | bytes 105000000 | tf_op jit(solution)/shard_map/back/pallas_call | solution.py:734
  126.3 1.9 %collective-permute-done.15.attn_in = bf16[800,384]{1,0:T(8,128)(2,1)S(1)} collective-permute-done((bf16[800,384]{1,0:T(8,128)(2,1)}, bf16[800,384]{1,0:T(8,128)(2,1)S(1)}, u32[]{:S(2)}, u32[]{:S(2)}) %collective-permute-start.15) | collective-permute-done | bytes 614432 | tf_op jit(solution)/shard_map/ppermute | solution.py:168
  129.9 1.8 %collective-permute-start.17 = (bf16[320,384]{1,0:T(8,128)(2,1)S(1)}, bf16[320,384]{1,0:T(8,128)(2,1)S(1)}, u32[]{:S(2)}, u32[]{:S(2)}) collective-permute-start(bf16[320,384]{1,0:T(8,128)(2,1)S(1)} %get-tuple-element.177), channel_id=1, source_target_pairs={{0,4},{1,5},{2,6},{3,7},{4,0},{5,1},{6,2},{7,3},{8,12},{9,13},{10,... | collective-permute-start | bytes 737288 | tf_op jit(solution)/shard_map/ppermute | solution.py:173
  131.7 1.4 collective-permute-start.18
  134.0 8.0 %unpack.1 = f32[25,198,384]{2,1,0:T(8,128)} custom-call(s32[25]{0:T(128)} %offs.9, s32[25,198]{1,0:T(8,128)} %keep.3, f32[2048,384]{1,0:T(8,128)} %get-tuple-element.175.input_grad), custom_call_target="tpu_custom_call" | custom-call | flops 1581465600 | bytes 31500000 | tf_op jit(solution)/shard_map/unpack/pallas_call | solution.py:793
  142.0 2.3 %collective-permute-done.18.in_c = bf16[320,384]{1,0:T(8,128)(2,1)S(1)} collective-permute-done((bf16[320,384]{1,0:T(8,128)(2,1)S(1)}, bf16[320,384]{1,0:T(8,128)(2,1)S(1)}, u32[]{:S(2)}, u32[]{:S(2)}) %collective-permute-start.18) | collective-permute-done | bytes 245792 | tf_op jit(solution)/shard_map/ppermute | solution.py:173
  144.9 2.1 %collective-permute-start.20 = (bf16[80,384]{1,0:T(8,128)(2,1)S(1)}, bf16[80,384]{1,0:T(8,128)(2,1)S(1)}, u32[]{:S(2)}, u32[]{:S(2)}) collective-permute-start(bf16[80,384]{1,0:T(8,128)(2,1)S(1)} %get-tuple-element.191), channel_id=1, source_target_pairs={{0,16},{4,20},{8,24},{12,28},{16,0},{20,4},{24,8},{28,12},{1,17},{... | collective-permute-start | bytes 184328 | tf_op jit(solution)/shard_map/ppermute | solution.py:177
  147.0 1.9 %collective-permute-start.21 = (bf16[80,384]{1,0:T(8,128)(2,1)S(1)}, bf16[80,384]{1,0:T(8,128)(2,1)S(1)}, u32[]{:S(2)}, u32[]{:S(2)}) collective-permute-start(bf16[80,384]{1,0:T(8,128)(2,1)S(1)} %get-tuple-element.192), channel_id=1, source_target_pairs={{0,24},{4,28},{8,16},{12,20},{16,8},{20,12},{24,0},{28,4},{1,25},{... | collective-permute-start | bytes 184328 | tf_op jit(solution)/shard_map/ppermute | solution.py:177
  149.0 1.5 finish_ffn.1
  153.1 1.4 finish_attn.1
  (108 shorter events, 16.7 us)
Async XLA Ops:
  3.2 12.0 %collective-permute-start = (bf16[160,384]{1,0:T(8,128)(2,1)S(1)}, bf16[160,384]{1,0:T(8,128)(2,1)S(1)}, u32[]{:S(2)}, u32[]{:S(2)}) collective-permute-start(bf16[160,384]{1,0:T(8,128)(2,1)S(1)} %fusion.1), channel_id=1, source_target_pairs={{0,8},{4,12},{8,0},{12,4},{16,24},{20,28},{24,16},{28,20},{1,9},{5... | collective-permute-start | bytes 368648 | tf_op jit(solution)/shard_map/ppermute | solution.py:177
  6.3 12.3 %collective-permute-start.1 = (bf16[160,384]{1,0:T(8,128)(2,1)S(1)}, bf16[160,384]{1,0:T(8,128)(2,1)S(1)}, u32[]{:S(2)}, u32[]{:S(2)}) collective-permute-start(bf16[160,384]{1,0:T(8,128)(2,1)S(1)} %fusion.1), channel_id=1, source_target_pairs={{0,16},{4,20},{8,24},{12,28},{16,0},{20,4},{24,8},{28,12},{1,17},{... | collective-permute-start | bytes 368648 | tf_op jit(solution)/shard_map/ppermute | solution.py:177
  8.8 9.7 %collective-permute-start.2 = (bf16[160,384]{1,0:T(8,128)(2,1)S(1)}, bf16[160,384]{1,0:T(8,128)(2,1)S(1)}, u32[]{:S(2)}, u32[]{:S(2)}) collective-permute-start(bf16[160,384]{1,0:T(8,128)(2,1)S(1)} %fusion.1), channel_id=1, source_target_pairs={{0,24},{4,28},{8,16},{12,20},{16,8},{20,12},{24,0},{28,4},{1,25},{... | collective-permute-start | bytes 368648 | tf_op jit(solution)/shard_map/ppermute | solution.py:177
  18.7 8.5 %collective-permute-start.3 = (bf16[192,384]{1,0:T(8,128)(2,1)S(1)}, bf16[192,384]{1,0:T(8,128)(2,1)S(1)}, u32[]{:S(2)}, u32[]{:S(2)}) collective-permute-start(bf16[192,384]{1,0:T(8,128)(2,1)S(1)} %pad_maximum_fusion.1), channel_id=1, source_target_pairs={{0,2},{1,3},{2,0},{3,1},{4,6},{5,7},{6,4},{7,5},{8,10},{9,11},{10,... | collective-permute-start | bytes 442376 | tf_op jit(solution)/shard_map/ppermute | solution.py:173
  20.3 7.0 %collective-permute-start.4 = (bf16[192,384]{1,0:T(8,128)(2,1)S(1)}, bf16[192,384]{1,0:T(8,128)(2,1)S(1)}, u32[]{:S(2)}, u32[]{:S(2)}) collective-permute-start(bf16[192,384]{1,0:T(8,128)(2,1)S(1)} %pad_maximum_fusion.1), channel_id=1, source_target_pairs={{0,4},{1,5},{2,6},{3,7},{4,0},{5,1},{6,2},{7,3},{8,12},{9,13},{10,... | collective-permute-start | bytes 442376 | tf_op jit(solution)/shard_map/ppermute | solution.py:173
  21.7 6.0 %collective-permute-start.5 = (bf16[192,384]{1,0:T(8,128)(2,1)S(1)}, bf16[192,384]{1,0:T(8,128)(2,1)S(1)}, u32[]{:S(2)}, u32[]{:S(2)}) collective-permute-start(bf16[192,384]{1,0:T(8,128)(2,1)S(1)} %pad_maximum_fusion.1), channel_id=1, source_target_pairs={{0,6},{1,7},{2,4},{3,5},{4,2},{5,3},{6,0},{7,1},{8,14},{9,15},{10,... | collective-permute-start | bytes 442376 | tf_op jit(solution)/shard_map/ppermute | solution.py:173
  27.8 3.6 %collective-permute-start.6 = (bf16[768,384]{1,0:T(8,128)(2,1)S(1)}, bf16[768,384]{1,0:T(8,128)(2,1)S(1)}, u32[]{:S(2)}, u32[]{:S(2)}) collective-permute-start(bf16[768,384]{1,0:T(8,128)(2,1)S(1)} %constant_dynamic-update-slice_fusion.mine), channel_id=1, source_target_pairs={{0,1},{1,0},{2,3},{3,2},{4,5},{5,4},{6,7},{7,6},{8,9},{9,8},{10,11... | collective-permute-start | bytes 1769480 | tf_op jit(solution)/shard_map/ppermute | solution.py:168
  27.9 21.5 %collective-permute-start.7 = (bf16[448,384]{1,0:T(8,128)(2,1)S(1)}, bf16[448,384]{1,0:T(8,128)(2,1)S(1)}, u32[]{:S(2)}, u32[]{:S(2)}) collective-permute-start(bf16[448,384]{1,0:T(8,128)(2,1)S(1)} %pad_maximum_fusion), channel_id=1, source_target_pairs={{0,2},{1,3},{2,0},{3,1},{4,6},{5,7},{6,4},{7,5},{8,10},{9,11},{10,... | collective-permute-start | bytes 1032200 | tf_op jit(solution)/shard_map/ppermute | solution.py:173
  29.0 20.4 %collective-permute-start.8 = (bf16[448,384]{1,0:T(8,128)(2,1)S(1)}, bf16[448,384]{1,0:T(8,128)(2,1)S(1)}, u32[]{:S(2)}, u32[]{:S(2)}) collective-permute-start(bf16[448,384]{1,0:T(8,128)(2,1)S(1)} %pad_maximum_fusion), channel_id=1, source_target_pairs={{0,4},{1,5},{2,6},{3,7},{4,0},{5,1},{6,2},{7,3},{8,12},{9,13},{10,... | collective-permute-start | bytes 1032200 | tf_op jit(solution)/shard_map/ppermute | solution.py:173
  30.5 18.9 %collective-permute-start.9 = (bf16[448,384]{1,0:T(8,128)(2,1)S(1)}, bf16[448,384]{1,0:T(8,128)(2,1)S(1)}, u32[]{:S(2)}, u32[]{:S(2)}) collective-permute-start(bf16[448,384]{1,0:T(8,128)(2,1)S(1)} %pad_maximum_fusion), channel_id=1, source_target_pairs={{0,6},{1,7},{2,4},{3,5},{4,2},{5,3},{6,0},{7,1},{8,14},{9,15},{10,... | collective-permute-start | bytes 1032200 | tf_op jit(solution)/shard_map/ppermute | solution.py:173
  49.6 6.6 %collective-permute-start.10 = (bf16[1792,384]{1,0:T(8,128)(2,1)S(1)}, bf16[1792,384]{1,0:T(8,128)(2,1)S(1)}, u32[]{:S(2)}, u32[]{:S(2)}) collective-permute-start(bf16[1792,384]{1,0:T(8,128)(2,1)S(1)} %constant_dynamic-update-slice_fusion.7.mine), channel_id=1, source_target_pairs={{0,1},{1,0},{2,3},{3,2},{4,5},{5,4},{6,7},{7,6},{8,9},{9,8},{10,11... | collective-permute-start | bytes 4128776 | tf_op jit(solution)/shard_map/ppermute | solution.py:168
  57.4 30.0 %copy-start.2 = (bf16[384,1536]{1,0:T(8,128)(2,1)S(1)}, bf16[384,1536]{1,0:T(8,128)(2,1)}, u32[]{:S(2)}) copy-start(bf16[384,1536]{1,0:T(8,128)(2,1)} %get-tuple-element.132.mixed_a) | copy-start | bytes 3538948
  57.4 30.0 %copy-start.5 = (bf16[384,512]{1,0:T(8,128)(2,1)S(1)}, bf16[384,512]{1,0:T(8,128)(2,1)}, u32[]{:S(2)}) copy-start(bf16[384,512]{1,0:T(8,128)(2,1)} %get-tuple-element.140.mixed_b) | copy-start | bytes 1179652
  87.1 3.3 %collective-permute-start.11 = (bf16[1568,384]{1,0:T(8,128)(2,1)}, bf16[1568,384]{1,0:T(8,128)(2,1)S(1)}, u32[]{:S(2)}, u32[]{:S(2)}) collective-permute-start(bf16[1568,384]{1,0:T(8,128)(2,1)} %get-tuple-element.151), channel_id=1, source_target_pairs={{0,1},{1,0},{2,3},{3,2},{4,5},{5,4},{6,7},{7,6},{8,9},{9,8},{10,11... | collective-permute-start | bytes 3612680 | tf_op jit(solution)/shard_map/ppermute | solution.py:168
  90.9 35.0 %collective-permute-start.12 = (bf16[416,384]{1,0:T(8,128)(2,1)S(1)}, bf16[416,384]{1,0:T(8,128)(2,1)S(1)}, u32[]{:S(2)}, u32[]{:S(2)}) collective-permute-start(bf16[416,384]{1,0:T(8,128)(2,1)S(1)} %get-tuple-element.162), channel_id=1, source_target_pairs={{0,8},{4,12},{8,0},{12,4},{16,24},{20,28},{24,16},{28,20},{1,9},{5... | collective-permute-start | bytes 958472 | tf_op jit(solution)/shard_map/ppermute | solution.py:177
  92.7 33.2 %collective-permute-start.13 = (bf16[416,384]{1,0:T(8,128)(2,1)S(1)}, bf16[416,384]{1,0:T(8,128)(2,1)S(1)}, u32[]{:S(2)}, u32[]{:S(2)}) collective-permute-start(bf16[416,384]{1,0:T(8,128)(2,1)S(1)} %get-tuple-element.163), channel_id=1, source_target_pairs={{0,16},{4,20},{8,24},{12,28},{16,0},{20,4},{24,8},{28,12},{1,17},{... | collective-permute-start | bytes 958472 | tf_op jit(solution)/shard_map/ppermute | solution.py:177
  94.5 31.4 %collective-permute-start.14 = (bf16[416,384]{1,0:T(8,128)(2,1)S(1)}, bf16[416,384]{1,0:T(8,128)(2,1)S(1)}, u32[]{:S(2)}, u32[]{:S(2)}) collective-permute-start(bf16[416,384]{1,0:T(8,128)(2,1)S(1)} %get-tuple-element.164), channel_id=1, source_target_pairs={{0,24},{4,28},{8,16},{12,20},{16,8},{20,12},{24,0},{28,4},{1,25},{... | collective-permute-start | bytes 958472 | tf_op jit(solution)/shard_map/ppermute | solution.py:177
  125.9 2.3 %collective-permute-start.15 = (bf16[800,384]{1,0:T(8,128)(2,1)}, bf16[800,384]{1,0:T(8,128)(2,1)S(1)}, u32[]{:S(2)}, u32[]{:S(2)}) collective-permute-start(bf16[800,384]{1,0:T(8,128)(2,1)} %get-tuple-element.171), channel_id=1, source_target_pairs={{0,1},{1,0},{2,3},{3,2},{4,5},{5,4},{6,7},{7,6},{8,9},{9,8},{10,11... | collective-permute-start | bytes 1843208 | tf_op jit(solution)/shard_map/ppermute | solution.py:168
  129.6 12.4 %collective-permute-start.16 = (bf16[320,384]{1,0:T(8,128)(2,1)S(1)}, bf16[320,384]{1,0:T(8,128)(2,1)S(1)}, u32[]{:S(2)}, u32[]{:S(2)}) collective-permute-start(bf16[320,384]{1,0:T(8,128)(2,1)S(1)} %get-tuple-element.176), channel_id=1, source_target_pairs={{0,2},{1,3},{2,0},{3,1},{4,6},{5,7},{6,4},{7,5},{8,10},{9,11},{10,... | collective-permute-start | bytes 737288 | tf_op jit(solution)/shard_map/ppermute | solution.py:173
  129.9 12.1 %collective-permute-start.17 = (bf16[320,384]{1,0:T(8,128)(2,1)S(1)}, bf16[320,384]{1,0:T(8,128)(2,1)S(1)}, u32[]{:S(2)}, u32[]{:S(2)}) collective-permute-start(bf16[320,384]{1,0:T(8,128)(2,1)S(1)} %get-tuple-element.177), channel_id=1, source_target_pairs={{0,4},{1,5},{2,6},{3,7},{4,0},{5,1},{6,2},{7,3},{8,12},{9,13},{10,... | collective-permute-start | bytes 737288 | tf_op jit(solution)/shard_map/ppermute | solution.py:173
  131.7 12.6 %collective-permute-start.18 = (bf16[320,384]{1,0:T(8,128)(2,1)S(1)}, bf16[320,384]{1,0:T(8,128)(2,1)S(1)}, u32[]{:S(2)}, u32[]{:S(2)}) collective-permute-start(bf16[320,384]{1,0:T(8,128)(2,1)S(1)} %get-tuple-element.178), channel_id=1, source_target_pairs={{0,6},{1,7},{2,4},{3,5},{4,2},{5,3},{6,0},{7,1},{8,14},{9,15},{10,... | collective-permute-start | bytes 737288 | tf_op jit(solution)/shard_map/ppermute | solution.py:173
  144.5 6.1 %collective-permute-start.19 = (bf16[80,384]{1,0:T(8,128)(2,1)S(1)}, bf16[80,384]{1,0:T(8,128)(2,1)S(1)}, u32[]{:S(2)}, u32[]{:S(2)}) collective-permute-start(bf16[80,384]{1,0:T(8,128)(2,1)S(1)} %get-tuple-element.190), channel_id=1, source_target_pairs={{0,8},{4,12},{8,0},{12,4},{16,24},{20,28},{24,16},{28,20},{1,9},{5... | collective-permute-start | bytes 184328 | tf_op jit(solution)/shard_map/ppermute | solution.py:177
  144.9 6.8 %collective-permute-start.20 = (bf16[80,384]{1,0:T(8,128)(2,1)S(1)}, bf16[80,384]{1,0:T(8,128)(2,1)S(1)}, u32[]{:S(2)}, u32[]{:S(2)}) collective-permute-start(bf16[80,384]{1,0:T(8,128)(2,1)S(1)} %get-tuple-element.191), channel_id=1, source_target_pairs={{0,16},{4,20},{8,24},{12,28},{16,0},{20,4},{24,8},{28,12},{1,17},{... | collective-permute-start | bytes 184328 | tf_op jit(solution)/shard_map/ppermute | solution.py:177
  147.0 6.0 %collective-permute-start.21 = (bf16[80,384]{1,0:T(8,128)(2,1)S(1)}, bf16[80,384]{1,0:T(8,128)(2,1)S(1)}, u32[]{:S(2)}, u32[]{:S(2)}) collective-permute-start(bf16[80,384]{1,0:T(8,128)(2,1)S(1)} %get-tuple-element.192), channel_id=1, source_target_pairs={{0,24},{4,28},{8,16},{12,20},{16,8},{20,12},{24,0},{28,4},{1,25},{... | collective-permute-start | bytes 184328 | tf_op jit(solution)/shard_map/ppermute | solution.py:177
  (24 other events, 209.3 us)

commit v3 on v2

--- a/solution.py
+++ b/solution.py
@@ -164,6 +164,28 @@
     )(own, *received)
 
 
+def pieces_body(attn, ffn, bias, out, line):
+    piece, width = attn.shape
+    line[...] = jnp.zeros_like(line)
+    line[0:1, :piece] = bias[...]
+    out[:piece, :] = attn[...].astype(bf16)
+    for k in range(2):
+        out[(1 + k) * piece : (2 + k) * piece, :] = ffn[k].astype(bf16)
+    out[3 * piece :, :] = line[...].astype(bf16)
+
+
+def pieces_call(attn, ffn, bias):
+    piece, width = attn.shape
+    return kernel_call(
+        pieces_body,
+        [VM] * 3,
+        (S((3 * piece + 16, width), bf16),),
+        [pltpu.VMEM((16, width), f32)],
+        name="pieces",
+        mib=60,
+    )(attn, ffn, bias)[0]
+
+
 def over_core(values):
     return lax.ppermute(values, "mp", [(i, i ^ 1) for i in range(lax.axis_size("mp"))])
 
@@ -270,15 +292,14 @@
     )(packed, seg_rows, vec)
 
 
-def window(seg, offs, counts, j, images_here, tiles):
+def window(seg, offs, counts, j, images_here, tiles, step):
     first = seg[j * BLK]
     last = seg[j * BLK + BLK - 1]
     used = last < images_here
     last_here = jnp.where(used, last, 0)
     end = jnp.where(used, offs[last_here] + counts[last_here], tiles * BLK)
-    low = offs[first] // BLK
-    size = jnp.maximum((end + BLK - 1) // BLK - low, 2)
-    return jnp.minimum(low, tiles - size), size
+    low = jnp.minimum(offs[first] // BLK, tiles - 2)
+    return low, jnp.maximum((end + step - 1) // step - low * (BLK // step), 2 * BLK // step)
 
 
 def masked_pair(pair):
@@ -293,16 +314,16 @@
     return jnp.concatenate([lim, lim], axis=1)
 
 
-def over_windows(seg, offs, counts, tiles, base, first, blocks, block, before=None):
+def over_windows(seg, offs, counts, tiles, base, first, blocks, block, step=BLK, before=None):
     def one(j, carry):
         if before is not None:
             before(j)
-        low, size = window(seg, offs, counts, j, offs.shape[0], tiles)
-        for n in range(2, REACH + 1):
+        low, size = window(seg, offs, counts, j, offs.shape[0], tiles, step)
+        for n in range(2 * BLK // step, REACH * BLK // step + 1):
 
             @pl.when(size == n)
             def _():
-                block(j, pl.ds(pl.multiple_of((low - base) * BLK, BLK), n * BLK))
+                block(j, pl.ds(pl.multiple_of((low - base) * BLK, BLK), n * step))
 
         return carry
 
@@ -464,7 +485,7 @@
             joined = jnp.concatenate([query_t[:HEAD, :BLK], query_t[HEAD:, BLK:]], axis=0)
             qkv_grad[here, ats[p]] = joined.T.astype(bf16)
 
-    over_windows(seg, offs, counts, rows // BLK, 0, 0, rows // BLK, block, before)
+    over_windows(seg, offs, counts, rows // BLK, 0, 0, rows // BLK, block, BLK // 2, before)
 
 
 def bias_line(rows_of, units):
@@ -695,26 +716,33 @@
         sl = tile_rows(i, size)
         return pltpu.make_async_copy(input_grad.at[sl, :], input_out.at[sl, :], out_sems.at[i])
 
-    def one(i, carry):
-        sl = tile_rows(i, size)
+    tiles = [slice(i * size, (i + 1) * size) for i in range(rows // size)]
+    for sl in tiles:
         qkv_grad[sl, width : 2 * width] = (key_grad[sl, :] * SCALE).astype(bf16)
         qkv_grad[sl, 2 * width :] = value_grad[sl, :].astype(bf16)
-        grads = qkv_grad[sl, :]
-        normed_grad = dot(grads, weights)
+
+    def finish(i, normed_grad):
+        sl = tiles[i]
         unit, inverse = norm_parts(packed[sl, :].astype(f32))
         sums[0:8, :] += row_sums(normed_grad * unit)
         sums[8:16, :] += row_sums(normed_grad)
-        sums[16:24, :] += row_sums(grads[:, :width].astype(f32))
-        sums[24:32, :] += row_sums(grads[:, 2 * width :].astype(f32))
+        sums[16:24, :] += row_sums(qkv_grad[sl, :width].astype(f32))
+        sums[24:32, :] += row_sums(qkv_grad[sl, 2 * width :].astype(f32))
         input_grad[sl, :] = middle_grad[sl, :] + norm_back(unit, inverse, vec[0:1, :], normed_grad)
         result(i).start()
-        return carry
-
-    lax.fori_loop(0, rows // size, one, 0)
-    for lower in range(0, 3 * width, width):
-        pieces = dot(normed_t[...], qkv_grad[:, lower : lower + width]).T.astype(bf16)
-        pieces = pieces.reshape(width // piece, piece, width)
+
+    def weight_part(lower, wide):
+        pieces = dot(normed_t[...], qkv_grad[:, lower : lower + wide]).T.astype(bf16)
+        pieces = pieces.reshape(wide // piece, piece, width)
         store_pieces(me, lower // piece, pieces, keep, send, 0, piece, plane_first)
+
+    grads = [dot(qkv_grad[sl, :], weights) for sl in tiles]
+    for i in range(len(tiles)):
+        if i == 0:
+            weight_part(0, 2 * width)
+        if i == 2:
+            weight_part(2 * width, width)
+        finish(i, grads[i])
     pieces = out_grad[...].reshape(width // piece, piece, width)
     store_pieces(me, 3 * width // piece, pieces, keep, send, 0, piece, plane_first)
     lines = [jnp.sum(sums[8 * row : 8 * row + 8, :], axis=0, keepdims=True) for row in range(4)]
@@ -981,16 +1009,13 @@
     both = ("dp", "mp")
     piece = attn_weight.shape[1]
     tree = lax.axis_size("dp") == 8 and lax.axis_size("mp") == 4
-    bias_row = jnp.pad(up_bias.astype(bf16)[None, :], ((0, 15), (0, width - piece)))
     seg_rows = segment_ids.reshape(rows // BLK, BLK)
     placed = place_call(images, keep_mask, pack_offsets, rows)
     count = step[0].astype(f32)
     powers = jnp.stack([1.0 - jnp.power(BETA_ONE, count), 1.0 - jnp.power(BETA_TWO, count)])
     if tree:
         own = (lax.axis_index("dp") * 4 + lax.axis_index("mp")).astype(jnp.int32)[None]
-        pieces = jnp.concatenate(
-            [attn_weight.astype(bf16).T, ffn_weight[0].astype(bf16).T, ffn_weight[1].astype(bf16).T, bias_row], axis=0
-        )
+        pieces = pieces_call(attn_weight.T, jnp.swapaxes(ffn_weight, 1, 2), up_bias[None, :])
         lines = [pieces] + [over_line(pieces, k) for k in (1, 2, 3)]
         placed, *lines = tie(placed, *lines)
         attn_line = jnp.concatenate([line[:piece] for line in lines], axis=0)

time: 155 us -> 153 us (0.987)
  other arithmetic: 2.62 us -> 0.13 us
    pallas_call x0 -> x1, Pallas kernels: none -> 1.62 us  [pieces_call(): kernel_call(pieces_body, [VM] * 3, (S((3 * piece + 16, width), bf16),), [...]
    unnamed x57 -> x59, local copies, waits for them, and re-layouts: 5.45 us -> 5.35 us
where the time goes in v3:
time: 153 us; the launch traced here: 152 us
  Pallas kernels  107 us (70%)
  starting transfers between devices  25.7 us (17%)
  waiting for transfers between devices  11.4 us (7%)
  local copies, waits for them, and re-layouts  5.52 us (4%)
  between operations  2.04 us (1%)
    pallas_call x1, Pallas kernels, feed_call(): kernel_call(functools.partial(feed_body, size), [SM, row_block, pl.BlockS...  29.7 us
    pallas_call x1, Pallas kernels, back_call(): kernel_call(back_body, [SM] * 4 + [HB] * 3 + [VM] * 4 + [HB] * 4 + [VM] *...  28.8 us
    pallas_call x1, Pallas kernels, attend_first_call(): kernel_call(attend_first_body, [SM, SM, SM, SM, VM, VM, VM, VM, VM, VM],...  16.9 us
    ppermute x9, starting transfers between devices, over_line(): lax.ppermute(values, 'dp', [(i, i ^ 2 * apart) for i in range(lax.axis_si...  14.7 us
    ppermute x9, starting transfers between devices, over_plane(): lax.ppermute(values, ('dp', 'mp'), [(i, i ^ 2 * apart) for i in range(dev...  10.7 us
    pallas_call x1, Pallas kernels, unpack_call(): kernel_call(functools.partial(unpack_body, win), [SM, whole(keep.shape),...  8.04 us
    pallas_call x1, Pallas kernels, attend_last_call(): kernel_call(functools.partial(attend_blocks, tiles - part // BLK, tiles -...  6.67 us
    ppermute x9, waiting for transfers between devices, over_line(): lax.ppermute(values, 'dp', [(i, i ^ 2 * apart) for i in range(lax.axis_si...  6.44 us
  transfers between devices with their start and end apart: 22, of which 6 were waited for; matrix products, arithmetic and copies ran while one was open for 0% of the time, Pallas kernels for 49%

profile of v3, /device:TPU:0, one launch (start us, length us, event | category | flops | bytes accessed | tf_op | source)
XLA Modules:
  0.0 152.3 jit_solution(9335023899885534633)
XLA Ops:
  0.7 1.6 %pieces.1 = bf16[160,384]{1,0:T(8,128)(2,1)} custom-call(f32[48,384]{1,0:T(8,128)} %bitcast.31, f32[2,48,384]{2,1,0:T(8,128)} %bitcast.29, f32[1,48]{1,0:T(1,128)} %bitcast.39), custom_call_target="tpu_custom_call" | custom-call | bytes 3500000 | tf_op jit(solution)/shard_map/pieces/pallas_call | solution.py:179
  2.3 3.0 %collective-permute-start = (bf16[160,384]{1,0:T(8,128)(2,1)}, bf16[160,384]{1,0:T(8,128)(2,1)S(1)}, u32[]{:S(2)}, u32[]{:S(2)}) collective-permute-start(bf16[160,384]{1,0:T(8,128)(2,1)} %pieces.1), channel_id=1, source_target_pairs={{0,8},{4,12},{8,0},{12,4},{16,24},{20,28},{24,16},{28,20},{1,9},{5... | collective-permute-start | bytes 368648 | tf_op jit(solution)/shard_map/ppermute | solution.py:199
  5.3 2.6 %collective-permute-start.1 = (bf16[160,384]{1,0:T(8,128)(2,1)}, bf16[160,384]{1,0:T(8,128)(2,1)S(1)}, u32[]{:S(2)}, u32[]{:S(2)}) collective-permute-start(bf16[160,384]{1,0:T(8,128)(2,1)} %pieces.1), channel_id=1, source_target_pairs={{0,16},{4,20},{8,24},{12,28},{16,0},{20,4},{24,8},{28,12},{1,17},{... | collective-permute-start | bytes 368648 | tf_op jit(solution)/shard_map/ppermute | solution.py:199
  7.9 6.3 %place.1.packed.packed_in = bf16[2048,384]{1,0:T(8,128)(2,1)} custom-call(s32[25]{0:T(128)} %offs.9, bf16[25,198,384]{2,1,0:T(8,128)(2,1)} %images.1, s32[25,198]{1,0:T(8,128)} %keep.3), custom_call_target="tpu_custom_call" | custom-call | flops 790732800 | bytes 21000000 | tf_op jit(solution)/shard_map/place/pallas_call | solution.py:245
  14.2 3.6 %collective-permute-done.1 = bf16[160,384]{1,0:T(8,128)(2,1)S(1)} collective-permute-done((bf16[160,384]{1,0:T(8,128)(2,1)}, bf16[160,384]{1,0:T(8,128)(2,1)S(1)}, u32[]{:S(2)}, u32[]{:S(2)}) %collective-permute-start.1) | collective-permute-done | bytes 122912 | tf_op jit(solution)/shard_map/ppermute | solution.py:199
  17.9 1.6 %collective-permute-start.3 = (bf16[192,384]{1,0:T(8,128)(2,1)S(1)}, bf16[192,384]{1,0:T(8,128)(2,1)S(1)}, u32[]{:S(2)}, u32[]{:S(2)}) collective-permute-start(bf16[192,384]{1,0:T(8,128)(2,1)S(1)} %pad_maximum_fusion.1), channel_id=1, source_target_pairs={{0,2},{1,3},{2,0},{3,1},{4,6},{5,7},{6,4},{7,5},{8,10},{9,11},{10,... | collective-permute-start | bytes 442376 | tf_op jit(solution)/shard_map/ppermute | solution.py:195
  19.5 1.5 collective-permute-start.4
  21.6 4.9 %norm.1 = (bf16[2048,384]{1,0:T(8,128)(2,1)}, bf16[384,2048]{1,0:T(8,128)(2,1)}, s32[2048,128]{1,0:T(8,128)}) custom-call(bf16[2048,384]{1,0:T(8,128)(2,1)} %place.1.packed.packed_in, s32[16,128]{1,0:T(8,128)} %bitcast.44, f32[8,384]{1,0:T(8,128)} %refs_4_.1), custom_call_target="tpu_custom_call" | custom-call | flops 9437184 | bytes 17500000 | tf_op jit(solution)/shard_map/norm/pallas_call | solution.py:278
  28.3 1.5 collective-permute-start.8
  31.6 16.9 %attend_first.1 = (bf16[2048,1152]{1,0:T(8,128)(2,1)}, bf16[384,2048]{1,0:T(8,128)(2,1)}, bf16[384,2048]{1,0:T(8,128)(2,1)}, bf16[32,48,384]{2,1,0:T(8,128)(2,1)...) custom-call(s32[1]{0:T(128)} %bitcast.own.me, s32[2048]{0:T(1024)} %seg.5, s32[25]{0:T(128)} %offs.9, s32[25]{0:T(128)} %counts.5, ...), custom_call_target="tpu_custom_call" | custom-call | flops 1811939328 | bytes 70000000 | tf_op jit(solution)/shard_map/attend_first/pallas_call | solution.py:408
  48.9 6.7 %attend_last.1 = (bf16[384,512]{1,0:T(8,128)(2,1)}, f32[4,768]{1,0:T(4,128)}) custom-call(s32[2048]{0:T(1024)} %seg.5, s32[25]{0:T(128)} %offs.9, s32[25]{0:T(128)} %counts.5, bf16[2048,1152]{1,0:T(8,128)(2,1)} %get-tuple-element.133.qkv.qkv_in, bf16[384,2048]{1,0:T(8,128)(2,1)} %get-tuple-element.134.value_t, s32[16,128]{1,0:T(8,128)} %bitcast.46, ...), custom_call_target="tpu_custom_call" | custom-call | flops 402653184 | bytes 17500000 | tf_op jit(solution)/shard_map/attend_last/pallas_call | solution.py:429
  56.7 29.7 %feed.1 = (bf16[2048,384]{1,0:T(8,128)(2,1)}, f32[2048,384]{1,0:T(8,128)}, bf16[2048,384]{1,0:T(8,128)(2,1)}, bf16[1568,384]{1,0:T(8,128)(2,1)}, bf16[1568,384]{1,0:T(8,128)(2,1)}) custom-call(s32[1]{0:T(128)} %bitcast.own.me, bf16[2048,384]{1,0:T(8,128)(2,1)} %place.1.packed.packed_in, bf16[384,1536]{1,0:T(8,128)(2,1)} %get-tuple-element.132.mixed_a, ...), custom_call_target="tpu_custom_call" | custom-call | flops 16307453952 | bytes 105000000 | tf_op jit(solution)/shard_map/feed/pallas_call | solution.py:605
  86.5 1.9 %copy-done = f32[2048,384]{1,0:T(8,128)S(1)} copy-done((f32[2048,384]{1,0:T(8,128)S(1)}, f32[2048,384]{1,0:T(8,128)}, u32[]{:S(2)}) %copy-start) | copy-done | bytes 3145752
  90.0 1.8 %collective-permute-start.12 = (bf16[416,384]{1,0:T(8,128)(2,1)S(1)}, bf16[416,384]{1,0:T(8,128)(2,1)S(1)}, u32[]{:S(2)}, u32[]{:S(2)}) collective-permute-start(bf16[416,384]{1,0:T(8,128)(2,1)S(1)} %get-tuple-element.162), channel_id=1, source_target_pairs={{0,8},{4,12},{8,0},{12,4},{16,24},{20,28},{24,16},{28,20},{1,9},{5... | collective-permute-start | bytes 958472 | tf_op jit(solution)/shard_map/ppermute | solution.py:199
  91.7 1.6 %collective-permute-start.13 = (bf16[416,384]{1,0:T(8,128)(2,1)S(1)}, bf16[416,384]{1,0:T(8,128)(2,1)S(1)}, u32[]{:S(2)}, u32[]{:S(2)}) collective-permute-start(bf16[416,384]{1,0:T(8,128)(2,1)S(1)} %get-tuple-element.163), channel_id=1, source_target_pairs={{0,16},{4,20},{8,24},{12,28},{16,0},{20,4},{24,8},{28,12},{1,17},{... | collective-permute-start | bytes 958472 | tf_op jit(solution)/shard_map/ppermute | solution.py:199
  94.6 28.8 %back.1 = (f32[2048,384]{1,0:T(8,128)}, bf16[800,384]{1,0:T(8,128)(2,1)}, bf16[800,384]{1,0:T(8,128)(2,1)}) custom-call(s32[1]{0:T(128)} %bitcast.own.me, s32[2048]{0:T(1024)} %seg.5, s32[25]{0:T(128)} %offs.9, s32[25]{0:T(128)} %counts.5, bf16[2048,1152]{1,0:T(8,128)(2,1)} %get-tuple-element.133.qkv.qkv_in, bf16[384,2048]{1,0:T(8,128)(2,1)} %get-tuple-element.145.key_in, ...), custom_call_target="tpu_custom_call" | custom-call | flops 6643777536 | bytes 105000000 | tf_op jit(solution)/shard_map/back/pallas_call | solution.py:762
  123.5 2.2 %collective-permute-done.15.attn_in = bf16[800,384]{1,0:T(8,128)(2,1)S(1)} collective-permute-done((bf16[800,384]{1,0:T(8,128)(2,1)}, bf16[800,384]{1,0:T(8,128)(2,1)S(1)}, u32[]{:S(2)}, u32[]{:S(2)}) %collective-permute-start.15) | collective-permute-done | bytes 614432 | tf_op jit(solution)/shard_map/ppermute | solution.py:190
  128.8 1.9 %collective-permute-start.18 = (bf16[320,384]{1,0:T(8,128)(2,1)S(1)}, bf16[320,384]{1,0:T(8,128)(2,1)S(1)}, u32[]{:S(2)}, u32[]{:S(2)}) collective-permute-start(bf16[320,384]{1,0:T(8,128)(2,1)S(1)} %get-tuple-element.178), channel_id=1, source_target_pairs={{0,6},{1,7},{2,4},{3,5},{4,2},{5,3},{6,0},{7,1},{8,14},{9,15},{10,... | collective-permute-start | bytes 737288 | tf_op jit(solution)/shard_map/ppermute | solution.py:195
  131.5 8.0 %unpack.1 = f32[25,198,384]{2,1,0:T(8,128)} custom-call(s32[25]{0:T(128)} %offs.9, s32[25,198]{1,0:T(8,128)} %keep.3, f32[2048,384]{1,0:T(8,128)} %get-tuple-element.175.input_grad), custom_call_target="tpu_custom_call" | custom-call | flops 1581465600 | bytes 31500000 | tf_op jit(solution)/shard_map/unpack/pallas_call | solution.py:821
  139.6 2.1 %collective-permute-done.18.in_c = bf16[320,384]{1,0:T(8,128)(2,1)S(1)} collective-permute-done((bf16[320,384]{1,0:T(8,128)(2,1)S(1)}, bf16[320,384]{1,0:T(8,128)(2,1)S(1)}, u32[]{:S(2)}, u32[]{:S(2)}) %collective-permute-start.18) | collective-permute-done | bytes 245792 | tf_op jit(solution)/shard_map/ppermute | solution.py:195
  142.2 2.5 %collective-permute-start.20 = (bf16[80,384]{1,0:T(8,128)(2,1)S(1)}, bf16[80,384]{1,0:T(8,128)(2,1)S(1)}, u32[]{:S(2)}, u32[]{:S(2)}) collective-permute-start(bf16[80,384]{1,0:T(8,128)(2,1)S(1)} %get-tuple-element.191), channel_id=1, source_target_pairs={{0,16},{4,20},{8,24},{12,28},{16,0},{20,4},{24,8},{28,12},{1,17},{... | collective-permute-start | bytes 184328 | tf_op jit(solution)/shard_map/ppermute | solution.py:199
  144.7 1.6 %collective-permute-start.21 = (bf16[80,384]{1,0:T(8,128)(2,1)S(1)}, bf16[80,384]{1,0:T(8,128)(2,1)S(1)}, u32[]{:S(2)}, u32[]{:S(2)}) collective-permute-start(bf16[80,384]{1,0:T(8,128)(2,1)S(1)} %get-tuple-element.192), channel_id=1, source_target_pairs={{0,24},{4,28},{8,16},{12,20},{16,8},{20,12},{24,0},{28,4},{1,25},{... | collective-permute-start | bytes 184328 | tf_op jit(solution)/shard_map/ppermute | solution.py:199
  146.4 1.5 finish_ffn.1
  147.9 2.8 %collective-permute-done.21.in_c = bf16[80,384]{1,0:T(8,128)(2,1)S(1)} collective-permute-done((bf16[80,384]{1,0:T(8,128)(2,1)S(1)}, bf16[80,384]{1,0:T(8,128)(2,1)S(1)}, u32[]{:S(2)}, u32[]{:S(2)}) %collective-permute-start.21) | collective-permute-done | bytes 61472 | tf_op jit(solution)/shard_map/ppermute | solution.py:199
  (106 shorter events, 13.7 us)
Async XLA Ops:
  2.3 11.9 %collective-permute-start = (bf16[160,384]{1,0:T(8,128)(2,1)}, bf16[160,384]{1,0:T(8,128)(2,1)S(1)}, u32[]{:S(2)}, u32[]{:S(2)}) collective-permute-start(bf16[160,384]{1,0:T(8,128)(2,1)} %pieces.1), channel_id=1, source_target_pairs={{0,8},{4,12},{8,0},{12,4},{16,24},{20,28},{24,16},{28,20},{1,9},{5... | collective-permute-start | bytes 368648 | tf_op jit(solution)/shard_map/ppermute | solution.py:199
  5.3 12.5 %collective-permute-start.1 = (bf16[160,384]{1,0:T(8,128)(2,1)}, bf16[160,384]{1,0:T(8,128)(2,1)S(1)}, u32[]{:S(2)}, u32[]{:S(2)}) collective-permute-start(bf16[160,384]{1,0:T(8,128)(2,1)} %pieces.1), channel_id=1, source_target_pairs={{0,16},{4,20},{8,24},{12,28},{16,0},{20,4},{24,8},{28,12},{1,17},{... | collective-permute-start | bytes 368648 | tf_op jit(solution)/shard_map/ppermute | solution.py:199
  7.9 9.9 %collective-permute-start.2 = (bf16[160,384]{1,0:T(8,128)(2,1)}, bf16[160,384]{1,0:T(8,128)(2,1)S(1)}, u32[]{:S(2)}, u32[]{:S(2)}) collective-permute-start(bf16[160,384]{1,0:T(8,128)(2,1)} %pieces.1), channel_id=1, source_target_pairs={{0,24},{4,28},{8,16},{12,20},{16,8},{20,12},{24,0},{28,4},{1,25},{... | collective-permute-start | bytes 368648 | tf_op jit(solution)/shard_map/ppermute | solution.py:199
  17.9 8.5 %collective-permute-start.3 = (bf16[192,384]{1,0:T(8,128)(2,1)S(1)}, bf16[192,384]{1,0:T(8,128)(2,1)S(1)}, u32[]{:S(2)}, u32[]{:S(2)}) collective-permute-start(bf16[192,384]{1,0:T(8,128)(2,1)S(1)} %pad_maximum_fusion.1), channel_id=1, source_target_pairs={{0,2},{1,3},{2,0},{3,1},{4,6},{5,7},{6,4},{7,5},{8,10},{9,11},{10,... | collective-permute-start | bytes 442376 | tf_op jit(solution)/shard_map/ppermute | solution.py:195
  19.5 7.0 %collective-permute-start.4 = (bf16[192,384]{1,0:T(8,128)(2,1)S(1)}, bf16[192,384]{1,0:T(8,128)(2,1)S(1)}, u32[]{:S(2)}, u32[]{:S(2)}) collective-permute-start(bf16[192,384]{1,0:T(8,128)(2,1)S(1)} %pad_maximum_fusion.1), channel_id=1, source_target_pairs={{0,4},{1,5},{2,6},{3,7},{4,0},{5,1},{6,2},{7,3},{8,12},{9,13},{10,... | collective-permute-start | bytes 442376 | tf_op jit(solution)/shard_map/ppermute | solution.py:195
  21.0 6.0 %collective-permute-start.5 = (bf16[192,384]{1,0:T(8,128)(2,1)S(1)}, bf16[192,384]{1,0:T(8,128)(2,1)S(1)}, u32[]{:S(2)}, u32[]{:S(2)}) collective-permute-start(bf16[192,384]{1,0:T(8,128)(2,1)S(1)} %pad_maximum_fusion.1), channel_id=1, source_target_pairs={{0,6},{1,7},{2,4},{3,5},{4,2},{5,3},{6,0},{7,1},{8,14},{9,15},{10,... | collective-permute-start | bytes 442376 | tf_op jit(solution)/shard_map/ppermute | solution.py:195
  27.1 3.6 %collective-permute-start.6 = (bf16[768,384]{1,0:T(8,128)(2,1)S(1)}, bf16[768,384]{1,0:T(8,128)(2,1)S(1)}, u32[]{:S(2)}, u32[]{:S(2)}) collective-permute-start(bf16[768,384]{1,0:T(8,128)(2,1)S(1)} %constant_dynamic-update-slice_fusion.mine), channel_id=1, source_target_pairs={{0,1},{1,0},{2,3},{3,2},{4,5},{5,4},{6,7},{7,6},{8,9},{9,8},{10,11... | collective-permute-start | bytes 1769480 | tf_op jit(solution)/shard_map/ppermute | solution.py:190
  27.2 21.3 %collective-permute-start.7 = (bf16[448,384]{1,0:T(8,128)(2,1)S(1)}, bf16[448,384]{1,0:T(8,128)(2,1)S(1)}, u32[]{:S(2)}, u32[]{:S(2)}) collective-permute-start(bf16[448,384]{1,0:T(8,128)(2,1)S(1)} %pad_maximum_fusion), channel_id=1, source_target_pairs={{0,2},{1,3},{2,0},{3,1},{4,6},{5,7},{6,4},{7,5},{8,10},{9,11},{10,... | collective-permute-start | bytes 1032200 | tf_op jit(solution)/shard_map/ppermute | solution.py:195
  28.3 20.3 %collective-permute-start.8 = (bf16[448,384]{1,0:T(8,128)(2,1)S(1)}, bf16[448,384]{1,0:T(8,128)(2,1)S(1)}, u32[]{:S(2)}, u32[]{:S(2)}) collective-permute-start(bf16[448,384]{1,0:T(8,128)(2,1)S(1)} %pad_maximum_fusion), channel_id=1, source_target_pairs={{0,4},{1,5},{2,6},{3,7},{4,0},{5,1},{6,2},{7,3},{8,12},{9,13},{10,... | collective-permute-start | bytes 1032200 | tf_op jit(solution)/shard_map/ppermute | solution.py:195
  29.8 18.8 %collective-permute-start.9 = (bf16[448,384]{1,0:T(8,128)(2,1)S(1)}, bf16[448,384]{1,0:T(8,128)(2,1)S(1)}, u32[]{:S(2)}, u32[]{:S(2)}) collective-permute-start(bf16[448,384]{1,0:T(8,128)(2,1)S(1)} %pad_maximum_fusion), channel_id=1, source_target_pairs={{0,6},{1,7},{2,4},{3,5},{4,2},{5,3},{6,0},{7,1},{8,14},{9,15},{10,... | collective-permute-start | bytes 1032200 | tf_op jit(solution)/shard_map/ppermute | solution.py:195
  48.8 6.8 %collective-permute-start.10 = (bf16[1792,384]{1,0:T(8,128)(2,1)S(1)}, bf16[1792,384]{1,0:T(8,128)(2,1)S(1)}, u32[]{:S(2)}, u32[]{:S(2)}) collective-permute-start(bf16[1792,384]{1,0:T(8,128)(2,1)S(1)} %constant_dynamic-update-slice_fusion.7.mine), channel_id=1, source_target_pairs={{0,1},{1,0},{2,3},{3,2},{4,5},{5,4},{6,7},{7,6},{8,9},{9,8},{10,11... | collective-permute-start | bytes 4128776 | tf_op jit(solution)/shard_map/ppermute | solution.py:190
  56.7 29.8 %copy-start.2 = (bf16[384,1536]{1,0:T(8,128)(2,1)S(1)}, bf16[384,1536]{1,0:T(8,128)(2,1)}, u32[]{:S(2)}) copy-start(bf16[384,1536]{1,0:T(8,128)(2,1)} %get-tuple-element.132.mixed_a) | copy-start | bytes 3538948
  56.7 29.8 %copy-start.5 = (bf16[384,512]{1,0:T(8,128)(2,1)S(1)}, bf16[384,512]{1,0:T(8,128)(2,1)}, u32[]{:S(2)}) copy-start(bf16[384,512]{1,0:T(8,128)(2,1)} %get-tuple-element.140.mixed_b) | copy-start | bytes 1179652
  86.4 3.2 %collective-permute-start.11 = (bf16[1568,384]{1,0:T(8,128)(2,1)}, bf16[1568,384]{1,0:T(8,128)(2,1)S(1)}, u32[]{:S(2)}, u32[]{:S(2)}) collective-permute-start(bf16[1568,384]{1,0:T(8,128)(2,1)} %get-tuple-element.151), channel_id=1, source_target_pairs={{0,1},{1,0},{2,3},{3,2},{4,5},{5,4},{6,7},{7,6},{8,9},{9,8},{10,11... | collective-permute-start | bytes 3612680 | tf_op jit(solution)/shard_map/ppermute | solution.py:190
  90.0 33.4 %collective-permute-start.12 = (bf16[416,384]{1,0:T(8,128)(2,1)S(1)}, bf16[416,384]{1,0:T(8,128)(2,1)S(1)}, u32[]{:S(2)}, u32[]{:S(2)}) collective-permute-start(bf16[416,384]{1,0:T(8,128)(2,1)S(1)} %get-tuple-element.162), channel_id=1, source_target_pairs={{0,8},{4,12},{8,0},{12,4},{16,24},{20,28},{24,16},{28,20},{1,9},{5... | collective-permute-start | bytes 958472 | tf_op jit(solution)/shard_map/ppermute | solution.py:199
  91.7 31.7 %collective-permute-start.13 = (bf16[416,384]{1,0:T(8,128)(2,1)S(1)}, bf16[416,384]{1,0:T(8,128)(2,1)S(1)}, u32[]{:S(2)}, u32[]{:S(2)}) collective-permute-start(bf16[416,384]{1,0:T(8,128)(2,1)S(1)} %get-tuple-element.163), channel_id=1, source_target_pairs={{0,16},{4,20},{8,24},{12,28},{16,0},{20,4},{24,8},{28,12},{1,17},{... | collective-permute-start | bytes 958472 | tf_op jit(solution)/shard_map/ppermute | solution.py:199
  93.3 30.1 %collective-permute-start.14 = (bf16[416,384]{1,0:T(8,128)(2,1)S(1)}, bf16[416,384]{1,0:T(8,128)(2,1)S(1)}, u32[]{:S(2)}, u32[]{:S(2)}) collective-permute-start(bf16[416,384]{1,0:T(8,128)(2,1)S(1)} %get-tuple-element.164), channel_id=1, source_target_pairs={{0,24},{4,28},{8,16},{12,20},{16,8},{20,12},{24,0},{28,4},{1,25},{... | collective-permute-start | bytes 958472 | tf_op jit(solution)/shard_map/ppermute | solution.py:199
  123.4 2.3 %collective-permute-start.15 = (bf16[800,384]{1,0:T(8,128)(2,1)}, bf16[800,384]{1,0:T(8,128)(2,1)S(1)}, u32[]{:S(2)}, u32[]{:S(2)}) collective-permute-start(bf16[800,384]{1,0:T(8,128)(2,1)} %get-tuple-element.171), channel_id=1, source_target_pairs={{0,1},{1,0},{2,3},{3,2},{4,5},{5,4},{6,7},{7,6},{8,9},{9,8},{10,11... | collective-permute-start | bytes 1843208 | tf_op jit(solution)/shard_map/ppermute | solution.py:190
  127.1 12.4 %collective-permute-start.16 = (bf16[320,384]{1,0:T(8,128)(2,1)S(1)}, bf16[320,384]{1,0:T(8,128)(2,1)S(1)}, u32[]{:S(2)}, u32[]{:S(2)}) collective-permute-start(bf16[320,384]{1,0:T(8,128)(2,1)S(1)} %get-tuple-element.176), channel_id=1, source_target_pairs={{0,2},{1,3},{2,0},{3,1},{4,6},{5,7},{6,4},{7,5},{8,10},{9,11},{10,... | collective-permute-start | bytes 737288 | tf_op jit(solution)/shard_map/ppermute | solution.py:195
  128.1 11.5 %collective-permute-start.17 = (bf16[320,384]{1,0:T(8,128)(2,1)S(1)}, bf16[320,384]{1,0:T(8,128)(2,1)S(1)}, u32[]{:S(2)}, u32[]{:S(2)}) collective-permute-start(bf16[320,384]{1,0:T(8,128)(2,1)S(1)} %get-tuple-element.177), channel_id=1, source_target_pairs={{0,4},{1,5},{2,6},{3,7},{4,0},{5,1},{6,2},{7,3},{8,12},{9,13},{10,... | collective-permute-start | bytes 737288 | tf_op jit(solution)/shard_map/ppermute | solution.py:195
  128.8 12.9 %collective-permute-start.18 = (bf16[320,384]{1,0:T(8,128)(2,1)S(1)}, bf16[320,384]{1,0:T(8,128)(2,1)S(1)}, u32[]{:S(2)}, u32[]{:S(2)}) collective-permute-start(bf16[320,384]{1,0:T(8,128)(2,1)S(1)} %get-tuple-element.178), channel_id=1, source_target_pairs={{0,6},{1,7},{2,4},{3,5},{4,2},{5,3},{6,0},{7,1},{8,14},{9,15},{10,... | collective-permute-start | bytes 737288 | tf_op jit(solution)/shard_map/ppermute | solution.py:195
  141.8 6.1 %collective-permute-start.19 = (bf16[80,384]{1,0:T(8,128)(2,1)S(1)}, bf16[80,384]{1,0:T(8,128)(2,1)S(1)}, u32[]{:S(2)}, u32[]{:S(2)}) collective-permute-start(bf16[80,384]{1,0:T(8,128)(2,1)S(1)} %get-tuple-element.190), channel_id=1, source_target_pairs={{0,8},{4,12},{8,0},{12,4},{16,24},{20,28},{24,16},{28,20},{1,9},{5... | collective-permute-start | bytes 184328 | tf_op jit(solution)/shard_map/ppermute | solution.py:199
  142.2 5.8 %collective-permute-start.20 = (bf16[80,384]{1,0:T(8,128)(2,1)S(1)}, bf16[80,384]{1,0:T(8,128)(2,1)S(1)}, u32[]{:S(2)}, u32[]{:S(2)}) collective-permute-start(bf16[80,384]{1,0:T(8,128)(2,1)S(1)} %get-tuple-element.191), channel_id=1, source_target_pairs={{0,16},{4,20},{8,24},{12,28},{16,0},{20,4},{24,8},{28,12},{1,17},{... | collective-permute-start | bytes 184328 | tf_op jit(solution)/shard_map/ppermute | solution.py:199
  144.7 6.0 %collective-permute-start.21 = (bf16[80,384]{1,0:T(8,128)(2,1)S(1)}, bf16[80,384]{1,0:T(8,128)(2,1)S(1)}, u32[]{:S(2)}, u32[]{:S(2)}) collective-permute-start(bf16[80,384]{1,0:T(8,128)(2,1)S(1)} %get-tuple-element.192), channel_id=1, source_target_pairs={{0,24},{4,28},{8,16},{12,20},{16,8},{20,12},{24,0},{28,4},{1,25},{... | collective-permute-start | bytes 184328 | tf_op jit(solution)/shard_map/ppermute | solution.py:199
  (25 other events, 226.2 us)

commit v4 on v3

--- a/solution.py
+++ b/solution.py
@@ -360,12 +360,21 @@
 
 
 def attend_first_body(
-    own, seg, offs, counts, normed, mine, other, vec, seg_rows, seg_cols,
+    own, seg, offs, counts, normed_in, mine, other, vec, seg_rows, cols_in,
     qkv_out, key_out, value_out, w_out, mixed_t, stats,
-    qkv, key_t, value_t, w_t, sems,
+    qkv, key_t, value_t, w_t, normed, seg_cols, sems, in_sems,
 ):
     rows, width = normed.shape
     size = 512
+
+    def reads(i):
+        sl = tile_rows(i, size)
+        return pltpu.make_async_copy(normed_in.at[sl, :], normed.at[sl, :], in_sems.at[i])
+
+    cols = pltpu.make_async_copy(cols_in, seg_cols, in_sems.at[rows // size])
+    for i in range(rows // size):
+        reads(i).start()
+    cols.start()
     spread_pieces(own[0], (mine, other), w_t)
     units = w_t.shape[0] * w_t.shape[1]
     weights = w_t[...].reshape(units, width)[: 3 * width]
@@ -383,6 +392,7 @@
 
     def project(i, carry):
         sl = tile_rows(i, size)
+        reads(i).wait()
         low = (dot(normed[sl, :], weights, NT) + bias).astype(bf16)
         qkv[sl, :] = low
         key_t[:, sl] = low[:, width : 2 * width].T
@@ -392,6 +402,7 @@
         return carry
 
     lax.fori_loop(0, rows // size, project, 0)
+    cols.wait()
     attend_blocks(
         0, 0, mixed_t.shape[1] // BLK, seg, offs, counts, qkv, value_t, seg_rows, seg_cols, mixed_t, stats
     )
@@ -407,10 +418,16 @@
     kept = ((rows, 3 * width), (width, rows), (width, rows), (CHUNKS, piece, width))
     return kernel_call(
         attend_first_body,
-        [SM, SM, SM, SM, VM, VM, VM, VM, VM, VM],
+        [SM, SM, SM, SM, HB, VM, VM, VM, VM, HB],
         tuple(S(shape, bf16) for shape in kept)
         + (S((width, blocks * BLK), bf16), S((blocks, HEADS * BLK), f32)),
-        [pltpu.VMEM(shape, bf16) for shape in kept] + [pltpu.SemaphoreType.DMA((4, rows // 512))],
+        [pltpu.VMEM(shape, bf16) for shape in kept]
+        + [
+            pltpu.VMEM(normed.shape, bf16),
+            pltpu.VMEM(seg_cols.shape, jnp.int32),
+            pltpu.SemaphoreType.DMA((4, rows // 512)),
+            pltpu.SemaphoreType.DMA((rows // 512 + 1,)),
+        ],
         flops=2 * rows * width * 3 * width,
         micros=20,
         name="attend_first",
@@ -634,7 +651,7 @@
         flops=12 * rows * width * units + 6 * rows * width * width,
         micros=30,
         name="feed",
-        mib=60,
+        mib=50,
     )(own, packed, mixed_a, mixed_b, cot, vec, w_t, mine, other)
 
 
@@ -913,7 +930,12 @@
         total = own[rows, :] + wide_of(in_a, rows) + wide_of(in_b, rows) + wide_of(in_c, rows)
         to = out if part == 0 else pieces[part - 1]
         to[:size, :] = total.astype(to.dtype)
-    put_extra(paired([own[-EXTRA:, :]] + [whole_extra(r) for r in received]), out, pieces)
+    high, low = split_low(paired([own[-EXTRA:, :]] + [whole_extra(r) for r in received]))
+    high, low = high.astype(f32), low.astype(f32)
+    out[-EXTRA:, :] = high + low
+    few = jnp.concatenate([high[: EXTRA // 2], low[: EXTRA // 2]], axis=0).astype(bf16)
+    for piece in pieces:
+        piece[-EXTRA:, :] = few
 
 
 def merge_second_call(skip, own, received):
@@ -922,7 +944,7 @@
     out = kernel_call(
         functools.partial(merge_second_body, skip),
         [VM] * 4,
-        (S((size + EXTRA, width), f32),) + (S((size + 2 * EXTRA, width), bf16),) * 3,
+        (S((size + EXTRA, width), f32),) + (S((size + EXTRA, width), bf16),) * 3,
         micros=2,
         name="merge_second",
     )(own, *received)
@@ -980,7 +1002,8 @@
     rows = slice(0, piece)
     grad = own[rows, :] + wide_of(in_a, rows) + wide_of(in_b, rows) + wide_of(in_c, rows)
     update(powers, states[:4], grad, MATRIX_RATE, WEIGHT_DECAY, outs[0], outs[2:6])
-    sums = paired([own[-EXTRA:, :]] + [whole_extra(r) for r in (in_a, in_b, in_c)])
+    few = [wide_of(r, slice(-EXTRA, None)) for r in (in_a, in_b, in_c)]
+    sums = paired([own[-EXTRA : -EXTRA // 2, :]] + [v[: EXTRA // 2] + v[EXTRA // 2 :] for v in few])
     vec = jnp.concatenate([sums[:4], own[-EXTRA + 4 : -EXTRA + 8, :]], axis=0)
     update(powers, states[4:], vec, VECTOR_RATE, 0.0, outs[1], outs[6:])
 

time: 153 us -> 151 us (0.987)
  transfers between devices with their start and end apart: 22 -> 22, of which waited for: 6 -> 7; matrix products, arithmetic and copies ran while one was open for 0% -> 0% of each run, Pallas kernels for 49% -> 49%
where the time goes in v4:
time: 151 us
  Pallas kernels  107 us (71%)
  starting transfers between devices  25.6 us (17%)
  waiting for transfers between devices  10.9 us (7%)
  local copies, waits for them, and re-layouts  5.26 us (3%)
  between operations  2.07 us (1%)
    pallas_call x1, Pallas kernels, back_call(): kernel_call(back_body, [SM] * 4 + [HB] * 3 + [VM] * 4 + [HB] * 4 + [VM] *...  28.8 us
    pallas_call x1, Pallas kernels, feed_call(): kernel_call(functools.partial(feed_body, size), [SM, row_block, pl.BlockS...  28.6 us
    pallas_call x1, Pallas kernels, attend_first_call(): kernel_call(attend_first_body, [SM, SM, SM, SM, HB, VM, VM, VM, VM, HB],...  17.2 us
    ppermute x9, starting transfers between devices, over_line(): lax.ppermute(values, 'dp', [(i, i ^ 2 * apart) for i in range(lax.axis_si...  14.6 us
    ppermute x9, starting transfers between devices, over_plane(): lax.ppermute(values, ('dp', 'mp'), [(i, i ^ 2 * apart) for i in range(dev...  10.7 us
    pallas_call x1, Pallas kernels, unpack_call(): kernel_call(functools.partial(unpack_body, win), [SM, whole(keep.shape),...  8.04 us
    pallas_call x1, Pallas kernels, attend_last_call(): kernel_call(functools.partial(attend_blocks, tiles - part // BLK, tiles -...  6.73 us
    pallas_call x1, Pallas kernels, place_call(): kernel_call(functools.partial(place_body, win), [SM, pl.BlockSpec((size,...  6.24 us
  transfers between devices with their start and end apart: 22, of which 7 were waited for; matrix products, arithmetic and copies ran while one was open for 0% of the time, Pallas kernels for 49%

profile of v4, /device:TPU:0, one launch (start us, length us, event | category | flops | bytes accessed | tf_op | source)
XLA Modules:
  0.0 150.6 jit_solution(8883224658697776853)
XLA Ops:
  0.7 1.6 %pieces.1 = bf16[160,384]{1,0:T(8,128)(2,1)} custom-call(f32[48,384]{1,0:T(8,128)} %bitcast.31, f32[2,48,384]{2,1,0:T(8,128)} %bitcast.29, f32[1,48]{1,0:T(1,128)} %bitcast.39), custom_call_target="tpu_custom_call" | custom-call | bytes 3500000 | tf_op jit(solution)/shard_map/pieces/pallas_call | solution.py:179
  2.3 3.0 %collective-permute-start = (bf16[160,384]{1,0:T(8,128)(2,1)}, bf16[160,384]{1,0:T(8,128)(2,1)S(1)}, u32[]{:S(2)}, u32[]{:S(2)}) collective-permute-start(bf16[160,384]{1,0:T(8,128)(2,1)} %pieces.1), channel_id=1, source_target_pairs={{0,8},{4,12},{8,0},{12,4},{16,24},{20,28},{24,16},{28,20},{1,9},{5... | collective-permute-start | bytes 368648 | tf_op jit(solution)/shard_map/ppermute | solution.py:199
  5.3 2.6 %collective-permute-start.1 = (bf16[160,384]{1,0:T(8,128)(2,1)}, bf16[160,384]{1,0:T(8,128)(2,1)S(1)}, u32[]{:S(2)}, u32[]{:S(2)}) collective-permute-start(bf16[160,384]{1,0:T(8,128)(2,1)} %pieces.1), channel_id=1, source_target_pairs={{0,16},{4,20},{8,24},{12,28},{16,0},{20,4},{24,8},{28,12},{1,17},{... | collective-permute-start | bytes 368648 | tf_op jit(solution)/shard_map/ppermute | solution.py:199
  7.9 6.2 %place.1.packed.packed_in = bf16[2048,384]{1,0:T(8,128)(2,1)} custom-call(s32[25]{0:T(128)} %offs.9, bf16[25,198,384]{2,1,0:T(8,128)(2,1)} %images.1, s32[25,198]{1,0:T(8,128)} %keep.3), custom_call_target="tpu_custom_call" | custom-call | flops 790732800 | bytes 21000000 | tf_op jit(solution)/shard_map/place/pallas_call | solution.py:245
  14.1 3.7 %collective-permute-done.1 = bf16[160,384]{1,0:T(8,128)(2,1)S(1)} collective-permute-done((bf16[160,384]{1,0:T(8,128)(2,1)}, bf16[160,384]{1,0:T(8,128)(2,1)S(1)}, u32[]{:S(2)}, u32[]{:S(2)}) %collective-permute-start.1) | collective-permute-done | bytes 122912 | tf_op jit(solution)/shard_map/ppermute | solution.py:199
  17.9 1.6 %collective-permute-start.3 = (bf16[192,384]{1,0:T(8,128)(2,1)S(1)}, bf16[192,384]{1,0:T(8,128)(2,1)S(1)}, u32[]{:S(2)}, u32[]{:S(2)}) collective-permute-start(bf16[192,384]{1,0:T(8,128)(2,1)S(1)} %pad_maximum_fusion.1), channel_id=1, source_target_pairs={{0,2},{1,3},{2,0},{3,1},{4,6},{5,7},{6,4},{7,5},{8,10},{9,11},{10,... | collective-permute-start | bytes 442376 | tf_op jit(solution)/shard_map/ppermute | solution.py:195
  19.5 1.5 collective-permute-start.4
  21.6 4.9 %norm.1 = (bf16[2048,384]{1,0:T(8,128)(2,1)}, bf16[384,2048]{1,0:T(8,128)(2,1)}, s32[2048,128]{1,0:T(8,128)}) custom-call(bf16[2048,384]{1,0:T(8,128)(2,1)} %place.1.packed.packed_in, s32[16,128]{1,0:T(8,128)} %bitcast.44, f32[8,384]{1,0:T(8,128)} %refs_4_.1), custom_call_target="tpu_custom_call" | custom-call | flops 9437184 | bytes 17500000 | tf_op jit(solution)/shard_map/norm/pallas_call | solution.py:278
  28.3 1.5 collective-permute-start.8
  31.6 17.2 %attend_first.1 = (bf16[2048,1152]{1,0:T(8,128)(2,1)}, bf16[384,2048]{1,0:T(8,128)(2,1)}, bf16[384,2048]{1,0:T(8,128)(2,1)}, bf16[32,48,384]{2,1,0:T(8,128)(2,1)...) custom-call(s32[1]{0:T(128)} %bitcast.own.me, s32[2048]{0:T(1024)} %seg.5, s32[25]{0:T(128)} %offs.9, s32[25]{0:T(128)} %counts.5, ...), custom_call_target="tpu_custom_call" | custom-call | flops 1811939328 | bytes 70000000 | tf_op jit(solution)/shard_map/attend_first/pallas_call | solution.py:419
  49.2 6.7 %attend_last.1 = (bf16[384,512]{1,0:T(8,128)(2,1)}, f32[4,768]{1,0:T(4,128)}) custom-call(s32[2048]{0:T(1024)} %seg.5, s32[25]{0:T(128)} %offs.9, s32[25]{0:T(128)} %counts.5, bf16[2048,1152]{1,0:T(8,128)(2,1)} %get-tuple-element.133.qkv.qkv_in, bf16[384,2048]{1,0:T(8,128)(2,1)} %get-tuple-element.134.value_t, s32[16,128]{1,0:T(8,128)} %bitcast.46, ...), custom_call_target="tpu_custom_call" | custom-call | flops 402653184 | bytes 17500000 | tf_op jit(solution)/shard_map/attend_last/pallas_call | solution.py:446
  56.9 28.6 %feed.1 = (bf16[2048,384]{1,0:T(8,128)(2,1)}, f32[2048,384]{1,0:T(8,128)}, bf16[2048,384]{1,0:T(8,128)(2,1)}, bf16[1568,384]{1,0:T(8,128)(2,1)S(1)}, bf16[1568,384]{1,0:T(8,128)(2,1)}) custom-call(s32[1]{0:T(128)} %bitcast.own.me, bf16[2048,384]{1,0:T(8,128)(2,1)} %place.1.packed.packed_in, bf16[384,1536]{1,0:T(8,128)(2,1)S(1)} %copy-done.1, ...), custom_call_target="tpu_custom_call" | custom-call | flops 16307453952 | bytes 105000000 | tf_op jit(solution)/shard_map/feed/pallas_call | solution.py:622
  85.6 1.9 %copy-done = f32[2048,384]{1,0:T(8,128)S(1)} copy-done((f32[2048,384]{1,0:T(8,128)S(1)}, f32[2048,384]{1,0:T(8,128)}, u32[]{:S(2)}) %copy-start) | copy-done | bytes 3145752
  89.0 1.4 collective-permute-start.12
  90.4 1.9 %collective-permute-start.13 = (bf16[416,384]{1,0:T(8,128)(2,1)S(1)}, bf16[416,384]{1,0:T(8,128)(2,1)S(1)}, u32[]{:S(2)}, u32[]{:S(2)}) collective-permute-start(bf16[416,384]{1,0:T(8,128)(2,1)S(1)} %get-tuple-element.163), channel_id=1, source_target_pairs={{0,16},{4,20},{8,24},{12,28},{16,0},{20,4},{24,8},{28,12},{1,17},{... | collective-permute-start | bytes 958472 | tf_op jit(solution)/shard_map/ppermute | solution.py:199
  93.5 28.8 %back.1 = (f32[2048,384]{1,0:T(8,128)}, bf16[800,384]{1,0:T(8,128)(2,1)}, bf16[800,384]{1,0:T(8,128)(2,1)}) custom-call(s32[1]{0:T(128)} %bitcast.own.me, s32[2048]{0:T(1024)} %seg.5, s32[25]{0:T(128)} %offs.9, s32[25]{0:T(128)} %counts.5, bf16[2048,1152]{1,0:T(8,128)(2,1)} %get-tuple-element.133.qkv.qkv_in, bf16[384,2048]{1,0:T(8,128)(2,1)} %get-tuple-element.145.key_in, ...), custom_call_target="tpu_custom_call" | custom-call | flops 6643777536 | bytes 105000000 | tf_op jit(solution)/shard_map/back/pallas_call | solution.py:779
  122.4 2.2 %collective-permute-done.15.attn_in = bf16[800,384]{1,0:T(8,128)(2,1)S(1)} collective-permute-done((bf16[800,384]{1,0:T(8,128)(2,1)}, bf16[800,384]{1,0:T(8,128)(2,1)S(1)}, u32[]{:S(2)}, u32[]{:S(2)}) %collective-permute-start.15) | collective-permute-done | bytes 614432 | tf_op jit(solution)/shard_map/ppermute | solution.py:190
  128.2 1.4 collective-permute-start.18
  130.4 8.0 %unpack.1 = f32[25,198,384]{2,1,0:T(8,128)} custom-call(s32[25]{0:T(128)} %offs.9, s32[25,198]{1,0:T(8,128)} %keep.3, f32[2048,384]{1,0:T(8,128)} %get-tuple-element.175.input_grad), custom_call_target="tpu_custom_call" | custom-call | flops 1581465600 | bytes 31500000 | tf_op jit(solution)/shard_map/unpack/pallas_call | solution.py:838
  138.5 2.1 %collective-permute-done.18.in_c = bf16[320,384]{1,0:T(8,128)(2,1)S(1)} collective-permute-done((bf16[320,384]{1,0:T(8,128)(2,1)S(1)}, bf16[320,384]{1,0:T(8,128)(2,1)S(1)}, u32[]{:S(2)}, u32[]{:S(2)}) %collective-permute-start.18) | collective-permute-done | bytes 245792 | tf_op jit(solution)/shard_map/ppermute | solution.py:195
  141.8 1.4 collective-permute-start.20
  143.2 2.0 %collective-permute-start.21 = (bf16[64,384]{1,0:T(8,128)(2,1)S(1)}, bf16[64,384]{1,0:T(8,128)(2,1)S(1)}, u32[]{:S(2)}, u32[]{:S(2)}) collective-permute-start(bf16[64,384]{1,0:T(8,128)(2,1)S(1)} %get-tuple-element.192), channel_id=1, source_target_pairs={{0,24},{4,28},{8,16},{12,20},{16,8},{20,12},{24,0},{28,4},{1,25},{... | collective-permute-start | bytes 147464 | tf_op jit(solution)/shard_map/ppermute | solution.py:199
  145.3 1.5 %finish_ffn.1 = (f32[2,48,384]{2,1,0:T(8,128)}, f32[1,48]{1,0:T(1,128)}, f32[2,48,384]{2,1,0:T(8,128)}, f32[2,48,384]{2,1,0:T(8,128)}, f32[2,48,384]{2,1,0:T(8,1...) custom-call(s32[1]{0:T(128)} %bitcast.own.me, ...), custom_call_target="tpu_custom_call" | custom-call | bytes 7000000 | tf_op jit(solution)/shard_map/finish_ffn/pallas_call | solution.py:989
  149.1 1.4 finish_attn.1
  (106 shorter events, 15.5 us)
Async XLA Ops:
  2.3 15.6 %copy-start.23 = (bf16[160,384]{1,0:T(8,128)(2,1)S(1)}, bf16[160,384]{1,0:T(8,128)(2,1)}, u32[]{:S(2)}) copy-start(bf16[160,384]{1,0:T(8,128)(2,1)} %pieces.1) | copy-start | bytes 368644
  2.3 11.9 %collective-permute-start = (bf16[160,384]{1,0:T(8,128)(2,1)}, bf16[160,384]{1,0:T(8,128)(2,1)S(1)}, u32[]{:S(2)}, u32[]{:S(2)}) collective-permute-start(bf16[160,384]{1,0:T(8,128)(2,1)} %pieces.1), channel_id=1, source_target_pairs={{0,8},{4,12},{8,0},{12,4},{16,24},{20,28},{24,16},{28,20},{1,9},{5... | collective-permute-start | bytes 368648 | tf_op jit(solution)/shard_map/ppermute | solution.py:199
  5.3 12.5 %collective-permute-start.1 = (bf16[160,384]{1,0:T(8,128)(2,1)}, bf16[160,384]{1,0:T(8,128)(2,1)S(1)}, u32[]{:S(2)}, u32[]{:S(2)}) collective-permute-start(bf16[160,384]{1,0:T(8,128)(2,1)} %pieces.1), channel_id=1, source_target_pairs={{0,16},{4,20},{8,24},{12,28},{16,0},{20,4},{24,8},{28,12},{1,17},{... | collective-permute-start | bytes 368648 | tf_op jit(solution)/shard_map/ppermute | solution.py:199
  7.9 9.9 %collective-permute-start.2 = (bf16[160,384]{1,0:T(8,128)(2,1)}, bf16[160,384]{1,0:T(8,128)(2,1)S(1)}, u32[]{:S(2)}, u32[]{:S(2)}) collective-permute-start(bf16[160,384]{1,0:T(8,128)(2,1)} %pieces.1), channel_id=1, source_target_pairs={{0,24},{4,28},{8,16},{12,20},{16,8},{20,12},{24,0},{28,4},{1,25},{... | collective-permute-start | bytes 368648 | tf_op jit(solution)/shard_map/ppermute | solution.py:199
  17.9 8.6 %collective-permute-start.3 = (bf16[192,384]{1,0:T(8,128)(2,1)S(1)}, bf16[192,384]{1,0:T(8,128)(2,1)S(1)}, u32[]{:S(2)}, u32[]{:S(2)}) collective-permute-start(bf16[192,384]{1,0:T(8,128)(2,1)S(1)} %pad_maximum_fusion.1), channel_id=1, source_target_pairs={{0,2},{1,3},{2,0},{3,1},{4,6},{5,7},{6,4},{7,5},{8,10},{9,11},{10,... | collective-permute-start | bytes 442376 | tf_op jit(solution)/shard_map/ppermute | solution.py:195
  19.5 7.0 %collective-permute-start.4 = (bf16[192,384]{1,0:T(8,128)(2,1)S(1)}, bf16[192,384]{1,0:T(8,128)(2,1)S(1)}, u32[]{:S(2)}, u32[]{:S(2)}) collective-permute-start(bf16[192,384]{1,0:T(8,128)(2,1)S(1)} %pad_maximum_fusion.1), channel_id=1, source_target_pairs={{0,4},{1,5},{2,6},{3,7},{4,0},{5,1},{6,2},{7,3},{8,12},{9,13},{10,... | collective-permute-start | bytes 442376 | tf_op jit(solution)/shard_map/ppermute | solution.py:195
  21.0 6.0 %collective-permute-start.5 = (bf16[192,384]{1,0:T(8,128)(2,1)S(1)}, bf16[192,384]{1,0:T(8,128)(2,1)S(1)}, u32[]{:S(2)}, u32[]{:S(2)}) collective-permute-start(bf16[192,384]{1,0:T(8,128)(2,1)S(1)} %pad_maximum_fusion.1), channel_id=1, source_target_pairs={{0,6},{1,7},{2,4},{3,5},{4,2},{5,3},{6,0},{7,1},{8,14},{9,15},{10,... | collective-permute-start | bytes 442376 | tf_op jit(solution)/shard_map/ppermute | solution.py:195
  27.1 3.6 %collective-permute-start.6 = (bf16[768,384]{1,0:T(8,128)(2,1)S(1)}, bf16[768,384]{1,0:T(8,128)(2,1)S(1)}, u32[]{:S(2)}, u32[]{:S(2)}) collective-permute-start(bf16[768,384]{1,0:T(8,128)(2,1)S(1)} %constant_dynamic-update-slice_fusion.mine), channel_id=1, source_target_pairs={{0,1},{1,0},{2,3},{3,2},{4,5},{5,4},{6,7},{7,6},{8,9},{9,8},{10,11... | collective-permute-start | bytes 1769480 | tf_op jit(solution)/shard_map/ppermute | solution.py:190
  27.2 21.6 %collective-permute-start.7 = (bf16[448,384]{1,0:T(8,128)(2,1)S(1)}, bf16[448,384]{1,0:T(8,128)(2,1)S(1)}, u32[]{:S(2)}, u32[]{:S(2)}) collective-permute-start(bf16[448,384]{1,0:T(8,128)(2,1)S(1)} %pad_maximum_fusion), channel_id=1, source_target_pairs={{0,2},{1,3},{2,0},{3,1},{4,6},{5,7},{6,4},{7,5},{8,10},{9,11},{10,... | collective-permute-start | bytes 1032200 | tf_op jit(solution)/shard_map/ppermute | solution.py:195
  28.3 20.5 %collective-permute-start.8 = (bf16[448,384]{1,0:T(8,128)(2,1)S(1)}, bf16[448,384]{1,0:T(8,128)(2,1)S(1)}, u32[]{:S(2)}, u32[]{:S(2)}) collective-permute-start(bf16[448,384]{1,0:T(8,128)(2,1)S(1)} %pad_maximum_fusion), channel_id=1, source_target_pairs={{0,4},{1,5},{2,6},{3,7},{4,0},{5,1},{6,2},{7,3},{8,12},{9,13},{10,... | collective-permute-start | bytes 1032200 | tf_op jit(solution)/shard_map/ppermute | solution.py:195
  29.8 19.0 %collective-permute-start.9 = (bf16[448,384]{1,0:T(8,128)(2,1)S(1)}, bf16[448,384]{1,0:T(8,128)(2,1)S(1)}, u32[]{:S(2)}, u32[]{:S(2)}) collective-permute-start(bf16[448,384]{1,0:T(8,128)(2,1)S(1)} %pad_maximum_fusion), channel_id=1, source_target_pairs={{0,6},{1,7},{2,4},{3,5},{4,2},{5,3},{6,0},{7,1},{8,14},{9,15},{10,... | collective-permute-start | bytes 1032200 | tf_op jit(solution)/shard_map/ppermute | solution.py:195
  49.1 6.8 %collective-permute-start.10 = (bf16[1792,384]{1,0:T(8,128)(2,1)S(1)}, bf16[1792,384]{1,0:T(8,128)(2,1)}, u32[]{:S(2)}, u32[]{:S(2)}) collective-permute-start(bf16[1792,384]{1,0:T(8,128)(2,1)S(1)} %constant_dynamic-update-slice_fusion.7.mine), channel_id=1, source_target_pairs={{0,1},{1,0},{2,3},{3,2},{4,5},{5,4},{6,7},{7,6},{8,9},{9,8},{10,11... | collective-permute-start | bytes 4128776 | tf_op jit(solution)/shard_map/ppermute | solution.py:190
  85.5 3.2 %collective-permute-start.11 = (bf16[1568,384]{1,0:T(8,128)(2,1)}, bf16[1568,384]{1,0:T(8,128)(2,1)S(1)}, u32[]{:S(2)}, u32[]{:S(2)}) collective-permute-start(bf16[1568,384]{1,0:T(8,128)(2,1)} %get-tuple-element.151), channel_id=1, source_target_pairs={{0,1},{1,0},{2,3},{3,2},{4,5},{5,4},{6,7},{7,6},{8,9},{9,8},{10,11... | collective-permute-start | bytes 3612680 | tf_op jit(solution)/shard_map/ppermute | solution.py:190
  89.0 33.4 %collective-permute-start.12 = (bf16[416,384]{1,0:T(8,128)(2,1)S(1)}, bf16[416,384]{1,0:T(8,128)(2,1)S(1)}, u32[]{:S(2)}, u32[]{:S(2)}) collective-permute-start(bf16[416,384]{1,0:T(8,128)(2,1)S(1)} %get-tuple-element.162), channel_id=1, source_target_pairs={{0,8},{4,12},{8,0},{12,4},{16,24},{20,28},{24,16},{28,20},{1,9},{5... | collective-permute-start | bytes 958472 | tf_op jit(solution)/shard_map/ppermute | solution.py:199
  90.4 31.9 %collective-permute-start.13 = (bf16[416,384]{1,0:T(8,128)(2,1)S(1)}, bf16[416,384]{1,0:T(8,128)(2,1)S(1)}, u32[]{:S(2)}, u32[]{:S(2)}) collective-permute-start(bf16[416,384]{1,0:T(8,128)(2,1)S(1)} %get-tuple-element.163), channel_id=1, source_target_pairs={{0,16},{4,20},{8,24},{12,28},{16,0},{20,4},{24,8},{28,12},{1,17},{... | collective-permute-start | bytes 958472 | tf_op jit(solution)/shard_map/ppermute | solution.py:199
  92.3 30.1 %collective-permute-start.14 = (bf16[416,384]{1,0:T(8,128)(2,1)S(1)}, bf16[416,384]{1,0:T(8,128)(2,1)S(1)}, u32[]{:S(2)}, u32[]{:S(2)}) collective-permute-start(bf16[416,384]{1,0:T(8,128)(2,1)S(1)} %get-tuple-element.164), channel_id=1, source_target_pairs={{0,24},{4,28},{8,16},{12,20},{16,8},{20,12},{24,0},{28,4},{1,25},{... | collective-permute-start | bytes 958472 | tf_op jit(solution)/shard_map/ppermute | solution.py:199
  122.4 2.3 %collective-permute-start.15 = (bf16[800,384]{1,0:T(8,128)(2,1)}, bf16[800,384]{1,0:T(8,128)(2,1)S(1)}, u32[]{:S(2)}, u32[]{:S(2)}) collective-permute-start(bf16[800,384]{1,0:T(8,128)(2,1)} %get-tuple-element.171), channel_id=1, source_target_pairs={{0,1},{1,0},{2,3},{3,2},{4,5},{5,4},{6,7},{7,6},{8,9},{9,8},{10,11... | collective-permute-start | bytes 1843208 | tf_op jit(solution)/shard_map/ppermute | solution.py:190
  126.1 12.4 %collective-permute-start.16 = (bf16[320,384]{1,0:T(8,128)(2,1)S(1)}, bf16[320,384]{1,0:T(8,128)(2,1)S(1)}, u32[]{:S(2)}, u32[]{:S(2)}) collective-permute-start(bf16[320,384]{1,0:T(8,128)(2,1)S(1)} %get-tuple-element.176), channel_id=1, source_target_pairs={{0,2},{1,3},{2,0},{3,1},{4,6},{5,7},{6,4},{7,5},{8,10},{9,11},{10,... | collective-permute-start | bytes 737288 | tf_op jit(solution)/shard_map/ppermute | solution.py:195
  127.0 11.5 %collective-permute-start.17 = (bf16[320,384]{1,0:T(8,128)(2,1)S(1)}, bf16[320,384]{1,0:T(8,128)(2,1)S(1)}, u32[]{:S(2)}, u32[]{:S(2)}) collective-permute-start(bf16[320,384]{1,0:T(8,128)(2,1)S(1)} %get-tuple-element.177), channel_id=1, source_target_pairs={{0,4},{1,5},{2,6},{3,7},{4,0},{5,1},{6,2},{7,3},{8,12},{9,13},{10,... | collective-permute-start | bytes 737288 | tf_op jit(solution)/shard_map/ppermute | solution.py:195
  128.2 12.3 %collective-permute-start.18 = (bf16[320,384]{1,0:T(8,128)(2,1)S(1)}, bf16[320,384]{1,0:T(8,128)(2,1)S(1)}, u32[]{:S(2)}, u32[]{:S(2)}) collective-permute-start(bf16[320,384]{1,0:T(8,128)(2,1)S(1)} %get-tuple-element.178), channel_id=1, source_target_pairs={{0,6},{1,7},{2,4},{3,5},{4,2},{5,3},{6,0},{7,1},{8,14},{9,15},{10,... | collective-permute-start | bytes 737288 | tf_op jit(solution)/shard_map/ppermute | solution.py:195
  130.4 14.9 %copy-start.3 = (f32[2,384,48]{1,2,0:T(8,128)S(1)}, f32[2,384,48]{1,2,0:T(8,128)}, u32[]{:S(2)}) copy-start(f32[2,384,48]{1,2,0:T(8,128)} %param.30) | copy-start | bytes 442372
  140.7 6.1 %collective-permute-start.19 = (bf16[64,384]{1,0:T(8,128)(2,1)S(1)}, bf16[64,384]{1,0:T(8,128)(2,1)S(1)}, u32[]{:S(2)}, u32[]{:S(2)}) collective-permute-start(bf16[64,384]{1,0:T(8,128)(2,1)S(1)} %get-tuple-element.190), channel_id=1, source_target_pairs={{0,8},{4,12},{8,0},{12,4},{16,24},{20,28},{24,16},{28,20},{1,9},{5... | collective-permute-start | bytes 147464 | tf_op jit(solution)/shard_map/ppermute | solution.py:199
  141.8 6.0 %collective-permute-start.20 = (bf16[64,384]{1,0:T(8,128)(2,1)S(1)}, bf16[64,384]{1,0:T(8,128)(2,1)S(1)}, u32[]{:S(2)}, u32[]{:S(2)}) collective-permute-start(bf16[64,384]{1,0:T(8,128)(2,1)S(1)} %get-tuple-element.191), channel_id=1, source_target_pairs={{0,16},{4,20},{8,24},{12,28},{16,0},{20,4},{24,8},{28,12},{1,17},{... | collective-permute-start | bytes 147464 | tf_op jit(solution)/shard_map/ppermute | solution.py:199
  143.2 5.9 %collective-permute-start.21 = (bf16[64,384]{1,0:T(8,128)(2,1)S(1)}, bf16[64,384]{1,0:T(8,128)(2,1)S(1)}, u32[]{:S(2)}, u32[]{:S(2)}) collective-permute-start(bf16[64,384]{1,0:T(8,128)(2,1)S(1)} %get-tuple-element.192), channel_id=1, source_target_pairs={{0,24},{4,28},{8,16},{12,20},{16,8},{20,12},{24,0},{28,4},{1,25},{... | collective-permute-start | bytes 147464 | tf_op jit(solution)/shard_map/ppermute | solution.py:199
  (25 other events, 209.7 us)

commit v5 on v4

--- a/solution.py
+++ b/solution.py
@@ -795,7 +795,7 @@
         flops=22 * rows * width * width,
         micros=30,
         name="back",
-        mib=60,
+        mib=50,
         out_specs=(HB, VM, VM),
     )(
         own, seg, offs, counts, qkv, key_t, mixed_grad, stats_a, stats_b, seg_rows, seg_cols,

time: 151 us -> 149 us (0.987)
  Pallas kernels: 107 us -> 105 us
    unnamed x59 -> x65, local copies, waits for them, and re-layouts: 5.09 us -> 4.04 us
  transfers between devices with their start and end apart: 22 -> 22, of which waited for: 7 -> 6; matrix products, arithmetic and copies ran while one was open for 0% -> 0% of each run, Pallas kernels for 49% -> 49%
where the time goes in v5:
time: 149 us; the launch traced here: 148 us
  Pallas kernels  105 us (70%)
  starting transfers between devices  25.6 us (17%)
  waiting for transfers between devices  11.3 us (8%)
  local copies, waits for them, and re-layouts  4.21 us (3%)
  between operations  2.1 us (1%)
    pallas_call x1, Pallas kernels, feed_call(): kernel_call(functools.partial(feed_body, size), [SM, row_block, pl.BlockS...  28.6 us
    pallas_call x1, Pallas kernels, back_call(): kernel_call(back_body, [SM] * 4 + [HB] * 3 + [VM] * 4 + [HB] * 4 + [VM] *...  27.3 us
    pallas_call x1, Pallas kernels, attend_first_call(): kernel_call(attend_first_body, [SM, SM, SM, SM, HB, VM, VM, VM, VM, HB],...  17.4 us
    ppermute x9, starting transfers between devices, over_line(): lax.ppermute(values, 'dp', [(i, i ^ 2 * apart) for i in range(lax.axis_si...  14.5 us
    ppermute x9, starting transfers between devices, over_plane(): lax.ppermute(values, ('dp', 'mp'), [(i, i ^ 2 * apart) for i in range(dev...  10.7 us
    pallas_call x1, Pallas kernels, unpack_call(): kernel_call(functools.partial(unpack_body, win), [SM, whole(keep.shape),...  8.04 us
    ppermute x9, waiting for transfers between devices, over_line(): lax.ppermute(values, 'dp', [(i, i ^ 2 * apart) for i in range(lax.axis_si...  6.64 us
    pallas_call x1, Pallas kernels, place_call(): kernel_call(functools.partial(place_body, win), [SM, pl.BlockSpec((size,...  6.26 us
  transfers between devices with their start and end apart: 22, of which 6 were waited for; matrix products, arithmetic and copies ran while one was open for 0% of the time, Pallas kernels for 49%

profile of v5, /device:TPU:0, one launch (start us, length us, event | category | flops | bytes accessed | tf_op | source)
XLA Modules:
  0.0 148.4 jit_solution(11526986691172756916)
XLA Ops:
  0.7 1.6 %pieces.1 = bf16[160,384]{1,0:T(8,128)(2,1)} custom-call(f32[48,384]{1,0:T(8,128)} %bitcast.31, f32[2,48,384]{2,1,0:T(8,128)} %bitcast.29, f32[1,48]{1,0:T(1,128)} %bitcast.43), custom_call_target="tpu_custom_call" | custom-call | bytes 3500000 | tf_op jit(solution)/shard_map/pieces/pallas_call | solution.py:179
  2.3 3.0 %collective-permute-start = (bf16[160,384]{1,0:T(8,128)(2,1)}, bf16[160,384]{1,0:T(8,128)(2,1)S(1)}, u32[]{:S(2)}, u32[]{:S(2)}) collective-permute-start(bf16[160,384]{1,0:T(8,128)(2,1)} %pieces.1), channel_id=1, source_target_pairs={{0,8},{4,12},{8,0},{12,4},{16,24},{20,28},{24,16},{28,20},{1,9},{5... | collective-permute-start | bytes 368648 | tf_op jit(solution)/shard_map/ppermute | solution.py:199
  5.3 2.6 %collective-permute-start.1 = (bf16[160,384]{1,0:T(8,128)(2,1)}, bf16[160,384]{1,0:T(8,128)(2,1)S(1)}, u32[]{:S(2)}, u32[]{:S(2)}) collective-permute-start(bf16[160,384]{1,0:T(8,128)(2,1)} %pieces.1), channel_id=1, source_target_pairs={{0,16},{4,20},{8,24},{12,28},{16,0},{20,4},{24,8},{28,12},{1,17},{... | collective-permute-start | bytes 368648 | tf_op jit(solution)/shard_map/ppermute | solution.py:199
  7.9 6.3 %place.1.packed.packed_in = bf16[2048,384]{1,0:T(8,128)(2,1)} custom-call(s32[25]{0:T(128)} %offs.9, bf16[25,198,384]{2,1,0:T(8,128)(2,1)} %images.1, s32[25,198]{1,0:T(8,128)} %keep.3), custom_call_target="tpu_custom_call" | custom-call | flops 790732800 | bytes 21000000 | tf_op jit(solution)/shard_map/place/pallas_call | solution.py:245
  14.2 3.7 %collective-permute-done.1 = bf16[160,384]{1,0:T(8,128)(2,1)S(1)} collective-permute-done((bf16[160,384]{1,0:T(8,128)(2,1)}, bf16[160,384]{1,0:T(8,128)(2,1)S(1)}, u32[]{:S(2)}, u32[]{:S(2)}) %collective-permute-start.1) | collective-permute-done | bytes 122912 | tf_op jit(solution)/shard_map/ppermute | solution.py:199
  17.9 1.6 %collective-permute-start.3 = (bf16[192,384]{1,0:T(8,128)(2,1)S(1)}, bf16[192,384]{1,0:T(8,128)(2,1)S(1)}, u32[]{:S(2)}, u32[]{:S(2)}) collective-permute-start(bf16[192,384]{1,0:T(8,128)(2,1)S(1)} %pad_maximum_fusion.1), channel_id=1, source_target_pairs={{0,2},{1,3},{2,0},{3,1},{4,6},{5,7},{6,4},{7,5},{8,10},{9,11},{10,... | collective-permute-start | bytes 442376 | tf_op jit(solution)/shard_map/ppermute | solution.py:195
  19.5 1.5 %collective-permute-start.4 = (bf16[192,384]{1,0:T(8,128)(2,1)S(1)}, bf16[192,384]{1,0:T(8,128)(2,1)S(1)}, u32[]{:S(2)}, u32[]{:S(2)}) collective-permute-start(bf16[192,384]{1,0:T(8,128)(2,1)S(1)} %pad_maximum_fusion.1), channel_id=1, source_target_pairs={{0,4},{1,5},{2,6},{3,7},{4,0},{5,1},{6,2},{7,3},{8,12},{9,13},{10,... | collective-permute-start | bytes 442376 | tf_op jit(solution)/shard_map/ppermute | solution.py:195
  21.6 4.9 %norm.1 = (bf16[2048,384]{1,0:T(8,128)(2,1)}, bf16[384,2048]{1,0:T(8,128)(2,1)}, s32[2048,128]{1,0:T(8,128)}) custom-call(bf16[2048,384]{1,0:T(8,128)(2,1)} %place.1.packed.packed_in, s32[16,128]{1,0:T(8,128)} %bitcast.39, f32[8,384]{1,0:T(8,128)} %refs_4_.1), custom_call_target="tpu_custom_call" | custom-call | flops 9437184 | bytes 17500000 | tf_op jit(solution)/shard_map/norm/pallas_call | solution.py:278
  28.3 1.5 %collective-permute-start.8 = (bf16[448,384]{1,0:T(8,128)(2,1)S(1)}, bf16[448,384]{1,0:T(8,128)(2,1)S(1)}, u32[]{:S(2)}, u32[]{:S(2)}) collective-permute-start(bf16[448,384]{1,0:T(8,128)(2,1)S(1)} %pad_maximum_fusion), channel_id=1, source_target_pairs={{0,4},{1,5},{2,6},{3,7},{4,0},{5,1},{6,2},{7,3},{8,12},{9,13},{10,... | collective-permute-start | bytes 1032200 | tf_op jit(solution)/shard_map/ppermute | solution.py:195
  31.6 17.4 %attend_first.1 = (bf16[2048,1152]{1,0:T(8,128)(2,1)}, bf16[384,2048]{1,0:T(8,128)(2,1)}, bf16[384,2048]{1,0:T(8,128)(2,1)}, bf16[32,48,384]{2,1,0:T(8,128)(2,1)...) custom-call(s32[1]{0:T(128)} %bitcast.own.me, s32[2048]{0:T(1024)} %seg.5, s32[25]{0:T(128)} %offs.9, s32[25]{0:T(128)} %counts.5, ...), custom_call_target="tpu_custom_call" | custom-call | flops 1811939328 | bytes 70000000 | tf_op jit(solution)/shard_map/attend_first/pallas_call | solution.py:419
  49.4 6.2 %attend_last.1 = (bf16[384,512]{1,0:T(8,128)(2,1)}, f32[4,768]{1,0:T(4,128)}) custom-call(s32[2048]{0:T(1024)} %seg.5, s32[25]{0:T(128)} %offs.9, s32[25]{0:T(128)} %counts.5, bf16[2048,1152]{1,0:T(8,128)(2,1)} %get-tuple-element.133.qkv.qkv_in, bf16[384,2048]{1,0:T(8,128)(2,1)} %get-tuple-element.134.value_t, s32[16,128]{1,0:T(8,128)} %bitcast.41, ...), custom_call_target="tpu_custom_call" | custom-call | flops 402653184 | bytes 17500000 | tf_op jit(solution)/shard_map/attend_last/pallas_call | solution.py:446
  56.7 28.6 %feed.1 = (bf16[2048,384]{1,0:T(8,128)(2,1)}, f32[2048,384]{1,0:T(8,128)}, bf16[2048,384]{1,0:T(8,128)(2,1)}, bf16[1568,384]{1,0:T(8,128)(2,1)S(1)}, bf16[1568,384]{1,0:T(8,128)(2,1)}) custom-call(s32[1]{0:T(128)} %bitcast.own.me, bf16[2048,384]{1,0:T(8,128)(2,1)} %place.1.packed.packed_in, bf16[384,1536]{1,0:T(8,128)(2,1)S(1)} %copy-done.1, ...), custom_call_target="tpu_custom_call" | custom-call | flops 16307453952 | bytes 105000000 | tf_op jit(solution)/shard_map/feed/pallas_call | solution.py:622
  85.5 1.9 %copy-done = f32[2048,384]{1,0:T(8,128)S(1)} copy-done((f32[2048,384]{1,0:T(8,128)S(1)}, f32[2048,384]{1,0:T(8,128)}, u32[]{:S(2)}) %copy-start) | copy-done | bytes 3145752
  88.9 1.7 %collective-permute-start.12 = (bf16[416,384]{1,0:T(8,128)(2,1)S(1)}, bf16[416,384]{1,0:T(8,128)(2,1)S(1)}, u32[]{:S(2)}, u32[]{:S(2)}) collective-permute-start(bf16[416,384]{1,0:T(8,128)(2,1)S(1)} %get-tuple-element.162), channel_id=1, source_target_pairs={{0,8},{4,12},{8,0},{12,4},{16,24},{20,28},{24,16},{28,20},{1,9},{5... | collective-permute-start | bytes 958472 | tf_op jit(solution)/shard_map/ppermute | solution.py:199
  90.5 1.6 %collective-permute-start.13 = (bf16[416,384]{1,0:T(8,128)(2,1)S(1)}, bf16[416,384]{1,0:T(8,128)(2,1)S(1)}, u32[]{:S(2)}, u32[]{:S(2)}) collective-permute-start(bf16[416,384]{1,0:T(8,128)(2,1)S(1)} %get-tuple-element.163), channel_id=1, source_target_pairs={{0,16},{4,20},{8,24},{12,28},{16,0},{20,4},{24,8},{28,12},{1,17},{... | collective-permute-start | bytes 958472 | tf_op jit(solution)/shard_map/ppermute | solution.py:199
  93.4 27.3 %back.1 = (f32[2048,384]{1,0:T(8,128)}, bf16[800,384]{1,0:T(8,128)(2,1)S(1)}, bf16[800,384]{1,0:T(8,128)(2,1)S(1)}) custom-call(s32[1]{0:T(128)} %bitcast.own.me, s32[2048]{0:T(1024)S(1)} %copy-done.12, s32[25]{0:T(128)S(1)} %copy-done.17, s32[25]{0:T(128)S(1)} %copy-done.19, bf16[2048,1152]{1,0:T(8,128)(2,1)} %get-tuple-element.133.qkv.qkv_in, ...), custom_call_target="tpu_custom_call" | custom-call | flops 6643777536 | bytes 105000000 | tf_op jit(solution)/shard_map/back/pallas_call | solution.py:779
  120.8 2.0 %collective-permute-done.15.attn_in = bf16[800,384]{1,0:T(8,128)(2,1)S(1)} collective-permute-done((bf16[800,384]{1,0:T(8,128)(2,1)S(1)}, bf16[800,384]{1,0:T(8,128)(2,1)S(1)}, u32[]{:S(2)}, u32[]{:S(2)}) %collective-permute-start.15) | collective-permute-done | bytes 614432 | tf_op jit(solution)/shard_map/ppermute | solution.py:190
  124.8 1.9 %collective-permute-start.18 = (bf16[320,384]{1,0:T(8,128)(2,1)S(1)}, bf16[320,384]{1,0:T(8,128)(2,1)S(1)}, u32[]{:S(2)}, u32[]{:S(2)}) collective-permute-start(bf16[320,384]{1,0:T(8,128)(2,1)S(1)} %get-tuple-element.178), channel_id=1, source_target_pairs={{0,6},{1,7},{2,4},{3,5},{4,2},{5,3},{6,0},{7,1},{8,14},{9,15},{10,... | collective-permute-start | bytes 737288 | tf_op jit(solution)/shard_map/ppermute | solution.py:195
  127.5 8.0 %unpack.1 = f32[25,198,384]{2,1,0:T(8,128)} custom-call(s32[25]{0:T(128)} %offs.9, s32[25,198]{1,0:T(8,128)} %keep.3, f32[2048,384]{1,0:T(8,128)} %get-tuple-element.175.input_grad), custom_call_target="tpu_custom_call" | custom-call | flops 1581465600 | bytes 31500000 | tf_op jit(solution)/shard_map/unpack/pallas_call | solution.py:838
  135.6 2.1 %collective-permute-done.18.in_c = bf16[320,384]{1,0:T(8,128)(2,1)S(1)} collective-permute-done((bf16[320,384]{1,0:T(8,128)(2,1)S(1)}, bf16[320,384]{1,0:T(8,128)(2,1)S(1)}, u32[]{:S(2)}, u32[]{:S(2)}) %collective-permute-start.18) | collective-permute-done | bytes 245792 | tf_op jit(solution)/shard_map/ppermute | solution.py:195
  137.8 1.4 collective-permute-start.19
  139.2 1.8 %collective-permute-start.20 = (bf16[64,384]{1,0:T(8,128)(2,1)S(1)}, bf16[64,384]{1,0:T(8,128)(2,1)S(1)}, u32[]{:S(2)}, u32[]{:S(2)}) collective-permute-start(bf16[64,384]{1,0:T(8,128)(2,1)S(1)} %get-tuple-element.191), channel_id=1, source_target_pairs={{0,16},{4,20},{8,24},{12,28},{16,0},{20,4},{24,8},{28,12},{1,17},{... | collective-permute-start | bytes 147464 | tf_op jit(solution)/shard_map/ppermute | solution.py:199
  142.4 1.5 %finish_ffn.1 = (f32[2,48,384]{2,1,0:T(8,128)}, f32[1,48]{1,0:T(1,128)}, f32[2,48,384]{2,1,0:T(8,128)}, f32[2,48,384]{2,1,0:T(8,128)}, f32[2,48,384]{2,1,0:T(8,1...) custom-call(s32[1]{0:T(128)} %bitcast.own.me, ...), custom_call_target="tpu_custom_call" | custom-call | bytes 7000000 | tf_op jit(solution)/shard_map/finish_ffn/pallas_call | solution.py:989
  144.5 2.3 %collective-permute-done.21.in_c = bf16[64,384]{1,0:T(8,128)(2,1)S(1)} collective-permute-done((bf16[64,384]{1,0:T(8,128)(2,1)S(1)}, bf16[64,384]{1,0:T(8,128)(2,1)S(1)}, u32[]{:S(2)}, u32[]{:S(2)}) %collective-permute-start.21) | collective-permute-done | bytes 49184 | tf_op jit(solution)/shard_map/ppermute | solution.py:199
  (112 shorter events, 14.0 us)
Async XLA Ops:
  2.3 15.6 %copy-start.26 = (bf16[160,384]{1,0:T(8,128)(2,1)S(1)}, bf16[160,384]{1,0:T(8,128)(2,1)}, u32[]{:S(2)}) copy-start(bf16[160,384]{1,0:T(8,128)(2,1)} %pieces.1) | copy-start | bytes 368644
  2.3 11.9 %collective-permute-start = (bf16[160,384]{1,0:T(8,128)(2,1)}, bf16[160,384]{1,0:T(8,128)(2,1)S(1)}, u32[]{:S(2)}, u32[]{:S(2)}) collective-permute-start(bf16[160,384]{1,0:T(8,128)(2,1)} %pieces.1), channel_id=1, source_target_pairs={{0,8},{4,12},{8,0},{12,4},{16,24},{20,28},{24,16},{28,20},{1,9},{5... | collective-permute-start | bytes 368648 | tf_op jit(solution)/shard_map/ppermute | solution.py:199
  5.3 12.5 %collective-permute-start.1 = (bf16[160,384]{1,0:T(8,128)(2,1)}, bf16[160,384]{1,0:T(8,128)(2,1)S(1)}, u32[]{:S(2)}, u32[]{:S(2)}) collective-permute-start(bf16[160,384]{1,0:T(8,128)(2,1)} %pieces.1), channel_id=1, source_target_pairs={{0,16},{4,20},{8,24},{12,28},{16,0},{20,4},{24,8},{28,12},{1,17},{... | collective-permute-start | bytes 368648 | tf_op jit(solution)/shard_map/ppermute | solution.py:199
  7.9 9.9 %collective-permute-start.2 = (bf16[160,384]{1,0:T(8,128)(2,1)}, bf16[160,384]{1,0:T(8,128)(2,1)S(1)}, u32[]{:S(2)}, u32[]{:S(2)}) collective-permute-start(bf16[160,384]{1,0:T(8,128)(2,1)} %pieces.1), channel_id=1, source_target_pairs={{0,24},{4,28},{8,16},{12,20},{16,8},{20,12},{24,0},{28,4},{1,25},{... | collective-permute-start | bytes 368648 | tf_op jit(solution)/shard_map/ppermute | solution.py:199
  17.9 8.5 %collective-permute-start.3 = (bf16[192,384]{1,0:T(8,128)(2,1)S(1)}, bf16[192,384]{1,0:T(8,128)(2,1)S(1)}, u32[]{:S(2)}, u32[]{:S(2)}) collective-permute-start(bf16[192,384]{1,0:T(8,128)(2,1)S(1)} %pad_maximum_fusion.1), channel_id=1, source_target_pairs={{0,2},{1,3},{2,0},{3,1},{4,6},{5,7},{6,4},{7,5},{8,10},{9,11},{10,... | collective-permute-start | bytes 442376 | tf_op jit(solution)/shard_map/ppermute | solution.py:195
  19.5 7.0 %collective-permute-start.4 = (bf16[192,384]{1,0:T(8,128)(2,1)S(1)}, bf16[192,384]{1,0:T(8,128)(2,1)S(1)}, u32[]{:S(2)}, u32[]{:S(2)}) collective-permute-start(bf16[192,384]{1,0:T(8,128)(2,1)S(1)} %pad_maximum_fusion.1), channel_id=1, source_target_pairs={{0,4},{1,5},{2,6},{3,7},{4,0},{5,1},{6,2},{7,3},{8,12},{9,13},{10,... | collective-permute-start | bytes 442376 | tf_op jit(solution)/shard_map/ppermute | solution.py:195
  21.0 6.0 %collective-permute-start.5 = (bf16[192,384]{1,0:T(8,128)(2,1)S(1)}, bf16[192,384]{1,0:T(8,128)(2,1)S(1)}, u32[]{:S(2)}, u32[]{:S(2)}) collective-permute-start(bf16[192,384]{1,0:T(8,128)(2,1)S(1)} %pad_maximum_fusion.1), channel_id=1, source_target_pairs={{0,6},{1,7},{2,4},{3,5},{4,2},{5,3},{6,0},{7,1},{8,14},{9,15},{10,... | collective-permute-start | bytes 442376 | tf_op jit(solution)/shard_map/ppermute | solution.py:195
  27.1 3.6 %collective-permute-start.6 = (bf16[768,384]{1,0:T(8,128)(2,1)S(1)}, bf16[768,384]{1,0:T(8,128)(2,1)S(1)}, u32[]{:S(2)}, u32[]{:S(2)}) collective-permute-start(bf16[768,384]{1,0:T(8,128)(2,1)S(1)} %constant_dynamic-update-slice_fusion.mine), channel_id=1, source_target_pairs={{0,1},{1,0},{2,3},{3,2},{4,5},{5,4},{6,7},{7,6},{8,9},{9,8},{10,11... | collective-permute-start | bytes 1769480 | tf_op jit(solution)/shard_map/ppermute | solution.py:190
  27.2 21.8 %collective-permute-start.7 = (bf16[448,384]{1,0:T(8,128)(2,1)S(1)}, bf16[448,384]{1,0:T(8,128)(2,1)S(1)}, u32[]{:S(2)}, u32[]{:S(2)}) collective-permute-start(bf16[448,384]{1,0:T(8,128)(2,1)S(1)} %pad_maximum_fusion), channel_id=1, source_target_pairs={{0,2},{1,3},{2,0},{3,1},{4,6},{5,7},{6,4},{7,5},{8,10},{9,11},{10,... | collective-permute-start | bytes 1032200 | tf_op jit(solution)/shard_map/ppermute | solution.py:195
  28.3 20.7 %collective-permute-start.8 = (bf16[448,384]{1,0:T(8,128)(2,1)S(1)}, bf16[448,384]{1,0:T(8,128)(2,1)S(1)}, u32[]{:S(2)}, u32[]{:S(2)}) collective-permute-start(bf16[448,384]{1,0:T(8,128)(2,1)S(1)} %pad_maximum_fusion), channel_id=1, source_target_pairs={{0,4},{1,5},{2,6},{3,7},{4,0},{5,1},{6,2},{7,3},{8,12},{9,13},{10,... | collective-permute-start | bytes 1032200 | tf_op jit(solution)/shard_map/ppermute | solution.py:195
  29.8 19.3 %collective-permute-start.9 = (bf16[448,384]{1,0:T(8,128)(2,1)S(1)}, bf16[448,384]{1,0:T(8,128)(2,1)S(1)}, u32[]{:S(2)}, u32[]{:S(2)}) collective-permute-start(bf16[448,384]{1,0:T(8,128)(2,1)S(1)} %pad_maximum_fusion), channel_id=1, source_target_pairs={{0,6},{1,7},{2,4},{3,5},{4,2},{5,3},{6,0},{7,1},{8,14},{9,15},{10,... | collective-permute-start | bytes 1032200 | tf_op jit(solution)/shard_map/ppermute | solution.py:195
  49.3 6.3 %collective-permute-start.10 = (bf16[1792,384]{1,0:T(8,128)(2,1)S(1)}, bf16[1792,384]{1,0:T(8,128)(2,1)}, u32[]{:S(2)}, u32[]{:S(2)}) collective-permute-start(bf16[1792,384]{1,0:T(8,128)(2,1)S(1)} %constant_dynamic-update-slice_fusion.7.mine), channel_id=1, source_target_pairs={{0,1},{1,0},{2,3},{3,2},{4,5},{5,4},{6,7},{7,6},{8,9},{9,8},{10,11... | collective-permute-start | bytes 4128776 | tf_op jit(solution)/shard_map/ppermute | solution.py:190
  85.3 3.3 %collective-permute-start.11 = (bf16[1568,384]{1,0:T(8,128)(2,1)}, bf16[1568,384]{1,0:T(8,128)(2,1)S(1)}, u32[]{:S(2)}, u32[]{:S(2)}) collective-permute-start(bf16[1568,384]{1,0:T(8,128)(2,1)} %get-tuple-element.151), channel_id=1, source_target_pairs={{0,1},{1,0},{2,3},{3,2},{4,5},{5,4},{6,7},{7,6},{8,9},{9,8},{10,11... | collective-permute-start | bytes 3612680 | tf_op jit(solution)/shard_map/ppermute | solution.py:190
  88.9 31.8 %collective-permute-start.12 = (bf16[416,384]{1,0:T(8,128)(2,1)S(1)}, bf16[416,384]{1,0:T(8,128)(2,1)S(1)}, u32[]{:S(2)}, u32[]{:S(2)}) collective-permute-start(bf16[416,384]{1,0:T(8,128)(2,1)S(1)} %get-tuple-element.162), channel_id=1, source_target_pairs={{0,8},{4,12},{8,0},{12,4},{16,24},{20,28},{24,16},{28,20},{1,9},{5... | collective-permute-start | bytes 958472 | tf_op jit(solution)/shard_map/ppermute | solution.py:199
  90.5 30.1 %collective-permute-start.13 = (bf16[416,384]{1,0:T(8,128)(2,1)S(1)}, bf16[416,384]{1,0:T(8,128)(2,1)S(1)}, u32[]{:S(2)}, u32[]{:S(2)}) collective-permute-start(bf16[416,384]{1,0:T(8,128)(2,1)S(1)} %get-tuple-element.163), channel_id=1, source_target_pairs={{0,16},{4,20},{8,24},{12,28},{16,0},{20,4},{24,8},{28,12},{1,17},{... | collective-permute-start | bytes 958472 | tf_op jit(solution)/shard_map/ppermute | solution.py:199
  92.1 28.6 %collective-permute-start.14 = (bf16[416,384]{1,0:T(8,128)(2,1)S(1)}, bf16[416,384]{1,0:T(8,128)(2,1)S(1)}, u32[]{:S(2)}, u32[]{:S(2)}) collective-permute-start(bf16[416,384]{1,0:T(8,128)(2,1)S(1)} %get-tuple-element.164), channel_id=1, source_target_pairs={{0,24},{4,28},{8,16},{12,20},{16,8},{20,12},{24,0},{28,4},{1,25},{... | collective-permute-start | bytes 958472 | tf_op jit(solution)/shard_map/ppermute | solution.py:199
  120.7 2.1 %collective-permute-start.15 = (bf16[800,384]{1,0:T(8,128)(2,1)S(1)}, bf16[800,384]{1,0:T(8,128)(2,1)S(1)}, u32[]{:S(2)}, u32[]{:S(2)}) collective-permute-start(bf16[800,384]{1,0:T(8,128)(2,1)S(1)} %get-tuple-element.171), channel_id=1, source_target_pairs={{0,1},{1,0},{2,3},{3,2},{4,5},{5,4},{6,7},{7,6},{8,9},{9,8},{10,11... | collective-permute-start | bytes 1843208 | tf_op jit(solution)/shard_map/ppermute | solution.py:190
  123.1 12.4 %collective-permute-start.16 = (bf16[320,384]{1,0:T(8,128)(2,1)S(1)}, bf16[320,384]{1,0:T(8,128)(2,1)S(1)}, u32[]{:S(2)}, u32[]{:S(2)}) collective-permute-start(bf16[320,384]{1,0:T(8,128)(2,1)S(1)} %get-tuple-element.176), channel_id=1, source_target_pairs={{0,2},{1,3},{2,0},{3,1},{4,6},{5,7},{6,4},{7,5},{8,10},{9,11},{10,... | collective-permute-start | bytes 737288 | tf_op jit(solution)/shard_map/ppermute | solution.py:195
  124.3 11.2 %collective-permute-start.17 = (bf16[320,384]{1,0:T(8,128)(2,1)S(1)}, bf16[320,384]{1,0:T(8,128)(2,1)S(1)}, u32[]{:S(2)}, u32[]{:S(2)}) collective-permute-start(bf16[320,384]{1,0:T(8,128)(2,1)S(1)} %get-tuple-element.177), channel_id=1, source_target_pairs={{0,4},{1,5},{2,6},{3,7},{4,0},{5,1},{6,2},{7,3},{8,12},{9,13},{10,... | collective-permute-start | bytes 737288 | tf_op jit(solution)/shard_map/ppermute | solution.py:195
  124.8 12.8 %collective-permute-start.18 = (bf16[320,384]{1,0:T(8,128)(2,1)S(1)}, bf16[320,384]{1,0:T(8,128)(2,1)S(1)}, u32[]{:S(2)}, u32[]{:S(2)}) collective-permute-start(bf16[320,384]{1,0:T(8,128)(2,1)S(1)} %get-tuple-element.178), channel_id=1, source_target_pairs={{0,6},{1,7},{2,4},{3,5},{4,2},{5,3},{6,0},{7,1},{8,14},{9,15},{10,... | collective-permute-start | bytes 737288 | tf_op jit(solution)/shard_map/ppermute | solution.py:195
  127.4 14.9 %copy-start.3 = (f32[2,384,48]{1,2,0:T(8,128)S(1)}, f32[2,384,48]{1,2,0:T(8,128)}, u32[]{:S(2)}) copy-start(f32[2,384,48]{1,2,0:T(8,128)} %param.30) | copy-start | bytes 442372
  137.8 6.1 %collective-permute-start.19 = (bf16[64,384]{1,0:T(8,128)(2,1)S(1)}, bf16[64,384]{1,0:T(8,128)(2,1)S(1)}, u32[]{:S(2)}, u32[]{:S(2)}) collective-permute-start(bf16[64,384]{1,0:T(8,128)(2,1)S(1)} %get-tuple-element.190), channel_id=1, source_target_pairs={{0,8},{4,12},{8,0},{12,4},{16,24},{20,28},{24,16},{28,20},{1,9},{5... | collective-permute-start | bytes 147464 | tf_op jit(solution)/shard_map/ppermute | solution.py:199
  139.2 5.3 %collective-permute-start.20 = (bf16[64,384]{1,0:T(8,128)(2,1)S(1)}, bf16[64,384]{1,0:T(8,128)(2,1)S(1)}, u32[]{:S(2)}, u32[]{:S(2)}) collective-permute-start(bf16[64,384]{1,0:T(8,128)(2,1)S(1)} %get-tuple-element.191), channel_id=1, source_target_pairs={{0,16},{4,20},{8,24},{12,28},{16,0},{20,4},{24,8},{28,12},{1,17},{... | collective-permute-start | bytes 147464 | tf_op jit(solution)/shard_map/ppermute | solution.py:199
  140.9 5.9 %collective-permute-start.21 = (bf16[64,384]{1,0:T(8,128)(2,1)S(1)}, bf16[64,384]{1,0:T(8,128)(2,1)S(1)}, u32[]{:S(2)}, u32[]{:S(2)}) collective-permute-start(bf16[64,384]{1,0:T(8,128)(2,1)S(1)} %get-tuple-element.192), channel_id=1, source_target_pairs={{0,24},{4,28},{8,16},{12,20},{16,8},{20,12},{24,0},{28,4},{1,25},{... | collective-permute-start | bytes 147464 | tf_op jit(solution)/shard_map/ppermute | solution.py:199
  (28 other events, 230.0 us)
